TPU v7x, 32 devices: a whole 2x2x4 slice. The times are simulated.
32 devices in a mesh: wide: 4 (over y, core), narrow: 8 (over z, x).
Axes of the slice: x: 2, y: 2, z: 4, core: 2. Of those that a mesh axis runs over, the one named last changes fastest.
Arguments:
- loads: float32 [128, 24, 128], P(('wide', 'narrow')), may hold values from -6 to 6
- diagonal: float32 [128, 128], P(('wide', 'narrow')), may hold values from 2 to 7
- stiffness: float32 [128, 4, 128, 128], P(('wide', 'narrow')), may hold values from 0 to 0.001953125
- neighbors: int32 [128, 4], P(('wide', 'narrow')), may hold values from 0 to 7
- slot_mask: int32 [128, 4], P(('wide', 'narrow')), may hold values 0 or 1
- send_list: int32 [128], P(('wide', 'narrow')), may hold values from 0 to 3
- aggregate: int32 [128, 128], P(('wide', 'narrow')), may hold values from 0 to 127
- coarse_inverse: float32 [512, 512], P(('wide', 'narrow')), may hold values from -0.03125 to 0.03125
Outputs:
- correction: float32 [128, 24, 128], P(('wide', 'narrow'))
- residual: float32 [128, 24, 128], P(('wide', 'narrow'))
Inputs may be any that keep to these rules, and one draw needn't show every extreme that they name: `neighbors`: indices into the extended list of the block's group. `send_list`: block indices within the sending group. aggregate indices among the 128 aggregates of the particle's wide coordinate.
All inputs are finite; a program needn't handle non-finite values. No bound on the sum of `slot_mask` on one device may be relied on, other than what follows from the above.
Results may differ from a plain program's by a relative error of at most 0.00025.
Values sent between devices are 32-bit elements; how exact they have to be, the bound alone decides.
No kernel may reach another device: no remote copies, remote signals or barrier semaphores. Data moves between devices by JAX's collectives and lax.ppermute only.
A program may use at most 64 MiB of HBM per device.

v0:
```python
import jax
import jax.numpy as jnp
from jax import lax
from jax.sharding import PartitionSpec as P

SWEEPS = 2


highest = lax.Precision.HIGHEST


def with_halo(block, sides, width):
    for axis, dim in sides:
        count = lax.axis_size(axis)
        forward = [(i, i + 1) for i in range(count - 1)]
        backward = [(target, source) for source, target in forward]
        low = lax.ppermute(
            lax.slice_in_dim(block, block.shape[dim] - width, None, axis=dim), axis, forward
        )
        high = lax.ppermute(lax.slice_in_dim(block, 0, width, axis=dim), axis, backward)
        block = jnp.concatenate([low, block, high], axis=dim)
    return block


def shards(loads, diagonal, stiffness, neighbors, slot_mask, send_list, aggregate, coarse_inverse):
    ghost_rows = send_list.shape[0] // 2
    live_slots = slot_mask.astype(jnp.float32)
    diag_rows = diagonal[:, None, :]

    def operate(vector):
        outgoing = jnp.take(vector, send_list, axis=0)
        padded = with_halo(outgoing, (("wide", 0),), ghost_rows)
        extended = jnp.concatenate([vector, padded[:ghost_rows], padded[3 * ghost_rows :]], axis=0)
        gathered = jnp.take(extended, neighbors, axis=0) * live_slots[:, :, None, None]
        coupled = jnp.einsum("bscj,bsij->bci", gathered, stiffness, precision=highest)
        return diag_rows * vector - coupled

    scaled = loads / diag_rows
    row_sums = jnp.sum(jnp.sum(jnp.abs(stiffness), axis=3) * live_slots[:, :, None], axis=1)
    local_peak = jnp.max(row_sums / diagonal)
    upper_bound = 1.0 + lax.pmax(local_peak, ("wide", "narrow"))
    centre = 0.625 * upper_bound
    direction = scaled / centre
    applied = operate(direction)
    half_span = 0.375 * upper_bound
    spread_ratio = 5.0 / 3.0
    weight_prev = 0.6
    solution = direction
    remainder = loads
    for sweep_index in range(SWEEPS):
        if sweep_index > 0:
            applied = operate(direction)
        remainder = remainder - applied
        weight_now = 1.0 / (2.0 * spread_ratio - weight_prev)
        direction = (
            weight_now * weight_prev * direction
            + 2.0 * weight_now / half_span * remainder / diag_rows
        )
        solution = solution + direction
        weight_prev = weight_now
    residual = remainder - operate(direction)
    agg_cols = coarse_inverse.shape[0] * lax.axis_size("narrow")
    one_hot = (
        aggregate[:, :, None] == jnp.arange(agg_cols, dtype=jnp.int32)[None, None, :]
    ).astype(jnp.float32)
    part_sums = jnp.einsum("bci,big->cg", residual, one_hot, precision=highest)
    group_total = lax.psum(part_sums, "narrow")
    coarse_own = jnp.einsum(
        "ch,kh->ck",
        lax.all_gather(group_total, "wide", axis=1, tiled=True),
        coarse_inverse,
        precision=highest,
    )
    coarse_group = lax.all_gather(coarse_own, "narrow", axis=1, tiled=True)
    spread_back = jnp.einsum("cg,big->bci", coarse_group, one_hot, precision=highest)
    return (solution + spread_back, residual)


def solution(mesh):
    return jax.shard_map(
        shards,
        mesh=mesh,
        in_specs=(
            P(("wide", "narrow"), None, None),
            P(("wide", "narrow"), None),
            P(("wide", "narrow"), None, None, None),
            P(("wide", "narrow"), None),
            P(("wide", "narrow"), None),
            P(("wide", "narrow")),
            P(("wide", "narrow"), None),
            P(("wide", "narrow"), None),
        ),
        out_specs=(P(("wide", "narrow"), None, None), P(("wide", "narrow"), None, None)),
        check_vma=False,
    )
```

profile of v0, /device:TPU:0, one launch (start us, length us, event | category | flops | bytes accessed | tf_op | source)
XLA Modules:
  0.0 149.0 jit_solution(17401296957608247365)
XLA Ops:
  0.6 0.0 copy-start
  0.6 0.0 copy-start.8
  0.7 0.0 copy-start.6
  0.7 0.7 compare_and_fusion.1
  1.4 0.0 copy-done.8
  1.4 0.0 copy-done.6
  1.4 0.0 copy-start.1
  1.4 1.7 %abs_reduce_fusion = f32[4,4,128]{2,1,0:T(4,128)S(1)} fusion(f32[4,4,128,128]{3,2,1,0:T(8,128)} %param.14), kind=kLoop, calls=%fused_computation.18 | loop fusion | flops 522240 | bytes 1056768 | tf_op jit(solution)/shard_map/reduce_sum | solution.py:39
  3.1 0.0 copy-start.3
  3.1 0.1 multiply_reduce_fusion
  3.2 0.6 copy-done.3
  3.8 0.6 divide_reduce_fusion
  4.4 42.2 %pmax.7 = f32[]{:T(128)} all-reduce(f32[]{:T(128)} %divide_reduce_fusion), channel_id=1, replica_groups=mesh['wide'=4,'narrow'=8] {'wide','narrow'}, use_global_device_ids=true, to_apply=%region_3.0 | all-reduce | flops 1 | bytes 8 | tf_op jit(solution)/shard_map/pmax | solution.py:41
  47.2 0.8 broadcast_divide_fusion
  48.0 0.6 gather_fusion
  48.6 0.1 broadcast_select_fusion.2
  48.7 0.0 copy-start.5
  48.7 1.3 collective-permute-start
  50.0 1.3 collective-permute-start.1
  51.3 0.0 copy-done.5
  51.3 0.1 reshape.77
  51.5 0.0 collective-permute-done
  51.5 4.3 %collective-permute-done.1 = f32[2,24,128]{2,1,0:T(8,128)S(1)} collective-permute-done((f32[2,24,128]{2,1,0:T(8,128)S(1)}, f32[2,24,128]{2,1,0:T(8,128)S(1)}, u32[]{:S(2)}, u32[]{:S(2)}) %collective-permute-start.1) | collective-permute-done | bytes 24608 | tf_op jit(solution)/shard_map/ppermute | solution.py:20
  55.8 0.0 copy-start.2
  55.8 0.6 gather_fusion.1
  56.4 0.0 copy-done.1
  56.4 0.2 copy-done.2
  56.6 1.0 divide_add_fusion.1
  57.6 0.6 gather_fusion.2
  58.2 0.1 broadcast_select_fusion.1
  58.3 4.5 %collective-permute-start.2 = (f32[2,24,128]{2,1,0:T(8,128)S(1)}, f32[2,24,128]{2,1,0:T(8,128)S(1)}, u32[]{:S(2)}, u32[]{:S(2)}) collective-permute-start(f32[2,24,128]{2,1,0:T(8,128)S(1)} %get-tuple-element.6), channel_id=1, source_target_pairs={{0,8},{8,16},{16,24},{1,9},{9,17},{17,25},{2,10},{10,18},{18,26},{... | collective-permute-start | bytes 73736 | tf_op jit(solution)/shard_map/ppermute | solution.py:17
  62.7 1.3 collective-permute-start.3
  64.1 0.0 collective-permute-done.2
  64.1 1.7 %collective-permute-done.3 = f32[2,24,128]{2,1,0:T(8,128)S(1)} collective-permute-done((f32[2,24,128]{2,1,0:T(8,128)S(1)}, f32[2,24,128]{2,1,0:T(8,128)S(1)}, u32[]{:S(2)}, u32[]{:S(2)}) %collective-permute-start.3) | collective-permute-done | bytes 24608 | tf_op jit(solution)/shard_map/ppermute | solution.py:20
  65.8 0.6 gather_fusion.3
  66.4 1.0 divide_add_fusion
  67.4 0.6 gather_fusion.4
  68.0 0.1 broadcast_select_fusion
  68.1 4.0 %collective-permute-start.4 = (f32[2,24,128]{2,1,0:T(8,128)S(1)}, f32[2,24,128]{2,1,0:T(8,128)S(1)}, u32[]{:S(2)}, u32[]{:S(2)}) collective-permute-start(f32[2,24,128]{2,1,0:T(8,128)S(1)} %get-tuple-element.4), channel_id=1, source_target_pairs={{0,8},{8,16},{16,24},{1,9},{9,17},{17,25},{2,10},{10,18},{18,26},{... | collective-permute-start | bytes 73736 | tf_op jit(solution)/shard_map/ppermute | solution.py:17
  72.1 1.3 collective-permute-start.5
  73.4 0.0 collective-permute-done.4
  73.4 1.8 %collective-permute-done.5 = f32[2,24,128]{2,1,0:T(8,128)S(1)} collective-permute-done((f32[2,24,128]{2,1,0:T(8,128)S(1)}, f32[2,24,128]{2,1,0:T(8,128)S(1)}, u32[]{:S(2)}, u32[]{:S(2)}) %collective-permute-start.5) | collective-permute-done | bytes 24608 | tf_op jit(solution)/shard_map/ppermute | solution.py:20
  75.2 0.6 gather_fusion.5
  75.7 0.0 copy-start.7
  75.8 1.0 fusion.6
  76.8 0.0 copy-done.7
  76.8 0.0 copy-start.4
  76.8 0.3 convolution_bitcast_fusion.4
  77.1 35.1 %psum.7 = f32[24,128]{1,0:T(8,128)S(1)} all-reduce(f32[24,128]{1,0:T(8,128)S(1)} %convolution_bitcast_fusion.4), channel_id=1, replica_groups=mesh['wide'=4,'narrow'=8] {'narrow'}, use_global_device_ids=true, to_apply=%region_4.7 | all-reduce | flops 3072 | bytes 24576 | tf_op jit(solution)/shard_map/psum | solution.py:67
  112.1 0.0 copy-done.4
  112.1 5.2 %all_gather.6 = f32[24,512]{1,0:T(8,128)S(1)} all-gather(f32[24,128]{1,0:T(8,128)S(1)} %psum.7), channel_id=1, replica_groups=mesh['wide'=4,'narrow'=8] {'wide'}, dimensions={1}, use_global_device_ids=true | all-gather | bytes 61440 | tf_op jit(solution)/shard_map/all_gather | solution.py:70
  117.3 0.0 copy-done
  117.3 0.2 fusion.25
  117.5 30.5 %all_gather.7 = f32[24,128]{0,1:T(8,128)S(1)} all-gather(f32[24,16]{0,1:T(8,128)S(1)} %fusion.25), channel_id=1, replica_groups=mesh['wide'=4,'narrow'=8] {'narrow'}, dimensions={1}, use_global_device_ids=true | all-gather | bytes 13824 | tf_op jit(solution)/shard_map/all_gather | solution.py:74
  148.0 1.0 fusion
  (13 shorter events, 0.1 us)
Async XLA Ops:
  0.6 116.7 %copy-start = (f32[16,512]{1,0:T(8,128)S(1)}, f32[16,512]{1,0:T(8,128)}, u32[]{:S(2)}) copy-start(f32[16,512]{1,0:T(8,128)} %param.19) | copy-start | bytes 98308
  0.6 0.7 copy-start.8
  0.7 0.7 copy-start.6
  1.4 55.0 %copy-start.1 = (f32[4,4,128,128]{3,2,1,0:T(8,128)S(1)}, f32[4,4,128,128]{3,2,1,0:T(8,128)}, u32[]{:S(2)}) copy-start(f32[4,4,128,128]{3,2,1,0:T(8,128)} %param.14) | copy-start | bytes 3145732
  3.1 0.7 copy-start.3
  48.7 2.6 %copy-start.5 = (s32[4,4]{1,0:T(4,128)S(1)}, s32[4,4]{1,0:T(4,128)}, u32[]{:S(2)}) copy-start(s32[4,4]{1,0:T(4,128)} %param.15) | copy-start | bytes 196
  48.7 2.8 %collective-permute-start = (f32[2,24,128]{2,1,0:T(8,128)S(1)}, f32[2,24,128]{2,1,0:T(8,128)S(1)}, u32[]{:S(2)}, u32[]{:S(2)}) collective-permute-start(f32[2,24,128]{2,1,0:T(8,128)S(1)} %get-tuple-element.8), channel_id=1, source_target_pairs={{0,8},{8,16},{16,24},{1,9},{9,17},{17,25},{2,10},{10,18},{18,26},{... | collective-permute-start | bytes 73736 | tf_op jit(solution)/shard_map/ppermute | solution.py:17
  50.0 5.8 %collective-permute-start.1 = (f32[2,24,128]{2,1,0:T(8,128)S(1)}, f32[2,24,128]{2,1,0:T(8,128)S(1)}, u32[]{:S(2)}, u32[]{:S(2)}) collective-permute-start(f32[2,24,128]{2,1,0:T(8,128)S(1)} %get-tuple-element.9), channel_id=1, source_target_pairs={{8,0},{16,8},{24,16},{9,1},{17,9},{25,17},{10,2},{18,10},{26,18},{... | collective-permute-start | bytes 73736 | tf_op jit(solution)/shard_map/ppermute | solution.py:20
  55.8 0.8 copy-start.2
  58.3 5.8 %collective-permute-start.2 = (f32[2,24,128]{2,1,0:T(8,128)S(1)}, f32[2,24,128]{2,1,0:T(8,128)S(1)}, u32[]{:S(2)}, u32[]{:S(2)}) collective-permute-start(f32[2,24,128]{2,1,0:T(8,128)S(1)} %get-tuple-element.6), channel_id=1, source_target_pairs={{0,8},{8,16},{16,24},{1,9},{9,17},{17,25},{2,10},{10,18},{18,26},{... | collective-permute-start | bytes 73736 | tf_op jit(solution)/shard_map/ppermute | solution.py:17
  62.7 3.1 %collective-permute-start.3 = (f32[2,24,128]{2,1,0:T(8,128)S(1)}, f32[2,24,128]{2,1,0:T(8,128)S(1)}, u32[]{:S(2)}, u32[]{:S(2)}) collective-permute-start(f32[2,24,128]{2,1,0:T(8,128)S(1)} %get-tuple-element.7), channel_id=1, source_target_pairs={{8,0},{16,8},{24,16},{9,1},{17,9},{25,17},{10,2},{18,10},{26,18},{... | collective-permute-start | bytes 73736 | tf_op jit(solution)/shard_map/ppermute | solution.py:20
  68.1 5.3 %collective-permute-start.4 = (f32[2,24,128]{2,1,0:T(8,128)S(1)}, f32[2,24,128]{2,1,0:T(8,128)S(1)}, u32[]{:S(2)}, u32[]{:S(2)}) collective-permute-start(f32[2,24,128]{2,1,0:T(8,128)S(1)} %get-tuple-element.4), channel_id=1, source_target_pairs={{0,8},{8,16},{16,24},{1,9},{9,17},{17,25},{2,10},{10,18},{18,26},{... | collective-permute-start | bytes 73736 | tf_op jit(solution)/shard_map/ppermute | solution.py:17
  72.1 3.1 %collective-permute-start.5 = (f32[2,24,128]{2,1,0:T(8,128)S(1)}, f32[2,24,128]{2,1,0:T(8,128)S(1)}, u32[]{:S(2)}, u32[]{:S(2)}) collective-permute-start(f32[2,24,128]{2,1,0:T(8,128)S(1)} %get-tuple-element.5), channel_id=1, source_target_pairs={{8,0},{16,8},{24,16},{9,1},{17,9},{25,17},{10,2},{18,10},{26,18},{... | collective-permute-start | bytes 73736 | tf_op jit(solution)/shard_map/ppermute | solution.py:20
  75.7 1.0 copy-start.7
  76.8 35.4 %copy-start.4 = (f32[4,24,128]{2,1,0:T(8,128)}, f32[4,24,128]{2,1,0:T(8,128)S(1)}, u32[]{:S(2)}) copy-start(f32[4,24,128]{2,1,0:T(8,128)S(1)} %fusion.6) | copy-start | bytes 147460
where the time goes:
time: 150 us; the launch traced here: 149 us
  blocking collectives  113 us (75%)
  starting transfers between devices  13.6 us (9%)
  waiting for transfers between devices  7.83 us (5%)
  matrix products  4.43 us (3%)
  local copies, waits for them, and re-layouts  4.31 us (3%)
  other arithmetic  4.17 us (3%)
  between operations  1.67 us (1%)
    pmax x1, blocking collectives, shards(): upper_bound = 1.0 + lax.pmax(local_peak, ('wide', 'narrow'))  42.2 us
    psum x1, blocking collectives, shards(): group_total = lax.psum(part_sums, 'narrow')  35.1 us
    all_gather x1, blocking collectives, shards(): coarse_group = lax.all_gather(coarse_own, 'narrow', axis=1, tiled=True)  30.5 us
    ppermute x3, starting transfers between devices, with_halo(): lax.ppermute(lax.slice_in_dim(block, block.shape[dim] - width, None, axis...  9.73 us
    ppermute x3, waiting for transfers between devices, with_halo(): lax.ppermute(lax.slice_in_dim(block, 0, width, axis=dim), axis, backward)  7.82 us
    all_gather x1, blocking collectives, shards(): lax.all_gather(group_total, 'wide', axis=1, tiled=True)  5.21 us
    ppermute x3, starting transfers between devices, with_halo(): lax.ppermute(lax.slice_in_dim(block, 0, width, axis=dim), axis, backward)  3.88 us
    dot_general x3, matrix products, operate(): jnp.einsum('bscj,bsij->bci', gathered, stiffness, precision=highest)  3.03 us
  transfers between devices with their start and end apart: 6, of which 3 were waited for; matrix products, arithmetic and copies ran while one was open for 0% of the time, Pallas kernels for 0%

commit v1 on v0

v1 whole, which is shorter than its diff:
```python
import functools

import jax
import jax.numpy as jnp
from jax import lax
from jax.experimental import pallas as pl
from jax.experimental.pallas import tpu as pltpu
from jax.sharding import PartitionSpec as P

SWEEPS = 2
AXES = ("wide", "narrow")

VMEM = pl.BlockSpec(memory_space=pltpu.VMEM)
SMEM = pl.BlockSpec(memory_space=pltpu.SMEM)
LIMIT = pltpu.CompilerParams(vmem_limit_bytes=32 * 1024 * 1024)

f32 = jnp.float32
bf16 = jnp.bfloat16
TRANSPOSED = (((1,), (1,)), ((), ()))


def like(*shape, dtype=f32):
    return jax.ShapeDtypeStruct(shape, dtype)


def split(value):
    high = value.astype(bf16).astype(f32)
    return high, value - high


def parity():
    return lax.rem(lax.axis_index("wide"), 2)


def write_messages(send_ref, field_ref, near_ref, far_ref):
    odd = parity()
    ghosts = near_ref.shape[0]
    for j in range(ghosts):
        near_ref[j] = field_ref[send_ref[(1 - odd) * ghosts + j]]
        far_ref[j] = field_ref[send_ref[odd * ghosts + j]]


def start_kernel(send_ref, loads_ref, diagonal_ref, field_ref, near_ref, far_ref):
    for b in range(loads_ref.shape[0]):
        field_ref[b] = loads_ref[b] / diagonal_ref[b : b + 1, :]
    write_messages(send_ref, field_ref, near_ref, far_ref)


def prepare_kernel(mask_ref, stiffness_ref, diagonal_ref, parts_ref, peak_ref):
    blocks, slots, size, _ = stiffness_ref.shape
    peak = jnp.zeros((8, size), f32)
    for b in range(blocks):
        total = jnp.zeros((size, size), f32)
        for s in range(slots):
            live = stiffness_ref[b, s] * mask_ref[b, s].astype(f32)
            high, low = split(live)
            parts_ref[b, 0:size, s * size : (s + 1) * size] = high.astype(bf16)
            parts_ref[b, size : 2 * size, s * size : (s + 1) * size] = low.astype(bf16)
            total = total + jnp.abs(live)
        rows = lax.dot_general(
            jnp.ones((8, size), f32), total, TRANSPOSED,
            precision=lax.Precision.HIGHEST, preferred_element_type=f32,
        )
        peak = jnp.maximum(peak, rows / diagonal_ref[b : b + 1, :])
    peak_ref[...] = jnp.broadcast_to(jnp.max(peak, axis=1, keepdims=True), peak.shape)


def couple(neighbors_ref, field_ref, near_ref, far_ref, parts_ref, extended_ref, b_out):
    blocks, comps, size = field_ref.shape
    slots = neighbors_ref.shape[1]
    ghosts = near_ref.shape[0]
    wide = lax.axis_size("wide")
    me = lax.axis_index("wide")
    odd = parity()
    inside = jnp.where((me == 0) | (me == wide - 1), 0.0, 1.0).astype(f32)

    def put(place, value):
        extended_ref[place] = jnp.concatenate(split(value), axis=0).astype(bf16)

    for b in range(blocks):
        put(b, field_ref[b])
    for j in range(ghosts):
        put(blocks + j, near_ref[j])
        put(blocks + ghosts + j, far_ref[j] * inside)
    for b in range(blocks):
        rows = []
        for s in range(slots):
            entry = neighbors_ref[b, s]
            lower = entry < blocks + ghosts
            swapped = jnp.where(lower, entry + ghosts, entry - ghosts)
            entry = jnp.where((entry >= blocks) & (odd == 0), swapped, entry)
            rows.append(extended_ref[entry])
        product = lax.dot_general(
            jnp.concatenate(rows, axis=1), parts_ref[b], TRANSPOSED, preferred_element_type=f32
        )
        b_out(b, product[:comps, :size] + product[:comps, size:] + product[comps:, :size])


def step_kernel(
    neighbors_ref, send_ref, field_ref, near_ref, far_ref, parts_ref, diagonal_ref,
    next_ref, near_out, far_out, extended_ref,
):
    def put(b, coupled):
        next_ref[b] = coupled / diagonal_ref[b : b + 1, :]

    couple(neighbors_ref, field_ref, near_ref, far_ref, parts_ref, extended_ref, put)
    write_messages(send_ref, next_ref, near_out, far_out)


def coefficients(upper):
    half_span = 0.375 * upper
    zero = jnp.zeros_like(upper)
    ratio = 5.0 / 3.0
    before = 0.6

    def applied(d):
        return [d[0]] + [d[k] - d[k - 1] for k in range(1, len(d))] + [-d[-1]]

    def less(a, b):
        a = a + [zero] * (len(b) - len(a))
        return [x - y for x, y in zip(a, b)]

    direction = [1.0 / (0.625 * upper)]
    answer = list(direction)
    remainder = [jnp.ones_like(upper)]
    for _ in range(SWEEPS):
        remainder = less(remainder, applied(direction))
        now = 1.0 / (2.0 * ratio - before)
        longer = direction + [zero]
        direction = [now * before * d + (2.0 * now / half_span) * r for d, r in zip(longer, remainder)]
        answer = [a + d for a, d in zip(answer + [zero], direction)]
        before = now
    return less(remainder, applied(direction)), answer


def last_kernel(
    neighbors_ref, field0_ref, field1_ref, field2_ref, near_ref, far_ref, parts_ref, diagonal_ref, peak_ref, aggregate_ref,
    residual_ref, answer_ref, sums_ref, extended_ref,
):
    blocks, comps, size = field0_ref.shape
    members = sums_ref.shape[1]
    on_residual, on_answer = coefficients(1.0 + peak_ref[0:1, :])

    def put(b, coupled):
        scale = diagonal_ref[b : b + 1, :]
        fields = [field0_ref[b], field1_ref[b], field2_ref[b], coupled / scale]
        residual_ref[b] = scale * sum(c * f for c, f in zip(on_residual, fields))
        answer_ref[b] = sum(c * f for c, f in zip(on_answer, fields))

    couple(neighbors_ref, field2_ref, near_ref, far_ref, parts_ref, extended_ref, put)
    index = lax.broadcasted_iota(jnp.int32, (members, size), 0)
    values, places = [], []
    for b in range(blocks):
        values.append(jnp.concatenate(split(residual_ref[b]), axis=0).astype(bf16))
        places.append((index == aggregate_ref[b : b + 1, :]).astype(f32).astype(bf16))
    product = lax.dot_general(
        jnp.concatenate(values, axis=1), jnp.concatenate(places, axis=1), TRANSPOSED, preferred_element_type=f32
    )
    sums_ref[...] = product[:comps] + product[comps:]


def coarse_kernel(own_ref, other_ref, inverse_ref, aggregate_ref, answer_ref, correction_ref):
    blocks, comps, size = answer_ref.shape
    members, unknowns = inverse_ref.shape
    odd = parity()
    rank = lax.axis_index("narrow")
    rows_each = members // lax.axis_size("narrow")
    own, other = own_ref[...], other_ref[...]
    rhs = jnp.where(odd == 0, jnp.concatenate([own, other], axis=0), jnp.concatenate([other, own], axis=0))
    left = jnp.concatenate(split(rhs), axis=0).astype(bf16)
    right = jnp.concatenate(split(inverse_ref[...]), axis=0).astype(bf16)
    product = lax.dot_general(left, right, TRANSPOSED, preferred_element_type=f32)
    found = product[:comps, :members] + product[:comps, members:] + product[comps:, :members]
    found = jnp.concatenate(split(found), axis=0).astype(bf16)
    index = lax.broadcasted_iota(jnp.int32, (members, size), 0) ^ (rank * rows_each)
    for b in range(blocks):
        place = (index == aggregate_ref[b : b + 1, :]).astype(f32).astype(bf16)
        spread = jnp.dot(found, place, preferred_element_type=f32)
        correction_ref[b] = answer_ref[b] + spread[:comps] + spread[comps:]


def swap(value, axis, bit):
    return lax.ppermute(value, axis, [(i, i ^ bit) for i in range(lax.axis_size(axis))])


def swap_far(value):
    count = lax.axis_size("wide")
    return lax.ppermute(value, "wide", [(i, (i + 1 if i % 2 else i - 1) % count) for i in range(count)])


def bits(axis):
    return [1 << k for k in range(lax.axis_size(axis).bit_length() - 1)]


def shards(loads, diagonal, stiffness, neighbors, slot_mask, send_list, aggregate, coarse_inverse):
    blocks, comps, size = loads.shape
    slots = neighbors.shape[1]
    ghosts = send_list.shape[0] // 2
    wide, narrow = lax.axis_size("wide"), lax.axis_size("narrow")
    members = coarse_inverse.shape[0] * narrow
    field = like(blocks, comps, size)
    message = like(ghosts, comps, size)
    extended = pltpu.VMEM((blocks + 2 * ghosts, 2 * comps, size), bf16)

    def call(kernel, in_specs, out_shape, scratch=()):
        return pl.pallas_call(
            kernel, in_specs=in_specs, out_specs=jax.tree.map(lambda _: VMEM, out_shape), out_shape=out_shape,
            scratch_shapes=scratch, compiler_params=LIMIT,
        )

    field0, near, far = call(start_kernel, [SMEM, VMEM, VMEM], (field, message, message))(send_list, loads, diagonal)
    near, far = swap(near, "wide", 1), swap_far(far)
    parts, peak = call(
        prepare_kernel, [SMEM, VMEM, VMEM],
        (like(blocks, 2 * size, slots * size, dtype=bf16), like(8, size)),
    )(slot_mask, stiffness, diagonal)

    for axis in AXES:
        for bit in bits(axis):
            peak = jnp.maximum(peak, swap(peak, axis, bit))
    inverse = coarse_inverse
    for bit in bits("narrow"):
        inverse = jnp.concatenate([inverse, swap(inverse, "narrow", bit)], axis=0)

    step = call(step_kernel, [SMEM] * 2 + [VMEM] * 5, (field, message, message), [extended])
    field1, near, far = step(neighbors, send_list, field0, near, far, parts, diagonal)
    near, far = swap(near, "wide", 1), swap_far(far)
    field2, near, far = step(neighbors, send_list, field1, near, far, parts, diagonal)
    near, far = swap(near, "wide", 1), swap_far(far)
    residual, answer, sums = call(
        last_kernel, [SMEM] + [VMEM] * 9, (field, field, like(comps, members)), [extended]
    )(neighbors, field0, field1, field2, near, far, parts, diagonal, peak, aggregate)

    half = comps // 2
    quarter = half // 4
    outgoing = jnp.broadcast_to(
        sums.reshape(1, 2, 1, quarter, 4, members), (wide // 2, 2, narrow, quarter, 4, members)
    ).reshape(wide * narrow, quarter, 4, members)
    incoming = lax.all_to_all(outgoing, AXES, 0, 0)
    own = incoming.reshape(wide, narrow, half, members).sum(axis=1)
    own = own.transpose(1, 0, 2).reshape(half, wide * members)
    other = swap(own, "wide", 1)
    correction = call(coarse_kernel, [VMEM] * 5, field)(own, other, inverse, aggregate, answer)
    return correction, residual


def solution(mesh):
    return jax.shard_map(
        shards,
        mesh=mesh,
        in_specs=(
            P(AXES, None, None),
            P(AXES, None),
            P(AXES, None, None, None),
            P(AXES, None),
            P(AXES, None),
            P(AXES),
            P(AXES, None),
            P(AXES, None),
        ),
        out_specs=(P(AXES, None, None), P(AXES, None, None)),
        check_vma=False,
    )
```

time: 150 us -> 60.1 us (0.40)
  blocking collectives: 113 us -> 0 us
  waiting for transfers between devices: 7.83 us -> 22.4 us
  starting transfers between devices: 13.6 us -> 24.5 us
  Pallas kernels: 0 us -> 6.53 us
  matrix products: 4.43 us -> 0 us
  other arithmetic: 4.17 us -> 0.08 us
    pmax x1 -> x0, blocking collectives: 42.2 us -> none  [shards(): upper_bound = 1.0 + lax.pmax(local_peak, ('wide', 'narrow'))]
    all_gather x2 -> x0, blocking collectives: 35.7 us -> none  [the longest x1 30.5 us: shards(): coarse_group = lax.all_gather(coarse_own, 'narrow', axis=1, tiled=True)]
    psum x1 -> x0, blocking collectives: 35.1 us -> none  [shards(): group_total = lax.psum(part_sums, 'narrow')]
    ppermute x6 -> x15, waiting for transfers between devices: 7.83 us -> 22.4 us  [the longest x12 20.2 us: swap(): lax.ppermute(value, axis, [(i, i ^ bit) for i in range(lax.axis_size(axis...]
    pallas_call x0 -> x6, Pallas kernels: none -> 6.53 us  [the longest x1 1.62 us: shards(): call(last_kernel, [SMEM] + [VMEM] * 9, (field, field, like(comps, members...]
    all_to_all x0 -> x1, starting transfers between devices: none -> 5.89 us  [shards(): incoming = lax.all_to_all(outgoing, AXES, 0, 0)]
    ppermute x6 -> x15, starting transfers between devices: 13.6 us -> 18.6 us  [the longest x12 15.3 us: swap(): lax.ppermute(value, axis, [(i, i ^ bit) for i in range(lax.axis_size(axis...]
    dot_general x6 -> x0, matrix products: 4.43 us -> none  [the longest x3 3.03 us: operate(): jnp.einsum('bscj,bsij->bci', gathered, stiffness, precision=highest)]
  transfers between devices with their start and end apart: 6 -> 16, of which waited for: 3 -> 10; matrix products, arithmetic and copies ran while one was open for 0% -> 0% of each run, Pallas kernels for 0% -> 2%
where the time goes in v1:
time: 60.1 us; the launch traced here: 59.7 us
  starting transfers between devices  24.5 us (41%)
  waiting for transfers between devices  22.4 us (37%)
  Pallas kernels  6.53 us (11%)
  local copies, waits for them, and re-layouts  5.45 us (9%)
  between operations  0.77 us (1%)
    ppermute x12, waiting for transfers between devices, swap(): lax.ppermute(value, axis, [(i, i ^ bit) for i in range(lax.axis_size(axis...  20.2 us
    ppermute x12, starting transfers between devices, swap(): lax.ppermute(value, axis, [(i, i ^ bit) for i in range(lax.axis_size(axis...  15.3 us
    all_to_all x1, starting transfers between devices, shards(): incoming = lax.all_to_all(outgoing, AXES, 0, 0)  5.89 us
    unnamed x21, local copies, waits for them, and re-layouts  4.72 us
    ppermute x3, starting transfers between devices, swap_far(): lax.ppermute(value, 'wide', [(i, (i + 1 if i % 2 else i - 1) % count) for...  3.32 us
    ppermute x3, waiting for transfers between devices, swap_far(): lax.ppermute(value, 'wide', [(i, (i + 1 if i % 2 else i - 1) % count) for...  2.15 us
    pallas_call x1, Pallas kernels, shards(): call(last_kernel, [SMEM] + [VMEM] * 9, (field, field, like(comps, members...  1.62 us
    pallas_call x1, Pallas kernels, shards(): call(prepare_kernel, [SMEM, VMEM, VMEM], (like(blocks, 2 * size, slots *...  1.29 us
  transfers between devices with their start and end apart: 16, of which 10 were waited for; matrix products, arithmetic and copies ran while one was open for 0% of the time, Pallas kernels for 2%

profile of v1, /device:TPU:0, one launch (start us, length us, event | category | flops | bytes accessed | tf_op | source)
XLA Modules:
  0.0 59.7 jit_solution(5402607444803832956)
XLA Ops:
  0.6 0.0 copy-start.1
  0.6 0.7 %copy-done.1 = f32[4,128]{1,0:T(4,128)S(1)} copy-done((f32[4,128]{1,0:T(4,128)S(1)}, f32[4,128]{1,0:T(4,128)}, u32[]{:S(2)}) %copy-start.1) | copy-done | bytes 2072
  1.3 0.0 copy-start.3
  1.3 0.8 %copy-done.3 = f32[4,24,128]{2,1,0:T(8,128)S(1)} copy-done((f32[4,24,128]{2,1,0:T(8,128)S(1)}, f32[4,24,128]{2,1,0:T(8,128)}, u32[]{:S(2)}) %copy-start.3) | copy-done | bytes 49176
  2.1 0.0 copy-start.6
  2.1 0.7 %copy-done.6 = s32[4]{0:T(128)S(1)} copy-done((s32[4]{0:T(128)S(1)}, s32[4]{0:T(128)}, u32[]{:S(2)}) %copy-start.6) | copy-done | bytes 40
  2.8 0.0 copy-start.7
  2.8 0.6 shard_map.95
  3.3 0.0 copy-start.2
  3.4 0.5 collective-permute-start
  3.9 2.6 %collective-permute-start.1 = (f32[2,24,128]{2,1,0:T(8,128)S(1)}, f32[2,24,128]{2,1,0:T(8,128)S(1)}, u32[]{:S(2)}, u32[]{:S(2)}) collective-permute-start(f32[2,24,128]{2,1,0:T(8,128)S(1)} %get-tuple-element.18), channel_id=1, source_target_pairs={{0,24},{8,16},{16,8},{24,0},{1,25},{9,17},{17,9},{25,1},{2,26},{10... | collective-permute-start | bytes 73736 | tf_op jit(solution)/shard_map/ppermute | solution.py:188
  6.5 0.0 copy-done.7
  6.5 0.0 copy-done.2
  6.5 0.0 copy-start
  6.5 1.2 %copy-done = f32[4,4,128,128]{3,2,1,0:T(8,128)S(1)} copy-done((f32[4,4,128,128]{3,2,1,0:T(8,128)S(1)}, f32[4,4,128,128]{3,2,1,0:T(8,128)}, u32[]{:S(2)}) %copy-start) | copy-done | bytes 1048600
  7.7 1.3 %shard_map.96 = (bf16[4,256,512]{2,1,0:T(8,128)(2,1)S(1)}, f32[8,128]{1,0:T(8,128)S(1)}) custom-call(s32[4,4]{1,0:T(4,128)S(1)} %copy-done.7, f32[4,4,128,128]{3,2,1,0:T(8,128)S(1)} %copy-done, f32[4,128]{1,0:T(4,128)S(1)} %copy-done.2), custom_call_target="tpu_custom_call" | custom-call | tf_op jit(solution)/shard_map/pallas_call | solution.py:213
  9.0 0.0 copy-start.4
  9.0 0.0 collective-permute-done.near_ref
  9.0 0.0 collective-permute-done.1.far_ref
  9.1 0.7 %copy-done.4 = s32[4,4]{1,0:T(4,128)S(1)} copy-done((s32[4,4]{1,0:T(4,128)S(1)}, s32[4,4]{1,0:T(4,128)}, u32[]{:S(2)}) %copy-start.4) | copy-done | bytes 88
  9.7 1.0 %shard_map.97 = (f32[4,24,128]{2,1,0:T(8,128)S(1)}, f32[2,24,128]{2,1,0:T(8,128)S(1)}, f32[2,24,128]{2,1,0:T(8,128)S(1)}) custom-call(s32[4,4]{1,0:T(4,128)S(1)} %copy-done.4, s32[4]{0:T(128)S(1)} %copy-done.6, f32[4,24,128]{2,1,0:T(8,128)S(1)} %get-tuple-element.16.field_ref.field0_ref, f32[2,24,128]{2,1,0:T(8,128)S(1)} %collective-permute-done.near_ref, ...), custom_call_target="tpu_custom_call" | custom-call | tf_op jit(solution)/shard_map/pallas_call | solution.py:226
  10.7 0.1 collective-permute-start.2
  10.9 0.5 collective-permute-start.3
  11.4 0.6 %collective-permute-done.2.near_ref = f32[2,24,128]{2,1,0:T(8,128)S(1)} collective-permute-done((f32[2,24,128]{2,1,0:T(8,128)S(1)}, f32[2,24,128]{2,1,0:T(8,128)S(1)}, u32[]{:S(2)}, u32[]{:S(2)}) %collective-permute-start.2) | collective-permute-done | bytes 24608 | tf_op jit(solution)/shard_map/ppermute | solution.py:183
  12.0 2.1 %collective-permute-done.3.far_ref = f32[2,24,128]{2,1,0:T(8,128)S(1)} collective-permute-done((f32[2,24,128]{2,1,0:T(8,128)S(1)}, f32[2,24,128]{2,1,0:T(8,128)S(1)}, u32[]{:S(2)}, u32[]{:S(2)}) %collective-permute-start.3) | collective-permute-done | bytes 24608 | tf_op jit(solution)/shard_map/ppermute | solution.py:188
  14.1 1.0 %shard_map.98 = (f32[4,24,128]{2,1,0:T(8,128)S(1)}, f32[2,24,128]{2,1,0:T(8,128)S(1)}, f32[2,24,128]{2,1,0:T(8,128)S(1)}) custom-call(s32[4,4]{1,0:T(4,128)S(1)} %copy-done.4, s32[4]{0:T(128)S(1)} %copy-done.6, f32[4,24,128]{2,1,0:T(8,128)S(1)} %get-tuple-element.20.field_ref.field1_ref, f32[2,24,128]{2,1,0:T(8,128)S(1)} %collective-permute-done.2.near_ref, ...), custom_call_target="tpu_custom_call" | custom-call | tf_op jit(solution)/shard_map/pallas_call | solution.py:228
  15.1 0.5 collective-permute-start.4
  15.7 0.1 collective-permute-start.5
  15.8 0.4 collective-permute-start.6
  16.2 0.8 %collective-permute-done.6 = f32[8,128]{1,0:T(8,128)S(1)} collective-permute-done((f32[8,128]{1,0:T(8,128)S(1)}, f32[8,128]{1,0:T(8,128)S(1)}, u32[]{:S(2)}, u32[]{:S(2)}) %collective-permute-start.6) | collective-permute-done | bytes 4128 | tf_op jit(solution)/shard_map/ppermute | solution.py:183
  17.1 1.6 %collective-permute-start.7 = (f32[8,128]{1,0:T(8,128)S(1)}, f32[8,128]{1,0:T(8,128)S(1)}, u32[]{:S(2)}, u32[]{:S(2)}) collective-permute-start(f32[8,128]{1,0:T(8,128)S(1)} %max.15), channel_id=1, source_target_pairs={{0,16},{8,24},{16,0},{24,8},{1,17},{9,25},{17,1},{25,9},{2,18},{10... | collective-permute-start | bytes 12296 | tf_op jit(solution)/shard_map/ppermute | solution.py:183
  18.6 2.0 %collective-permute-done.7 = f32[8,128]{1,0:T(8,128)S(1)} collective-permute-done((f32[8,128]{1,0:T(8,128)S(1)}, f32[8,128]{1,0:T(8,128)S(1)}, u32[]{:S(2)}, u32[]{:S(2)}) %collective-permute-start.7) | collective-permute-done | bytes 4128 | tf_op jit(solution)/shard_map/ppermute | solution.py:183
  20.7 1.5 %collective-permute-start.8 = (f32[8,128]{1,0:T(8,128)S(1)}, f32[8,128]{1,0:T(8,128)S(1)}, u32[]{:S(2)}, u32[]{:S(2)}) collective-permute-start(f32[8,128]{1,0:T(8,128)S(1)} %max.16), channel_id=1, source_target_pairs={{0,1},{1,0},{2,3},{3,2},{4,5},{5,4},{6,7},{7,6},{8,9},{9,8},{10,11... | collective-permute-start | bytes 12296 | tf_op jit(solution)/shard_map/ppermute | solution.py:183
  22.2 2.1 %collective-permute-done.8 = f32[8,128]{1,0:T(8,128)S(1)} collective-permute-done((f32[8,128]{1,0:T(8,128)S(1)}, f32[8,128]{1,0:T(8,128)S(1)}, u32[]{:S(2)}, u32[]{:S(2)}) %collective-permute-start.8) | collective-permute-done | bytes 4128 | tf_op jit(solution)/shard_map/ppermute | solution.py:183
  24.3 1.6 %collective-permute-start.9 = (f32[8,128]{1,0:T(8,128)S(1)}, f32[8,128]{1,0:T(8,128)S(1)}, u32[]{:S(2)}, u32[]{:S(2)}) collective-permute-start(f32[8,128]{1,0:T(8,128)S(1)} %max.17), channel_id=1, source_target_pairs={{0,2},{1,3},{2,0},{3,1},{4,6},{5,7},{6,4},{7,5},{8,10},{9,11},{10,... | collective-permute-start | bytes 12296 | tf_op jit(solution)/shard_map/ppermute | solution.py:183
  25.9 2.0 %collective-permute-done.9 = f32[8,128]{1,0:T(8,128)S(1)} collective-permute-done((f32[8,128]{1,0:T(8,128)S(1)}, f32[8,128]{1,0:T(8,128)S(1)}, u32[]{:S(2)}, u32[]{:S(2)}) %collective-permute-start.9) | collective-permute-done | bytes 4128 | tf_op jit(solution)/shard_map/ppermute | solution.py:183
  27.9 2.6 %collective-permute-start.10 = (f32[8,128]{1,0:T(8,128)S(1)}, f32[8,128]{1,0:T(8,128)S(1)}, u32[]{:S(2)}, u32[]{:S(2)}) collective-permute-start(f32[8,128]{1,0:T(8,128)S(1)} %max.18), channel_id=1, source_target_pairs={{0,4},{1,5},{2,6},{3,7},{4,0},{5,1},{6,2},{7,3},{8,12},{9,13},{10,... | collective-permute-start | bytes 12296 | tf_op jit(solution)/shard_map/ppermute | solution.py:183
  30.5 1.9 %collective-permute-done.10 = f32[8,128]{1,0:T(8,128)S(1)} collective-permute-done((f32[8,128]{1,0:T(8,128)S(1)}, f32[8,128]{1,0:T(8,128)S(1)}, u32[]{:S(2)}, u32[]{:S(2)}) %collective-permute-start.10) | collective-permute-done | bytes 4128 | tf_op jit(solution)/shard_map/ppermute | solution.py:183
  32.4 0.0 copy-start.5
  32.4 0.0 collective-permute-done.4.near_ref
  32.4 0.0 collective-permute-done.5.far_ref
  32.4 0.7 %copy-done.5 = s32[4,128]{1,0:T(4,128)S(1)} copy-done((s32[4,128]{1,0:T(4,128)S(1)}, s32[4,128]{1,0:T(4,128)}, u32[]{:S(2)}) %copy-start.5) | copy-done | bytes 2072
  33.1 1.6 %shard_map.99 = (f32[4,24,128]{2,1,0:T(8,128)}, f32[4,24,128]{2,1,0:T(8,128)S(1)}, f32[24,128]{1,0:T(8,128)S(1)}) custom-call(s32[4,4]{1,0:T(4,128)S(1)} %copy-done.4, f32[4,24,128]{2,1,0:T(8,128)S(1)} %get-tuple-element.16.field_ref.field0_ref, f32[4,24,128]{2,1,0:T(8,128)S(1)} %get-tuple-element.20.field_ref.field1_ref, ...), custom_call_target="tpu_custom_call" | custom-call | tf_op jit(solution)/shard_map/pallas_call | solution.py:230
  34.7 0.7 %broadcast_in_dim.8 = f32[2,2,8,3,4,128]{5,4,3,2,1,0:T(4,128)} broadcast(f32[2,3,4,128]{3,2,1,0:T(4,128)S(1)} %bitcast.13), dimensions={1,3,4,5} | broadcast | bytes 208896 | tf_op jit(solution)/shard_map/broadcast_in_dim | solution.py:236
  35.4 0.0 copy-start.8
  35.4 5.9 %all-to-all-start = ((f32[32,3,4,128]{3,2,1,0:T(4,128)}), f32[32,3,4,128]{3,2,1,0:T(4,128)S(1)}, u32[]{:S(2)}, u32[]{:S(2)}) async-start(f32[32,3,4,128]{3,2,1,0:T(4,128)} %bitcast.1), calls=%async_computation | async-start | bytes 393216 | tf_op jit(solution)/shard_map/all_to_all | solution.py:239
  41.3 0.0 copy-done.8
  41.3 1.8 %collective-permute-start.12 = (f32[16,512]{1,0:T(8,128)S(1)}, f32[16,512]{1,0:T(8,128)S(1)}, u32[]{:S(2)}, u32[]{:S(2)}) collective-permute-start(f32[16,512]{1,0:T(8,128)S(1)} %copy-done.8), channel_id=1, source_target_pairs={{0,1},{1,0},{2,3},{3,2},{4,5},{5,4},{6,7},{7,6},{8,9},{9,8},{10,11... | collective-permute-start | bytes 98312 | tf_op jit(solution)/shard_map/ppermute | solution.py:183
  43.2 2.6 %collective-permute-done.12 = f32[16,512]{1,0:T(8,128)S(1)} collective-permute-done((f32[16,512]{1,0:T(8,128)S(1)}, f32[16,512]{1,0:T(8,128)S(1)}, u32[]{:S(2)}, u32[]{:S(2)}) %collective-permute-start.12) | collective-permute-done | bytes 32800 | tf_op jit(solution)/shard_map/ppermute | solution.py:183
  45.8 1.7 %collective-permute-start.13 = (f32[32,512]{1,0:T(8,128)S(1)}, f32[32,512]{1,0:T(8,128)S(1)}, u32[]{:S(2)}, u32[]{:S(2)}) collective-permute-start(f32[32,512]{1,0:T(8,128)S(1)} %pad_maximum_fusion.2), channel_id=1, source_target_pairs={{0,2},{1,3},{2,0},{3,1},{4,6},{5,7},{6,4},{7,5},{8,10},{9,11},{10,... | collective-permute-start | bytes 196616 | tf_op jit(solution)/shard_map/ppermute | solution.py:183
  47.4 2.6 %collective-permute-done.13 = f32[32,512]{1,0:T(8,128)S(1)} collective-permute-done((f32[32,512]{1,0:T(8,128)S(1)}, f32[32,512]{1,0:T(8,128)S(1)}, u32[]{:S(2)}, u32[]{:S(2)}) %collective-permute-start.13) | collective-permute-done | bytes 65568 | tf_op jit(solution)/shard_map/ppermute | solution.py:183
  50.1 2.8 %collective-permute-start.14 = (f32[64,512]{1,0:T(8,128)S(1)}, f32[64,512]{1,0:T(8,128)S(1)}, u32[]{:S(2)}, u32[]{:S(2)}) collective-permute-start(f32[64,512]{1,0:T(8,128)S(1)} %pad_maximum_fusion.1), channel_id=1, source_target_pairs={{0,4},{1,5},{2,6},{3,7},{4,0},{5,1},{6,2},{7,3},{8,12},{9,13},{10,... | collective-permute-start | bytes 393224 | tf_op jit(solution)/shard_map/ppermute | solution.py:183
  52.9 0.0 all-to-all-done
  53.0 0.1 collective-permute-start.11
  53.0 5.6 %collective-permute-done.14 = f32[64,512]{1,0:T(8,128)S(1)} collective-permute-done((f32[64,512]{1,0:T(8,128)S(1)}, f32[64,512]{1,0:T(8,128)S(1)}, u32[]{:S(2)}, u32[]{:S(2)}) %collective-permute-start.14) | collective-permute-done | bytes 131104 | tf_op jit(solution)/shard_map/ppermute | solution.py:183
  58.7 0.0 collective-permute-done.11.other_ref
  58.7 1.1 %shard_map.100 = f32[4,24,128]{2,1,0:T(8,128)} custom-call(f32[12,512]{1,0:T(8,128)S(1)} %bitcast.12, f32[12,512]{1,0:T(8,128)S(1)} %collective-permute-done.11.other_ref, f32[128,512]{1,0:T(8,128)S(1)} %pad_maximum_fusion.inverse_ref, s32[4,128]{1,0:T(4,128)S(1)} %copy-done.5, f32[4,24,128]{2,1,0:T(8,128)S(1)} %get-tuple-element.28.answer_ref), custom_call_target="tpu_custom_call" | custom-call | tf_op jit(solution)/shard_map/pallas_call | solution.py:243
  (12 shorter events, 0.1 us)
Async XLA Ops:
  0.6 0.7 %copy-start.1 = (f32[4,128]{1,0:T(4,128)S(1)}, f32[4,128]{1,0:T(4,128)}, u32[]{:S(2)}) copy-start(f32[4,128]{1,0:T(4,128)} %diagonal_ref.9) | copy-start | bytes 6148
  1.3 0.8 %copy-start.3 = (f32[4,24,128]{2,1,0:T(8,128)S(1)}, f32[4,24,128]{2,1,0:T(8,128)}, u32[]{:S(2)}) copy-start(f32[4,24,128]{2,1,0:T(8,128)} %loads_ref.1) | copy-start | bytes 147460
  2.1 0.7 %copy-start.6 = (s32[4]{0:T(128)S(1)}, s32[4]{0:T(128)}, u32[]{:S(2)}) copy-start(s32[4]{0:T(128)} %send_ref.5) | copy-start | bytes 52
  2.8 3.7 %copy-start.7 = (s32[4,4]{1,0:T(4,128)S(1)}, s32[4,4]{1,0:T(4,128)}, u32[]{:S(2)}) copy-start(s32[4,4]{1,0:T(4,128)} %mask_ref.1) | copy-start | bytes 196
  3.3 3.2 %copy-start.2 = (f32[4,128]{1,0:T(4,128)S(1)}, f32[4,128]{1,0:T(4,128)}, u32[]{:S(2)}) copy-start(f32[4,128]{1,0:T(4,128)} %diagonal_ref.9) | copy-start | bytes 6148
  3.4 5.7 %collective-permute-start = (f32[2,24,128]{2,1,0:T(8,128)S(1)}, f32[2,24,128]{2,1,0:T(8,128)S(1)}, u32[]{:S(2)}, u32[]{:S(2)}) collective-permute-start(f32[2,24,128]{2,1,0:T(8,128)S(1)} %get-tuple-element.17), channel_id=1, source_target_pairs={{0,8},{8,0},{16,24},{24,16},{1,9},{9,1},{17,25},{25,17},{2,10},{10... | collective-permute-start | bytes 73736 | tf_op jit(solution)/shard_map/ppermute | solution.py:183
  3.9 5.2 %collective-permute-start.1 = (f32[2,24,128]{2,1,0:T(8,128)S(1)}, f32[2,24,128]{2,1,0:T(8,128)S(1)}, u32[]{:S(2)}, u32[]{:S(2)}) collective-permute-start(f32[2,24,128]{2,1,0:T(8,128)S(1)} %get-tuple-element.18), channel_id=1, source_target_pairs={{0,24},{8,16},{16,8},{24,0},{1,25},{9,17},{17,9},{25,1},{2,26},{10... | collective-permute-start | bytes 73736 | tf_op jit(solution)/shard_map/ppermute | solution.py:188
  6.5 1.2 %copy-start = (f32[4,4,128,128]{3,2,1,0:T(8,128)S(1)}, f32[4,4,128,128]{3,2,1,0:T(8,128)}, u32[]{:S(2)}) copy-start(f32[4,4,128,128]{3,2,1,0:T(8,128)} %stiffness_ref.1) | copy-start | bytes 3145732
  9.0 0.7 %copy-start.4 = (s32[4,4]{1,0:T(4,128)S(1)}, s32[4,4]{1,0:T(4,128)}, u32[]{:S(2)}) copy-start(s32[4,4]{1,0:T(4,128)} %neighbors_ref.5) | copy-start | bytes 196
  10.7 1.3 %collective-permute-start.2 = (f32[2,24,128]{2,1,0:T(8,128)S(1)}, f32[2,24,128]{2,1,0:T(8,128)S(1)}, u32[]{:S(2)}, u32[]{:S(2)}) collective-permute-start(f32[2,24,128]{2,1,0:T(8,128)S(1)} %get-tuple-element.21), channel_id=1, source_target_pairs={{0,8},{8,0},{16,24},{24,16},{1,9},{9,1},{17,25},{25,17},{2,10},{10... | collective-permute-start | bytes 73736 | tf_op jit(solution)/shard_map/ppermute | solution.py:183
  10.9 3.3 %collective-permute-start.3 = (f32[2,24,128]{2,1,0:T(8,128)S(1)}, f32[2,24,128]{2,1,0:T(8,128)S(1)}, u32[]{:S(2)}, u32[]{:S(2)}) collective-permute-start(f32[2,24,128]{2,1,0:T(8,128)S(1)} %get-tuple-element.22), channel_id=1, source_target_pairs={{0,24},{8,16},{16,8},{24,0},{1,25},{9,17},{17,9},{25,1},{2,26},{10... | collective-permute-start | bytes 73736 | tf_op jit(solution)/shard_map/ppermute | solution.py:188
  15.1 17.3 %collective-permute-start.4 = (f32[2,24,128]{2,1,0:T(8,128)S(1)}, f32[2,24,128]{2,1,0:T(8,128)S(1)}, u32[]{:S(2)}, u32[]{:S(2)}) collective-permute-start(f32[2,24,128]{2,1,0:T(8,128)S(1)} %get-tuple-element.24), channel_id=1, source_target_pairs={{0,8},{8,0},{16,24},{24,16},{1,9},{9,1},{17,25},{25,17},{2,10},{10... | collective-permute-start | bytes 73736 | tf_op jit(solution)/shard_map/ppermute | solution.py:183
  15.7 16.8 %collective-permute-start.5 = (f32[2,24,128]{2,1,0:T(8,128)S(1)}, f32[2,24,128]{2,1,0:T(8,128)S(1)}, u32[]{:S(2)}, u32[]{:S(2)}) collective-permute-start(f32[2,24,128]{2,1,0:T(8,128)S(1)} %get-tuple-element.25), channel_id=1, source_target_pairs={{0,24},{8,16},{16,8},{24,0},{1,25},{9,17},{17,9},{25,1},{2,26},{10... | collective-permute-start | bytes 73736 | tf_op jit(solution)/shard_map/ppermute | solution.py:188
  15.8 1.3 %collective-permute-start.6 = (f32[8,128]{1,0:T(8,128)S(1)}, f32[8,128]{1,0:T(8,128)S(1)}, u32[]{:S(2)}, u32[]{:S(2)}) collective-permute-start(f32[8,128]{1,0:T(8,128)S(1)} %get-tuple-element.26), channel_id=1, source_target_pairs={{0,8},{8,0},{16,24},{24,16},{1,9},{9,1},{17,25},{25,17},{2,10},{10... | collective-permute-start | bytes 12296 | tf_op jit(solution)/shard_map/ppermute | solution.py:183
  17.1 3.6 %collective-permute-start.7 = (f32[8,128]{1,0:T(8,128)S(1)}, f32[8,128]{1,0:T(8,128)S(1)}, u32[]{:S(2)}, u32[]{:S(2)}) collective-permute-start(f32[8,128]{1,0:T(8,128)S(1)} %max.15), channel_id=1, source_target_pairs={{0,16},{8,24},{16,0},{24,8},{1,17},{9,25},{17,1},{25,9},{2,18},{10... | collective-permute-start | bytes 12296 | tf_op jit(solution)/shard_map/ppermute | solution.py:183
  20.7 3.6 %collective-permute-start.8 = (f32[8,128]{1,0:T(8,128)S(1)}, f32[8,128]{1,0:T(8,128)S(1)}, u32[]{:S(2)}, u32[]{:S(2)}) collective-permute-start(f32[8,128]{1,0:T(8,128)S(1)} %max.16), channel_id=1, source_target_pairs={{0,1},{1,0},{2,3},{3,2},{4,5},{5,4},{6,7},{7,6},{8,9},{9,8},{10,11... | collective-permute-start | bytes 12296 | tf_op jit(solution)/shard_map/ppermute | solution.py:183
  24.3 3.6 %collective-permute-start.9 = (f32[8,128]{1,0:T(8,128)S(1)}, f32[8,128]{1,0:T(8,128)S(1)}, u32[]{:S(2)}, u32[]{:S(2)}) collective-permute-start(f32[8,128]{1,0:T(8,128)S(1)} %max.17), channel_id=1, source_target_pairs={{0,2},{1,3},{2,0},{3,1},{4,6},{5,7},{6,4},{7,5},{8,10},{9,11},{10,... | collective-permute-start | bytes 12296 | tf_op jit(solution)/shard_map/ppermute | solution.py:183
  27.9 4.5 %collective-permute-start.10 = (f32[8,128]{1,0:T(8,128)S(1)}, f32[8,128]{1,0:T(8,128)S(1)}, u32[]{:S(2)}, u32[]{:S(2)}) collective-permute-start(f32[8,128]{1,0:T(8,128)S(1)} %max.18), channel_id=1, source_target_pairs={{0,4},{1,5},{2,6},{3,7},{4,0},{5,1},{6,2},{7,3},{8,12},{9,13},{10,... | collective-permute-start | bytes 12296 | tf_op jit(solution)/shard_map/ppermute | solution.py:183
  32.4 0.7 %copy-start.5 = (s32[4,128]{1,0:T(4,128)S(1)}, s32[4,128]{1,0:T(4,128)}, u32[]{:S(2)}) copy-start(s32[4,128]{1,0:T(4,128)} %aggregate_ref.3) | copy-start | bytes 6148
  35.4 5.9 %copy-start.8 = (f32[16,512]{1,0:T(8,128)S(1)}, f32[16,512]{1,0:T(8,128)}, u32[]{:S(2)}) copy-start(f32[16,512]{1,0:T(8,128)} %param.15) | copy-start | bytes 98308
  35.4 17.4 %all-to-all-start = ((f32[32,3,4,128]{3,2,1,0:T(4,128)}), f32[32,3,4,128]{3,2,1,0:T(4,128)S(1)}, u32[]{:S(2)}, u32[]{:S(2)}) async-start(f32[32,3,4,128]{3,2,1,0:T(4,128)} %bitcast.1), calls=%async_computation | async-start | bytes 393216 | tf_op jit(solution)/shard_map/all_to_all | solution.py:239
  41.3 4.4 %collective-permute-start.12 = (f32[16,512]{1,0:T(8,128)S(1)}, f32[16,512]{1,0:T(8,128)S(1)}, u32[]{:S(2)}, u32[]{:S(2)}) collective-permute-start(f32[16,512]{1,0:T(8,128)S(1)} %copy-done.8), channel_id=1, source_target_pairs={{0,1},{1,0},{2,3},{3,2},{4,5},{5,4},{6,7},{7,6},{8,9},{9,8},{10,11... | collective-permute-start | bytes 98312 | tf_op jit(solution)/shard_map/ppermute | solution.py:183
  45.8 4.3 %collective-permute-start.13 = (f32[32,512]{1,0:T(8,128)S(1)}, f32[32,512]{1,0:T(8,128)S(1)}, u32[]{:S(2)}, u32[]{:S(2)}) collective-permute-start(f32[32,512]{1,0:T(8,128)S(1)} %pad_maximum_fusion.2), channel_id=1, source_target_pairs={{0,2},{1,3},{2,0},{3,1},{4,6},{5,7},{6,4},{7,5},{8,10},{9,11},{10,... | collective-permute-start | bytes 196616 | tf_op jit(solution)/shard_map/ppermute | solution.py:183
  50.1 8.6 %collective-permute-start.14 = (f32[64,512]{1,0:T(8,128)S(1)}, f32[64,512]{1,0:T(8,128)S(1)}, u32[]{:S(2)}, u32[]{:S(2)}) collective-permute-start(f32[64,512]{1,0:T(8,128)S(1)} %pad_maximum_fusion.1), channel_id=1, source_target_pairs={{0,4},{1,5},{2,6},{3,7},{4,0},{5,1},{6,2},{7,3},{8,12},{9,13},{10,... | collective-permute-start | bytes 393224 | tf_op jit(solution)/shard_map/ppermute | solution.py:183
  53.0 5.7 %collective-permute-start.11 = (f32[12,512]{1,0:T(8,128)S(1)}, f32[12,512]{1,0:T(8,128)S(1)}, u32[]{:S(2)}, u32[]{:S(2)}) collective-permute-start(f32[12,512]{1,0:T(8,128)S(1)} %bitcast.11), channel_id=1, source_target_pairs={{0,8},{8,0},{16,24},{24,16},{1,9},{9,1},{17,25},{25,17},{2,10},{10... | collective-permute-start | bytes 73736 | tf_op jit(solution)/shard_map/ppermute | solution.py:183

commit v2 on v1

v2 whole, which is shorter than its diff:
```python
import jax
import jax.numpy as jnp
from jax import lax
from jax.experimental import pallas as pl
from jax.experimental.pallas import tpu as pltpu
from jax.sharding import PartitionSpec as P

SWEEPS = 2
AXES = ("wide", "narrow")

VMEM = pl.BlockSpec(memory_space=pltpu.VMEM)
SMEM = pl.BlockSpec(memory_space=pltpu.SMEM)
HBM = pl.BlockSpec(memory_space=pl.ANY)
LIMIT = pltpu.CompilerParams(vmem_limit_bytes=32 * 1024 * 1024)

f32 = jnp.float32
bf16 = jnp.bfloat16
TRANSPOSED = (((1,), (1,)), ((), ()))


def like(*shape, dtype=f32):
    return jax.ShapeDtypeStruct(shape, dtype)


def split(value):
    high = value.astype(bf16).astype(f32)
    return high, value - high


def stacked(value):
    return jnp.concatenate(split(value), axis=0).astype(bf16)


def beside(value):
    return jnp.concatenate(split(value), axis=1).astype(bf16)


def parity():
    return lax.rem(lax.axis_index("wide"), 2)


def write_messages(choice_ref, field_ref, near_ref, far_ref):
    blocks, comps, _ = field_ref.shape
    ghosts = near_ref.shape[0] // comps
    for side, ref in enumerate((near_ref, far_ref)):
        for j in range(ghosts):
            row = (side * ghosts + j) * blocks
            ref[j * comps : (j + 1) * comps] = sum(
                choice_ref[row + b : row + b + 1, :] * field_ref[b] for b in range(blocks)
            )


def start_copies(pairs, sems):
    copies = [pltpu.make_async_copy(source, target, sems.at[k]) for k, (source, target) in enumerate(pairs)]
    for copy in copies:
        copy.start()
    return copies


def start_kernel(
    send_hbm, loads_hbm, diagonal_hbm, stiffness_hbm,
    field_ref, near_ref, far_ref, diagonal_ref, choice_ref, stiffness_ref,
    loads_ref, send_ref, sems,
):
    blocks, _, size = loads_ref.shape
    ghosts = send_ref.shape[0] // 2
    copies = start_copies([
        (send_hbm, send_ref), (diagonal_hbm, diagonal_ref), (loads_hbm, loads_ref), (stiffness_hbm, stiffness_ref)
    ], sems)
    for copy in copies[:3]:
        copy.wait()
    odd = parity()
    for j in range(ghosts):
        for b in range(blocks):
            near = jnp.where(send_ref[(1 - odd) * ghosts + j] == b, 1.0, 0.0)
            far = jnp.where(send_ref[odd * ghosts + j] == b, 1.0, 0.0)
            choice_ref[j * blocks + b : j * blocks + b + 1, :] = jnp.full((1, size), near, f32)
            row = (ghosts + j) * blocks + b
            choice_ref[row : row + 1, :] = jnp.full((1, size), far, f32)
    for b in range(blocks):
        field_ref[b] = loads_ref[b] / diagonal_ref[b : b + 1, :]
    write_messages(choice_ref, field_ref, near_ref, far_ref)
    copies[3].wait()


def prepare_kernel(
    neighbors_hbm, mask_hbm, aggregate_hbm, stiffness_ref, diagonal_ref, parts_ref, places_ref, peak_ref,
    total_ref, aggregate_ref, neighbors_ref, mask_ref, sems,
):
    blocks, slots, size, _ = stiffness_ref.shape
    entries = total_ref.shape[0]
    ghosts = (entries - blocks) // 2
    copies = start_copies([
        (neighbors_hbm, neighbors_ref), (mask_hbm, mask_ref), (aggregate_hbm, aggregate_ref)
    ], sems)
    for copy in copies:
        copy.wait()
    odd = parity()
    peak = jnp.zeros((8, size), f32)
    for b in range(blocks):
        total_ref[...] = jnp.zeros_like(total_ref)
        ratio = jnp.zeros((size, size), f32)
        for s in range(slots):
            entry = neighbors_ref[b, s]
            swapped = jnp.where(entry < blocks + ghosts, entry + ghosts, entry - ghosts)
            entry = jnp.where((entry >= blocks) & (odd == 0), swapped, entry)
            live = stiffness_ref[b, s] * mask_ref[b, s].astype(f32)
            ratio = ratio + jnp.abs(live)
            total_ref[entry] = total_ref[entry] + live.T
        for entry in range(entries):
            parts_ref[b, entry * size : (entry + 1) * size, :] = beside(total_ref[entry])
        rows = lax.dot_general(
            jnp.ones((8, size), f32), ratio, TRANSPOSED,
            precision=lax.Precision.HIGHEST, preferred_element_type=f32,
        )
        peak = jnp.maximum(peak, rows / diagonal_ref[b : b + 1, :])
    peak_ref[...] = jnp.broadcast_to(jnp.max(peak, axis=1, keepdims=True), peak.shape)
    index = lax.broadcasted_iota(jnp.int32, (places_ref.shape[0], size), 0)
    for b in range(blocks):
        hit = index == aggregate_ref[b : b + 1, :]
        places_ref[:, b * size : (b + 1) * size] = hit.astype(f32).astype(bf16)


def couple(field_ref, near_ref, far_ref, parts_ref, diagonal_ref, next_ref):
    blocks, comps, size = field_ref.shape
    ghosts = near_ref.shape[0] // comps
    me = lax.axis_index("wide")
    inside = jnp.where((me == 0) | (me == lax.axis_size("wide") - 1), 0.0, 1.0).astype(f32)
    extended = [stacked(field_ref[b]) for b in range(blocks)]
    extended += [stacked(near_ref[j * comps : (j + 1) * comps]) for j in range(ghosts)]
    extended += [stacked(far_ref[j * comps : (j + 1) * comps] * inside) for j in range(ghosts)]
    extended = jnp.concatenate(extended, axis=1)
    for b in range(blocks):
        product = jnp.dot(extended, parts_ref[b], preferred_element_type=f32)
        coupled = product[:comps, :size] + product[:comps, size:] + product[comps:, :size]
        next_ref[b] = coupled / diagonal_ref[b : b + 1, :]


def step_kernel(field_ref, near_ref, far_ref, parts_ref, diagonal_ref, choice_ref, next_ref, near_out, far_out):
    couple(field_ref, near_ref, far_ref, parts_ref, diagonal_ref, next_ref)
    write_messages(choice_ref, next_ref, near_out, far_out)


def restrict(fields, diagonal_ref, places_ref):
    blocks, comps, size = fields[0].shape
    values = []
    for b in range(blocks):
        scale = diagonal_ref[b : b + 1, :]
        values.append(jnp.concatenate([stacked(field[b] * scale) for field in fields], axis=0))
    product = lax.dot_general(
        jnp.concatenate(values, axis=1), places_ref[...], TRANSPOSED, preferred_element_type=f32
    )
    return [product[2 * k * comps : (2 * k + 1) * comps] + product[(2 * k + 1) * comps : (2 * k + 2) * comps]
            for k in range(len(fields))]


def restrict_kernel(field0_ref, field1_ref, field2_ref, diagonal_ref, places_ref, sums_ref):
    for k, value in enumerate(restrict([field0_ref, field1_ref, field2_ref], diagonal_ref, places_ref)):
        sums_ref[k] = value


def last_step_kernel(field_ref, near_ref, far_ref, parts_ref, diagonal_ref, places_ref, next_ref, sums_ref):
    couple(field_ref, near_ref, far_ref, parts_ref, diagonal_ref, next_ref)
    (sums_ref[...],) = restrict([next_ref], diagonal_ref, places_ref)


def coefficients(upper):
    half_span = 0.375 * upper
    zero = jnp.zeros_like(upper)
    ratio = 5.0 / 3.0
    before = 0.6

    def applied(d):
        return [d[0]] + [d[k] - d[k - 1] for k in range(1, len(d))] + [-d[-1]]

    def less(a, b):
        a = a + [zero] * (len(b) - len(a))
        return [x - y for x, y in zip(a, b)]

    direction = [1.0 / (0.625 * upper)]
    answer = list(direction)
    remainder = [jnp.ones_like(upper)]
    for _ in range(SWEEPS):
        remainder = less(remainder, applied(direction))
        now = 1.0 / (2.0 * ratio - before)
        longer = direction + [zero]
        direction = [now * before * d + (2.0 * now / half_span) * r for d, r in zip(longer, remainder)]
        answer = [a + d for a, d in zip(answer + [zero], direction)]
        before = now
    return less(remainder, applied(direction)), answer


def largest(peaks_ref):
    return 1.0 + jnp.max(peaks_ref[...], axis=0, keepdims=True)


def outgoing_kernel(early_ref, late_ref, peaks_ref, after_ref, outgoing_ref):
    targets, quarter, four, _ = outgoing_ref.shape
    half = quarter * four
    on_residual, _ = coefficients(largest(peaks_ref))
    sums = sum(c * f for c, f in zip(on_residual, [early_ref[0], early_ref[1], early_ref[2], late_ref[...]]))
    narrow = lax.axis_size("narrow")
    for target in range(targets):
        low = (target // narrow) % 2 * half
        for q in range(quarter):
            outgoing_ref[target, q] = sums[low + four * q : low + four * (q + 1)]


def finish_kernel(field0_ref, field1_ref, field2_ref, field3_ref, diagonal_ref, peaks_ref, residual_ref, answer_ref):
    on_residual, on_answer = coefficients(largest(peaks_ref))
    for b in range(field0_ref.shape[0]):
        fields = [field0_ref[b], field1_ref[b], field2_ref[b], field3_ref[b]]
        residual_ref[b] = diagonal_ref[b : b + 1, :] * sum(c * f for c, f in zip(on_residual, fields))
        answer_ref[b] = sum(c * f for c, f in zip(on_answer, fields))


def inverse_kernel(first_ref, second_ref, aggregate_ref, right_ref, places_ref):
    members, span = places_ref.shape
    blocks, size = aggregate_ref.shape
    unknowns = first_ref.shape[1]
    rank, narrow = lax.axis_index("narrow"), lax.axis_size("narrow")
    rows_each = members // narrow
    rows = jnp.concatenate([first_ref[...], second_ref[...]], axis=0)
    for k in range(unknowns // size):
        right_ref[k * size : (k + 1) * size, :] = beside(rows[:, k * size : (k + 1) * size].T)
    index = lax.broadcasted_iota(jnp.int32, (members, size), 0)
    for b in range(blocks):
        aggregate = aggregate_ref[b : b + 1, :]
        offset = (aggregate // rows_each) ^ rank
        row = gathered_position(offset, narrow) * rows_each + aggregate % rows_each
        places_ref[:, b * size : (b + 1) * size] = (index == row).astype(f32).astype(bf16)


def coarse_kernel(own_ref, other_ref, right_ref, places_ref, answer_ref, correction_ref):
    blocks, comps, size = answer_ref.shape
    members = places_ref.shape[0]
    own, other = own_ref[...], other_ref[...]
    first = parity() == 0
    rhs = jnp.where(first, jnp.concatenate([own, other], axis=0), jnp.concatenate([other, own], axis=0))
    product = jnp.dot(stacked(rhs), right_ref[...], preferred_element_type=f32)
    found = stacked(product[:comps, :members] + product[:comps, members:] + product[comps:, :members])
    spread = jnp.dot(found, places_ref[...], preferred_element_type=f32)
    spread = spread[:comps] + spread[comps:]
    for b in range(blocks):
        correction_ref[b] = answer_ref[b] + spread[:, b * size : (b + 1) * size]


def from_hbm(*arrays):
    return [pltpu.with_memory_space_constraint(array, pltpu.HBM) for array in arrays]


def swap(value, axis, bit):
    return lax.ppermute(value, axis, [(i, i ^ bit) for i in range(lax.axis_size(axis))])


def swap_far(value):
    count = lax.axis_size("wide")
    return lax.ppermute(value, "wide", [(i, (i + 1 if i % 2 else i - 1) % count) for i in range(count)])


def gathered_position(offset, narrow):
    count = narrow.bit_length() - 1
    return sum(((offset >> k) & 1) << (count - 1 - k) for k in range(count))


def shards(loads, diagonal, stiffness, neighbors, slot_mask, send_list, aggregate, coarse_inverse):
    blocks, comps, size = loads.shape
    slots = neighbors.shape[1]
    ghosts = send_list.shape[0] // 2
    entries = blocks + 2 * ghosts
    wide, narrow = lax.axis_size("wide"), lax.axis_size("narrow")
    members = coarse_inverse.shape[0] * narrow
    unknowns = coarse_inverse.shape[1]
    field = like(blocks, comps, size)
    message = like(ghosts * comps, size)

    def call(kernel, in_specs, out_shape, scratch=()):
        return pl.pallas_call(
            kernel, in_specs=in_specs, out_specs=jax.tree.map(lambda _: VMEM, out_shape), out_shape=out_shape,
            scratch_shapes=scratch, compiler_params=LIMIT,
        )

    def halo(near, far):
        far = swap_far(far)
        return swap(near, "wide", 1), far

    field0, near, far, scale, choice, live = call(
        start_kernel, [HBM] * 4,
        (field, message, message, like(blocks, size), like(2 * ghosts * blocks, size), like(*stiffness.shape)),
        [
            pltpu.VMEM(loads.shape, f32), pltpu.SMEM(send_list.shape, jnp.int32), pltpu.SemaphoreType.DMA((4,)),
        ],
    )(*from_hbm(send_list, loads, diagonal, stiffness))
    near, far = halo(near, far)
    parts, places, peak = call(
        prepare_kernel, [HBM] * 3 + [VMEM] * 2,
        (
            like(blocks, entries * size, 2 * size, dtype=bf16), like(members, blocks * size, dtype=bf16), like(8, size),
        ),
        [
            pltpu.VMEM((entries, size, size), f32), pltpu.VMEM(aggregate.shape, jnp.int32),
            pltpu.SMEM(neighbors.shape, jnp.int32), pltpu.SMEM(slot_mask.shape, jnp.int32),
            pltpu.SemaphoreType.DMA((3,)),
        ],
    )(*from_hbm(neighbors, slot_mask, aggregate), live, scale)
    step = call(step_kernel, [VMEM] * 6, (field, message, message))
    field1, near, far = step(field0, near, far, parts, scale, choice)
    near, far = halo(near, far)
    peaks = lax.all_to_all(jnp.broadcast_to(peak[:1], (wide * narrow, 1, size)), AXES, 0, 0)
    peaks = peaks.reshape(wide * narrow, size)
    field2, near, far = step(field1, near, far, parts, scale, choice)
    near, far = halo(near, far)
    order = [1 << k for k in reversed(range(narrow.bit_length() - 1))]
    arrived = swap(coarse_inverse, "narrow", order[0])
    early = call(restrict_kernel, [VMEM] * 5, like(3, comps, members))(field0, field1, field2, scale, places)
    field3, late = call(last_step_kernel, [VMEM] * 6, (field, like(comps, members)))(
        field2, near, far, parts, scale, places
    )

    half = comps // 2
    outgoing = call(outgoing_kernel, [VMEM] * 4, like(wide * narrow, half // 4, 4, members))(early, late, peaks, arrived)
    incoming = lax.all_to_all(outgoing, AXES, 0, 0)
    residual, answer = call(finish_kernel, [VMEM] * 6, (field, field))(field0, field1, field2, field3, scale, peaks)
    inverse = jnp.concatenate([coarse_inverse, arrived], axis=0)
    for bit in order[1:-1]:
        inverse = jnp.concatenate([inverse, swap(inverse, "narrow", bit)], axis=0)
    right, reads = call(
        inverse_kernel, [VMEM] * 3,
        (like(unknowns, 2 * members, dtype=bf16), like(members, blocks * size, dtype=bf16)),
    )(inverse, swap(inverse, "narrow", order[-1]), aggregate)
    own = incoming.reshape(wide, narrow, half, members).sum(axis=1)
    own = own.transpose(1, 0, 2).reshape(half, wide * members)
    other = swap(own, "wide", 1)
    correction = call(coarse_kernel, [VMEM] * 5, field)(own, other, right, reads, answer)
    return correction, residual


def solution(mesh):
    return jax.shard_map(
        shards,
        mesh=mesh,
        in_specs=(
            P(AXES, None, None),
            P(AXES, None),
            P(AXES, None, None, None),
            P(AXES, None),
            P(AXES, None),
            P(AXES),
            P(AXES, None),
            P(AXES, None),
        ),
        out_specs=(P(AXES, None, None), P(AXES, None, None)),
        check_vma=False,
    )
```

time: 60.1 us -> 39.3 us (0.65)
  waiting for transfers between devices: 22.4 us -> 11.2 us
  starting transfers between devices: 24.5 us -> 19.1 us
  local copies, waits for them, and re-layouts: 5.45 us -> 0.66 us
  Pallas kernels: 6.53 us -> 7.25 us
    ppermute x12 -> x7, waiting for transfers between devices: 20.2 us -> 7.09 us  [swap(): lax.ppermute(value, axis, [(i, i ^ bit) for i in range(lax.axis_size(axis...]
    ppermute x12 -> x7, starting transfers between devices: 15.3 us -> 6.94 us  [swap(): lax.ppermute(value, axis, [(i, i ^ bit) for i in range(lax.axis_size(axis...]
    unnamed x21 -> x9, local copies, waits for them, and re-layouts: 4.72 us -> 0.04 us
    all_to_all x0 -> x1, starting transfers between devices: none -> 3.82 us  [shards(): lax.all_to_all(jnp.broadcast_to(peak[:1], (wide * narrow, 1, size)), AXES...]
    all_to_all x1, starting transfers between devices: 5.89 us -> 3.45 us  [shards(): incoming = lax.all_to_all(outgoing, AXES, 0, 0)]
    all_to_all x0 -> x1, waiting for transfers between devices: none -> 2.33 us  [shards(): lax.all_to_all(jnp.broadcast_to(peak[:1], (wide * narrow, 1, size)), AXES...]
    ppermute x3, starting transfers between devices: 3.32 us -> 4.9 us  [swap_far(): lax.ppermute(value, 'wide', [(i, (i + 1 if i % 2 else i - 1) % count) for...]
    ppermute x3, waiting for transfers between devices: 2.15 us -> 1.42 us  [swap_far(): lax.ppermute(value, 'wide', [(i, (i + 1 if i % 2 else i - 1) % count) for...]
  transfers between devices with their start and end apart: 16 -> 12, of which waited for: 10 -> 5; matrix products, arithmetic and copies ran while one was open for 0% -> 2% of each run, Pallas kernels for 2% -> 11%
where the time goes in v2:
time: 39.3 us; the launch traced here: 39.1 us
  starting transfers between devices  19.1 us (49%)
  waiting for transfers between devices  11.2 us (28%)
  Pallas kernels  7.25 us (18%)
  between operations  0.81 us (2%)
  local copies, waits for them, and re-layouts  0.66 us (2%)
    ppermute x7, waiting for transfers between devices, swap(): lax.ppermute(value, axis, [(i, i ^ bit) for i in range(lax.axis_size(axis...  7.09 us
    ppermute x7, starting transfers between devices, swap(): lax.ppermute(value, axis, [(i, i ^ bit) for i in range(lax.axis_size(axis...  6.94 us
    ppermute x3, starting transfers between devices, swap_far(): lax.ppermute(value, 'wide', [(i, (i + 1 if i % 2 else i - 1) % count) for...  4.9 us
    all_to_all x1, starting transfers between devices, shards(): lax.all_to_all(jnp.broadcast_to(peak[:1], (wide * narrow, 1, size)), AXES...  3.82 us
    all_to_all x1, starting transfers between devices, shards(): incoming = lax.all_to_all(outgoing, AXES, 0, 0)  3.45 us
    all_to_all x1, waiting for transfers between devices, shards(): lax.all_to_all(jnp.broadcast_to(peak[:1], (wide * narrow, 1, size)), AXES...  2.33 us
    pallas_call x1, Pallas kernels, shards(): call(prepare_kernel, [HBM] * 3 + [VMEM] * 2, (like(blocks, entries * size...  1.69 us
    ppermute x3, waiting for transfers between devices, swap_far(): lax.ppermute(value, 'wide', [(i, (i + 1 if i % 2 else i - 1) % count) for...  1.42 us
  transfers between devices with their start and end apart: 12, of which 5 were waited for; matrix products, arithmetic and copies ran while one was open for 2% of the time, Pallas kernels for 11%

profile of v2, /device:TPU:0, one launch (start us, length us, event | category | flops | bytes accessed | tf_op | source)
XLA Modules:
  0.0 39.1 jit_solution(9849743182031247213)
XLA Ops:
  0.6 1.3 %shard_map.95 = (f32[4,24,128]{2,1,0:T(8,128)S(1)}, f32[48,128]{1,0:T(8,128)S(1)}, f32[48,128]{1,0:T(8,128)S(1)}, f32[4,128]{1,0:T(4,128)S(1)}, f32[16,128]{1,0:T(8,128)S(1)}, /*index=5*/f32[4,4,128,128]{3,2,1,0:T(8,128)S(1)}) custom-call(s32[4]{0:T(128)} %send_hbm.1, f32[4,24,128]{2,1,0:T(8,128)} %loads_hbm.1, f32[4,128]{1,0:T(4,128)} %diagonal_hbm.1, ...), custom_call_target="tpu_custom_call" | custom-call | tf_op jit(solution)/shard_map/pallas_call | solution.py:287
  1.9 0.5 %collective-permute-start = (f32[48,128]{1,0:T(8,128)S(1)}, f32[48,128]{1,0:T(8,128)S(1)}, u32[]{:S(2)}, u32[]{:S(2)}) collective-permute-start(f32[48,128]{1,0:T(8,128)S(1)} %get-tuple-element.24), channel_id=1, source_target_pairs={{0,8},{8,0},{16,24},{24,16},{1,9},{9,1},{17,25},{25,17},{2,10},{10... | collective-permute-start | bytes 73736 | tf_op jit(solution)/shard_map/ppermute | solution.py:253
  2.5 2.6 %collective-permute-start.1 = (f32[48,128]{1,0:T(8,128)S(1)}, f32[48,128]{1,0:T(8,128)S(1)}, u32[]{:S(2)}, u32[]{:S(2)}) collective-permute-start(f32[48,128]{1,0:T(8,128)S(1)} %get-tuple-element.25), channel_id=1, source_target_pairs={{0,24},{8,16},{16,8},{24,0},{1,25},{9,17},{17,9},{25,1},{2,26},{10... | collective-permute-start | bytes 73736 | tf_op jit(solution)/shard_map/ppermute | solution.py:258
  5.1 2.6 %collective-permute-start.6 = (f32[16,512]{1,0:T(8,128)}, f32[16,512]{1,0:T(8,128)S(1)}, u32[]{:S(2)}, u32[]{:S(2)}) collective-permute-start(f32[16,512]{1,0:T(8,128)} %param.15), channel_id=1, source_target_pairs={{0,4},{1,5},{2,6},{3,7},{4,0},{5,1},{6,2},{7,3},{8,12},{9,13},{10,... | collective-permute-start | bytes 98312 | tf_op jit(solution)/shard_map/ppermute | solution.py:253
  7.7 1.7 %shard_map.96 = (bf16[4,1024,256]{2,1,0:T(8,128)(2,1)S(1)}, bf16[128,512]{1,0:T(8,128)(2,1)S(1)}, f32[8,128]{1,0:T(8,128)S(1)}) custom-call(s32[4,4]{1,0:T(4,128)} %neighbors_hbm.1, s32[4,4]{1,0:T(4,128)} %mask_hbm.1, s32[4,128]{1,0:T(4,128)} %aggregate_ref.1, f32[4,4,128,128]{3,2,1,0:T(8,128)S(1)} %get-tuple-element.26.stiffness_ref, ...), custom_call_target="tpu_custom_call" | custom-call | tf_op jit(solution)/shard_map/pallas_call | solution.py:295
  9.4 0.0 collective-permute-done.near_ref
  9.4 0.0 collective-permute-done.1.far_ref
  9.4 0.5 %shard_map.97 = (f32[4,24,128]{2,1,0:T(8,128)S(1)}, f32[48,128]{1,0:T(8,128)S(1)}, f32[48,128]{1,0:T(8,128)S(1)}) custom-call(f32[4,24,128]{2,1,0:T(8,128)S(1)} %get-tuple-element.23.field_ref.field0_ref, f32[48,128]{1,0:T(8,128)S(1)} %collective-permute-done.near_ref, f32[48,128]{1,0:T(8,128)S(1)} %collective-permute-done.1.far_ref, ...), custom_call_target="tpu_custom_call" | custom-call | tf_op jit(solution)/shard_map/pallas_call | solution.py:307
  9.9 0.1 collective-permute-start.2
  10.0 0.6 %collective-permute-start.3 = (f32[48,128]{1,0:T(8,128)S(1)}, f32[48,128]{1,0:T(8,128)S(1)}, u32[]{:S(2)}, u32[]{:S(2)}) collective-permute-start(f32[48,128]{1,0:T(8,128)S(1)} %get-tuple-element.32), channel_id=1, source_target_pairs={{0,24},{8,16},{16,8},{24,0},{1,25},{9,17},{17,9},{25,1},{2,26},{10... | collective-permute-start | bytes 73736 | tf_op jit(solution)/shard_map/ppermute | solution.py:258
  10.6 0.6 %broadcast_in_dim.3 = f32[32,1,128]{2,1,0:T(1,128)} broadcast(f32[128]{0:T(128)S(1)} %slice_bitcast_fusion), dimensions={2} | broadcast | bytes 16896 | tf_op jit(solution)/shard_map/broadcast_in_dim | solution.py:309
  11.2 3.8 %all-to-all-start = ((f32[32,1,128]{2,1,0:T(1,128)}), f32[32,1,128]{2,1,0:T(1,128)S(1)}, u32[]{:S(2)}, u32[]{:S(2)}) async-start(f32[32,1,128]{2,1,0:T(1,128)} %broadcast_in_dim.3), calls=%async_computation | async-start | bytes 32768 | tf_op jit(solution)/shard_map/all_to_all | solution.py:309
  15.1 0.0 collective-permute-done.2.near_ref
  15.1 0.0 collective-permute-done.3.far_ref
  15.1 0.5 %shard_map.98 = (f32[4,24,128]{2,1,0:T(8,128)S(1)}, f32[48,128]{1,0:T(8,128)S(1)}, f32[48,128]{1,0:T(8,128)S(1)}) custom-call(f32[4,24,128]{2,1,0:T(8,128)S(1)} %get-tuple-element.30.field_ref.field1_ref, f32[48,128]{1,0:T(8,128)S(1)} %collective-permute-done.2.near_ref, f32[48,128]{1,0:T(8,128)S(1)} %collective-permute-done.3.far_ref, ...), custom_call_target="tpu_custom_call" | custom-call | tf_op jit(solution)/shard_map/pallas_call | solution.py:311
  15.6 0.0 copy-start.1
  15.6 0.3 collective-permute-start.4
  15.9 1.6 %collective-permute-start.5 = (f32[48,128]{1,0:T(8,128)S(1)}, f32[48,128]{1,0:T(8,128)S(1)}, u32[]{:S(2)}, u32[]{:S(2)}) collective-permute-start(f32[48,128]{1,0:T(8,128)S(1)} %get-tuple-element.36), channel_id=1, source_target_pairs={{0,24},{8,16},{16,8},{24,0},{1,25},{9,17},{17,9},{25,1},{2,26},{10... | collective-permute-start | bytes 73736 | tf_op jit(solution)/shard_map/ppermute | solution.py:258
  17.5 0.0 copy-start
  17.5 0.2 shard_map.99.early_ref
  17.7 0.0 collective-permute-done.4.near_ref
  17.7 1.4 %collective-permute-done.5.far_ref = f32[48,128]{1,0:T(8,128)S(1)} collective-permute-done((f32[48,128]{1,0:T(8,128)S(1)}, f32[48,128]{1,0:T(8,128)S(1)}, u32[]{:S(2)}, u32[]{:S(2)}) %collective-permute-start.5) | collective-permute-done | bytes 24608 | tf_op jit(solution)/shard_map/ppermute | solution.py:258
  19.2 0.6 %shard_map.100 = (f32[4,24,128]{2,1,0:T(8,128)S(1)}, f32[24,128]{1,0:T(8,128)S(1)}) custom-call(f32[4,24,128]{2,1,0:T(8,128)S(1)} %get-tuple-element.33.field2_ref.field_ref, f32[48,128]{1,0:T(8,128)S(1)} %collective-permute-done.4.near_ref, f32[48,128]{1,0:T(8,128)S(1)} %collective-permute-done.5.far_ref, ...), custom_call_target="tpu_custom_call" | custom-call | tf_op jit(solution)/shard_map/pallas_call | solution.py:316
  19.8 2.3 %all-to-all-done = f32[32,1,128]{2,1,0:T(1,128)S(1)} async-done(((f32[32,1,128]{2,1,0:T(1,128)}), f32[32,1,128]{2,1,0:T(1,128)S(1)}, u32[]{:S(2)}, u32[]{:S(2)}) %all-to-all-start) | async-done | bytes 16416 | tf_op jit(solution)/shard_map/all_to_all | solution.py:309
  22.1 0.0 collective-permute-done.6.after_ref
  22.1 0.7 %shard_map.101 = f32[32,3,4,128]{3,2,1,0:T(4,128)} custom-call(f32[3,24,128]{2,1,0:T(8,128)S(1)} %shard_map.99.early_ref, f32[24,128]{1,0:T(8,128)S(1)} %get-tuple-element.37.late_ref, f32[32,128]{1,0:T(8,128)S(1)} %bitcast.12, f32[16,512]{1,0:T(8,128)S(1)} %collective-permute-done.6.after_ref), custom_call_target="tpu_custom_call" | custom-call | tf_op jit(solution)/shard_map/pallas_call | solution.py:321
  22.8 3.4 %all-to-all-start.1 = ((f32[32,3,4,128]{3,2,1,0:T(4,128)}), f32[32,3,4,128]{3,2,1,0:T(4,128)S(1)}, u32[]{:S(2)}, u32[]{:S(2)}) async-start(f32[32,3,4,128]{3,2,1,0:T(4,128)} %shard_map.101), calls=%async_computation.1 | async-start | bytes 393216 | tf_op jit(solution)/shard_map/all_to_all | solution.py:322
  26.3 0.0 copy-done.1
  26.3 1.8 %collective-permute-start.8 = (f32[32,512]{1,0:T(8,128)S(1)}, f32[32,512]{1,0:T(8,128)S(1)}, u32[]{:S(2)}, u32[]{:S(2)}) collective-permute-start(f32[32,512]{1,0:T(8,128)S(1)} %pad_maximum_fusion), channel_id=1, source_target_pairs={{0,2},{1,3},{2,0},{3,1},{4,6},{5,7},{6,4},{7,5},{8,10},{9,11},{10,... | collective-permute-start | bytes 196616 | tf_op jit(solution)/shard_map/ppermute | solution.py:253
  28.2 4.8 %collective-permute-done.8 = f32[32,512]{1,0:T(8,128)S(1)} collective-permute-done((f32[32,512]{1,0:T(8,128)S(1)}, f32[32,512]{1,0:T(8,128)S(1)}, u32[]{:S(2)}, u32[]{:S(2)}) %collective-permute-start.8) | collective-permute-done | bytes 65568 | tf_op jit(solution)/shard_map/ppermute | solution.py:253
  33.0 1.4 %collective-permute-start.9 = (f32[64,512]{1,0:T(8,128)S(1)}, f32[64,512]{1,0:T(8,128)S(1)}, u32[]{:S(2)}, u32[]{:S(2)}) collective-permute-start(f32[64,512]{1,0:T(8,128)S(1)} %constant_dynamic-update-slice_fusion.first_ref), channel_id=1, source_target_pairs={{0,1},{1,0},{2,3},{3,2},{4,5},{5,4},{6,7},{7,6},{8,9},{9,8},{10,11... | collective-permute-start | bytes 393224 | tf_op jit(solution)/shard_map/ppermute | solution.py:253
  34.4 0.4 all-to-all-done.1
  34.9 0.2 collective-permute-start.7
  35.1 0.7 %shard_map.103 = (f32[4,24,128]{2,1,0:T(8,128)}, f32[4,24,128]{2,1,0:T(8,128)S(1)}) custom-call(f32[4,24,128]{2,1,0:T(8,128)S(1)} %get-tuple-element.23.field_ref.field0_ref, f32[4,24,128]{2,1,0:T(8,128)S(1)} %get-tuple-element.30.field_ref.field1_ref, f32[4,24,128]{2,1,0:T(8,128)S(1)} %get-tuple-element.33.field2_ref.field_ref, ...), custom_call_target="tpu_custom_call" | custom-call | tf_op jit(solution)/shard_map/pallas_call | solution.py:323
  35.7 2.2 %collective-permute-done.9.second_ref = f32[64,512]{1,0:T(8,128)S(1)} collective-permute-done((f32[64,512]{1,0:T(8,128)S(1)}, f32[64,512]{1,0:T(8,128)S(1)}, u32[]{:S(2)}, u32[]{:S(2)}) %collective-permute-start.9) | collective-permute-done | bytes 131104 | tf_op jit(solution)/shard_map/ppermute | solution.py:253
  38.0 0.0 copy-done
  38.0 0.1 shard_map.102
  38.1 0.0 collective-permute-done.7.other_ref
  38.1 1.0 %shard_map.104 = f32[4,24,128]{2,1,0:T(8,128)} custom-call(f32[12,512]{1,0:T(8,128)S(1)} %bitcast.15, f32[12,512]{1,0:T(8,128)S(1)} %collective-permute-done.7.other_ref, bf16[512,256]{1,0:T(8,128)(2,1)S(1)} %get-tuple-element.39.right_ref, bf16[128,512]{1,0:T(8,128)(2,1)S(1)} %get-tuple-element.40.places_ref, f32[4,24,128]{2,1,0:T(8,128)S(1)} %get-tuple-element.42.answer_ref), custom_call_target="tpu_custom_call" | custom-call | tf_op jit(solution)/shard_map/pallas_call | solution.py:334
  (9 shorter events, 0.1 us)
Async XLA Ops:
  1.9 7.5 %collective-permute-start = (f32[48,128]{1,0:T(8,128)S(1)}, f32[48,128]{1,0:T(8,128)S(1)}, u32[]{:S(2)}, u32[]{:S(2)}) collective-permute-start(f32[48,128]{1,0:T(8,128)S(1)} %get-tuple-element.24), channel_id=1, source_target_pairs={{0,8},{8,0},{16,24},{24,16},{1,9},{9,1},{17,25},{25,17},{2,10},{10... | collective-permute-start | bytes 73736 | tf_op jit(solution)/shard_map/ppermute | solution.py:253
  2.5 6.9 %collective-permute-start.1 = (f32[48,128]{1,0:T(8,128)S(1)}, f32[48,128]{1,0:T(8,128)S(1)}, u32[]{:S(2)}, u32[]{:S(2)}) collective-permute-start(f32[48,128]{1,0:T(8,128)S(1)} %get-tuple-element.25), channel_id=1, source_target_pairs={{0,24},{8,16},{16,8},{24,0},{1,25},{9,17},{17,9},{25,1},{2,26},{10... | collective-permute-start | bytes 73736 | tf_op jit(solution)/shard_map/ppermute | solution.py:258
  5.1 17.0 %collective-permute-start.6 = (f32[16,512]{1,0:T(8,128)}, f32[16,512]{1,0:T(8,128)S(1)}, u32[]{:S(2)}, u32[]{:S(2)}) collective-permute-start(f32[16,512]{1,0:T(8,128)} %param.15), channel_id=1, source_target_pairs={{0,4},{1,5},{2,6},{3,7},{4,0},{5,1},{6,2},{7,3},{8,12},{9,13},{10,... | collective-permute-start | bytes 98312 | tf_op jit(solution)/shard_map/ppermute | solution.py:253
  9.9 5.2 %collective-permute-start.2 = (f32[48,128]{1,0:T(8,128)S(1)}, f32[48,128]{1,0:T(8,128)S(1)}, u32[]{:S(2)}, u32[]{:S(2)}) collective-permute-start(f32[48,128]{1,0:T(8,128)S(1)} %get-tuple-element.31), channel_id=1, source_target_pairs={{0,8},{8,0},{16,24},{24,16},{1,9},{9,1},{17,25},{25,17},{2,10},{10... | collective-permute-start | bytes 73736 | tf_op jit(solution)/shard_map/ppermute | solution.py:253
  10.0 5.1 %collective-permute-start.3 = (f32[48,128]{1,0:T(8,128)S(1)}, f32[48,128]{1,0:T(8,128)S(1)}, u32[]{:S(2)}, u32[]{:S(2)}) collective-permute-start(f32[48,128]{1,0:T(8,128)S(1)} %get-tuple-element.32), channel_id=1, source_target_pairs={{0,24},{8,16},{16,8},{24,0},{1,25},{9,17},{17,9},{25,1},{2,26},{10... | collective-permute-start | bytes 73736 | tf_op jit(solution)/shard_map/ppermute | solution.py:258
  11.2 10.9 %all-to-all-start = ((f32[32,1,128]{2,1,0:T(1,128)}), f32[32,1,128]{2,1,0:T(1,128)S(1)}, u32[]{:S(2)}, u32[]{:S(2)}) async-start(f32[32,1,128]{2,1,0:T(1,128)} %broadcast_in_dim.3), calls=%async_computation | async-start | bytes 32768 | tf_op jit(solution)/shard_map/all_to_all | solution.py:309
  15.6 10.7 %copy-start.1 = (f32[16,512]{1,0:T(8,128)S(1)}, f32[16,512]{1,0:T(8,128)}, u32[]{:S(2)}) copy-start(f32[16,512]{1,0:T(8,128)} %param.15) | copy-start | bytes 98308
  15.6 2.2 %collective-permute-start.4 = (f32[48,128]{1,0:T(8,128)S(1)}, f32[48,128]{1,0:T(8,128)S(1)}, u32[]{:S(2)}, u32[]{:S(2)}) collective-permute-start(f32[48,128]{1,0:T(8,128)S(1)} %get-tuple-element.35), channel_id=1, source_target_pairs={{0,8},{8,0},{16,24},{24,16},{1,9},{9,1},{17,25},{25,17},{2,10},{10... | collective-permute-start | bytes 73736 | tf_op jit(solution)/shard_map/ppermute | solution.py:253
  15.9 3.3 %collective-permute-start.5 = (f32[48,128]{1,0:T(8,128)S(1)}, f32[48,128]{1,0:T(8,128)S(1)}, u32[]{:S(2)}, u32[]{:S(2)}) collective-permute-start(f32[48,128]{1,0:T(8,128)S(1)} %get-tuple-element.36), channel_id=1, source_target_pairs={{0,24},{8,16},{16,8},{24,0},{1,25},{9,17},{17,9},{25,1},{2,26},{10... | collective-permute-start | bytes 73736 | tf_op jit(solution)/shard_map/ppermute | solution.py:258
  17.5 20.4 %copy-start = (s32[4,128]{1,0:T(4,128)S(1)}, s32[4,128]{1,0:T(4,128)}, u32[]{:S(2)}) copy-start(s32[4,128]{1,0:T(4,128)} %aggregate_ref.1) | copy-start | bytes 6148
  22.8 12.0 %all-to-all-start.1 = ((f32[32,3,4,128]{3,2,1,0:T(4,128)}), f32[32,3,4,128]{3,2,1,0:T(4,128)S(1)}, u32[]{:S(2)}, u32[]{:S(2)}) async-start(f32[32,3,4,128]{3,2,1,0:T(4,128)} %shard_map.101), calls=%async_computation.1 | async-start | bytes 393216 | tf_op jit(solution)/shard_map/all_to_all | solution.py:322
  26.3 6.7 %collective-permute-start.8 = (f32[32,512]{1,0:T(8,128)S(1)}, f32[32,512]{1,0:T(8,128)S(1)}, u32[]{:S(2)}, u32[]{:S(2)}) collective-permute-start(f32[32,512]{1,0:T(8,128)S(1)} %pad_maximum_fusion), channel_id=1, source_target_pairs={{0,2},{1,3},{2,0},{3,1},{4,6},{5,7},{6,4},{7,5},{8,10},{9,11},{10,... | collective-permute-start | bytes 196616 | tf_op jit(solution)/shard_map/ppermute | solution.py:253
  33.0 5.0 %collective-permute-start.9 = (f32[64,512]{1,0:T(8,128)S(1)}, f32[64,512]{1,0:T(8,128)S(1)}, u32[]{:S(2)}, u32[]{:S(2)}) collective-permute-start(f32[64,512]{1,0:T(8,128)S(1)} %constant_dynamic-update-slice_fusion.first_ref), channel_id=1, source_target_pairs={{0,1},{1,0},{2,3},{3,2},{4,5},{5,4},{6,7},{7,6},{8,9},{9,8},{10,11... | collective-permute-start | bytes 393224 | tf_op jit(solution)/shard_map/ppermute | solution.py:253
  34.9 3.2 %collective-permute-start.7 = (f32[12,512]{1,0:T(8,128)S(1)}, f32[12,512]{1,0:T(8,128)S(1)}, u32[]{:S(2)}, u32[]{:S(2)}) collective-permute-start(f32[12,512]{1,0:T(8,128)S(1)} %bitcast.14), channel_id=1, source_target_pairs={{0,8},{8,0},{16,24},{24,16},{1,9},{9,1},{17,25},{25,17},{2,10},{10... | collective-permute-start | bytes 73736 | tf_op jit(solution)/shard_map/ppermute | solution.py:253

commit v3 on v2

--- a/solution.py
+++ b/solution.py
@@ -41,13 +41,15 @@
 
 def write_messages(choice_ref, field_ref, near_ref, far_ref):
     blocks, comps, _ = field_ref.shape
-    ghosts = near_ref.shape[0] // comps
+    ghosts = choice_ref.shape[0] // (2 * blocks)
     for side, ref in enumerate((near_ref, far_ref)):
         for j in range(ghosts):
             row = (side * ghosts + j) * blocks
             ref[j * comps : (j + 1) * comps] = sum(
                 choice_ref[row + b : row + b + 1, :] * field_ref[b] for b in range(blocks)
             )
+        if ref.shape[0] > ghosts * comps:
+            ref[ghosts * comps :] = jnp.zeros((ref.shape[0] - ghosts * comps, ref.shape[1]), f32)
 
 
 def start_copies(pairs, sems):
@@ -58,14 +60,15 @@
 
 
 def start_kernel(
-    send_hbm, loads_hbm, diagonal_hbm, stiffness_hbm,
-    field_ref, near_ref, far_ref, diagonal_ref, choice_ref, stiffness_ref,
+    send_hbm, loads_hbm, diagonal_hbm, stiffness_hbm, inverse_hbm,
+    field_ref, near_ref, far_ref, diagonal_ref, choice_ref, stiffness_ref, inverse_ref,
     loads_ref, send_ref, sems,
 ):
     blocks, _, size = loads_ref.shape
     ghosts = send_ref.shape[0] // 2
     copies = start_copies([
-        (send_hbm, send_ref), (diagonal_hbm, diagonal_ref), (loads_hbm, loads_ref), (stiffness_hbm, stiffness_ref)
+        (send_hbm, send_ref), (diagonal_hbm, diagonal_ref), (loads_hbm, loads_ref), (stiffness_hbm, stiffness_ref),
+        (inverse_hbm, inverse_ref),
     ], sems)
     for copy in copies[:3]:
         copy.wait()
@@ -80,11 +83,12 @@
     for b in range(blocks):
         field_ref[b] = loads_ref[b] / diagonal_ref[b : b + 1, :]
     write_messages(choice_ref, field_ref, near_ref, far_ref)
-    copies[3].wait()
+    for copy in copies[3:]:
+        copy.wait()
 
 
 def prepare_kernel(
-    neighbors_hbm, mask_hbm, aggregate_hbm, stiffness_ref, diagonal_ref, parts_ref, places_ref, peak_ref,
+    neighbors_hbm, mask_hbm, aggregate_hbm, stiffness_ref, diagonal_ref, parts_ref, places_ref, peaks_ref,
     total_ref, aggregate_ref, neighbors_ref, mask_ref, sems,
 ):
     blocks, slots, size, _ = stiffness_ref.shape
@@ -114,7 +118,8 @@
             precision=lax.Precision.HIGHEST, preferred_element_type=f32,
         )
         peak = jnp.maximum(peak, rows / diagonal_ref[b : b + 1, :])
-    peak_ref[...] = jnp.broadcast_to(jnp.max(peak, axis=1, keepdims=True), peak.shape)
+    peak = jnp.max(peak[:1], axis=1, keepdims=True).reshape(1, 1, 1)
+    peaks_ref[...] = jnp.broadcast_to(peak, peaks_ref.shape)
     index = lax.broadcasted_iota(jnp.int32, (places_ref.shape[0], size), 0)
     for b in range(blocks):
         hit = index == aggregate_ref[b : b + 1, :]
@@ -123,7 +128,7 @@
 
 def couple(field_ref, near_ref, far_ref, parts_ref, diagonal_ref, next_ref):
     blocks, comps, size = field_ref.shape
-    ghosts = near_ref.shape[0] // comps
+    ghosts = (parts_ref.shape[1] // size - blocks) // 2
     me = lax.axis_index("wide")
     inside = jnp.where((me == 0) | (me == lax.axis_size("wide") - 1), 0.0, 1.0).astype(f32)
     extended = [stacked(field_ref[b]) for b in range(blocks)]
@@ -139,6 +144,12 @@
 def step_kernel(field_ref, near_ref, far_ref, parts_ref, diagonal_ref, choice_ref, next_ref, near_out, far_out):
     couple(field_ref, near_ref, far_ref, parts_ref, diagonal_ref, next_ref)
     write_messages(choice_ref, next_ref, near_out, far_out)
+
+
+def passing_step_kernel(*refs):
+    *inputs, later_ref, next_ref, near_out, far_out, later_out = refs
+    later_out[...] = later_ref[...]
+    step_kernel(*inputs, next_ref, near_out, far_out)
 
 
 def restrict(fields, diagonal_ref, places_ref):
@@ -214,13 +225,14 @@
         answer_ref[b] = sum(c * f for c, f in zip(on_answer, fields))
 
 
-def inverse_kernel(first_ref, second_ref, aggregate_ref, right_ref, places_ref):
-    members, span = places_ref.shape
+def inverse_kernel(aggregate_ref, *refs):
+    *gathered, right_ref, places_ref = refs
+    members = places_ref.shape[0]
     blocks, size = aggregate_ref.shape
-    unknowns = first_ref.shape[1]
+    unknowns = right_ref.shape[0]
     rank, narrow = lax.axis_index("narrow"), lax.axis_size("narrow")
     rows_each = members // narrow
-    rows = jnp.concatenate([first_ref[...], second_ref[...]], axis=0)
+    rows = jnp.concatenate([ref[...] for ref in gathered], axis=0)
     for k in range(unknowns // size):
         right_ref[k * size : (k + 1) * size, :] = beside(rows[:, k * size : (k + 1) * size].T)
     index = lax.broadcasted_iota(jnp.int32, (members, size), 0)
@@ -259,8 +271,8 @@
 
 
 def gathered_position(offset, narrow):
-    count = narrow.bit_length() - 1
-    return sum(((offset >> k) & 1) << (count - 1 - k) for k in range(count))
+    half = narrow // 2
+    return (offset % half) * 2 + offset // half
 
 
 def shards(loads, diagonal, stiffness, neighbors, slot_mask, send_list, aggregate, coarse_inverse):
@@ -284,18 +296,22 @@
         far = swap_far(far)
         return swap(near, "wide", 1), far
 
-    field0, near, far, scale, choice, live = call(
-        start_kernel, [HBM] * 4,
-        (field, message, message, like(blocks, size), like(2 * ghosts * blocks, size), like(*stiffness.shape)),
+    field0, near, far, scale, choice, live, inverse = call(
+        start_kernel, [HBM] * 5,
+        (
+            field, message, message, like(blocks, size), like(2 * ghosts * blocks, size), like(*stiffness.shape),
+            like(*coarse_inverse.shape),
+        ),
         [
-            pltpu.VMEM(loads.shape, f32), pltpu.SMEM(send_list.shape, jnp.int32), pltpu.SemaphoreType.DMA((4,)),
+            pltpu.VMEM(loads.shape, f32), pltpu.SMEM(send_list.shape, jnp.int32), pltpu.SemaphoreType.DMA((5,)),
         ],
-    )(*from_hbm(send_list, loads, diagonal, stiffness))
+    )(*from_hbm(send_list, loads, diagonal, stiffness, coarse_inverse))
     near, far = halo(near, far)
-    parts, places, peak = call(
+    parts, places, peaks = call(
         prepare_kernel, [HBM] * 3 + [VMEM] * 2,
         (
-            like(blocks, entries * size, 2 * size, dtype=bf16), like(members, blocks * size, dtype=bf16), like(8, size),
+            like(blocks, entries * size, 2 * size, dtype=bf16), like(members, blocks * size, dtype=bf16),
+            like(wide * narrow, 2, size),
         ),
         [
             pltpu.VMEM((entries, size, size), f32), pltpu.VMEM(aggregate.shape, jnp.int32),
@@ -306,13 +322,15 @@
     step = call(step_kernel, [VMEM] * 6, (field, message, message))
     field1, near, far = step(field0, near, far, parts, scale, choice)
     near, far = halo(near, far)
-    peaks = lax.all_to_all(jnp.broadcast_to(peak[:1], (wide * narrow, 1, size)), AXES, 0, 0)
-    peaks = peaks.reshape(wide * narrow, size)
-    field2, near, far = step(field1, near, far, parts, scale, choice)
+    peaks = lax.all_to_all(peaks, AXES, 0, 0)
+    peaks = peaks[:, 0]
+    longer = like(2 * ghosts * comps, size)
+    field2, near, far, inverse = call(passing_step_kernel, [VMEM] * 7, (field, longer, longer, like(*coarse_inverse.shape)))(
+        field1, near, far, parts, scale, choice, inverse
+    )
     near, far = halo(near, far)
-    order = [1 << k for k in reversed(range(narrow.bit_length() - 1))]
-    arrived = swap(coarse_inverse, "narrow", order[0])
     early = call(restrict_kernel, [VMEM] * 5, like(3, comps, members))(field0, field1, field2, scale, places)
+    arrived = swap(inverse, "narrow", narrow // 2)
     field3, late = call(last_step_kernel, [VMEM] * 6, (field, like(comps, members)))(
         field2, near, far, parts, scale, places
     )
@@ -321,13 +339,12 @@
     outgoing = call(outgoing_kernel, [VMEM] * 4, like(wide * narrow, half // 4, 4, members))(early, late, peaks, arrived)
     incoming = lax.all_to_all(outgoing, AXES, 0, 0)
     residual, answer = call(finish_kernel, [VMEM] * 6, (field, field))(field0, field1, field2, field3, scale, peaks)
-    inverse = jnp.concatenate([coarse_inverse, arrived], axis=0)
-    for bit in order[1:-1]:
-        inverse = jnp.concatenate([inverse, swap(inverse, "narrow", bit)], axis=0)
+    inverse = jnp.concatenate([inverse, arrived], axis=0)
+    gathered = [inverse] + [swap(inverse, "narrow", offset) for offset in range(1, narrow // 2)]
     right, reads = call(
-        inverse_kernel, [VMEM] * 3,
+        inverse_kernel, [VMEM] * (1 + len(gathered)),
         (like(unknowns, 2 * members, dtype=bf16), like(members, blocks * size, dtype=bf16)),
-    )(inverse, swap(inverse, "narrow", order[-1]), aggregate)
+    )(aggregate, *gathered)
     own = incoming.reshape(wide, narrow, half, members).sum(axis=1)
     own = own.transpose(1, 0, 2).reshape(half, wide * members)
     other = swap(own, "wide", 1)

time: 39.3 us -> 38.6 us (0.982)
  waiting for transfers between devices: 11.2 us -> 7.47 us
  starting transfers between devices: 19.1 us -> 22 us
  Pallas kernels: 7.25 us -> 7.89 us
  local copies, waits for them, and re-layouts: 0.66 us -> 0.05 us
    ppermute x7 -> x8, waiting for transfers between devices: 7.09 us -> 0.29 us  [swap(): lax.ppermute(value, axis, [(i, i ^ bit) for i in range(lax.axis_size(axis...]
    all_to_all x1, waiting for transfers between devices: 0.38 us -> 4.96 us  [shards(): incoming = lax.all_to_all(outgoing, AXES, 0, 0)]
    all_to_all x1, starting transfers between devices: 3.82 us -> 5.5 us  [shards(): peaks = lax.all_to_all(peaks, AXES, 0, 0)]
    ppermute x3, waiting for transfers between devices: 1.42 us -> 0.01 us  [swap_far(): lax.ppermute(value, 'wide', [(i, (i + 1 if i % 2 else i - 1) % count) for...]
    all_to_all x1, starting transfers between devices: 3.45 us -> 4.25 us  [shards(): incoming = lax.all_to_all(outgoing, AXES, 0, 0)]
    pallas_call x1, Pallas kernels: 1.69 us -> 2.32 us  [shards(): call(prepare_kernel, [HBM] * 3 + [VMEM] * 2, (like(blocks, entries * size...]
    broadcast_in_dim x1 -> x0, local copies, waits for them, and re-layouts: 0.62 us -> none  [shards(): jnp.broadcast_to(peak[:1], (wide * narrow, 1, size))]
    ppermute x7 -> x8, starting transfers between devices: 6.94 us -> 7.08 us  [swap(): lax.ppermute(value, axis, [(i, i ^ bit) for i in range(lax.axis_size(axis...]
  transfers between devices with their start and end apart: 12 -> 13, of which waited for: 5 -> 3; matrix products, arithmetic and copies ran while one was open for 2% -> 0% of each run, Pallas kernels for 11% -> 12%
where the time goes in v3:
time: 38.6 us; the launch traced here: 38.3 us
  starting transfers between devices  22 us (57%)
  Pallas kernels  7.89 us (20%)
  waiting for transfers between devices  7.47 us (19%)
  between operations  0.81 us (2%)
    ppermute x8, starting transfers between devices, swap(): lax.ppermute(value, axis, [(i, i ^ bit) for i in range(lax.axis_size(axis...  7.08 us
    all_to_all x1, starting transfers between devices, shards(): peaks = lax.all_to_all(peaks, AXES, 0, 0)  5.5 us
    ppermute x3, starting transfers between devices, swap_far(): lax.ppermute(value, 'wide', [(i, (i + 1 if i % 2 else i - 1) % count) for...  5.19 us
    all_to_all x1, waiting for transfers between devices, shards(): incoming = lax.all_to_all(outgoing, AXES, 0, 0)  4.96 us
    all_to_all x1, starting transfers between devices, shards(): incoming = lax.all_to_all(outgoing, AXES, 0, 0)  4.25 us
    pallas_call x1, Pallas kernels, shards(): call(prepare_kernel, [HBM] * 3 + [VMEM] * 2, (like(blocks, entries * size...  2.32 us
    all_to_all x1, waiting for transfers between devices, shards(): peaks = lax.all_to_all(peaks, AXES, 0, 0)  2.21 us
    pallas_call x1, Pallas kernels, shards(): call(start_kernel, [HBM] * 5, (field, message, message, like(blocks, size...  1.32 us
  transfers between devices with their start and end apart: 13, of which 3 were waited for; matrix products, arithmetic and copies ran while one was open for 0% of the time, Pallas kernels for 12%

profile of v3, /device:TPU:0, one launch (start us, length us, event | category | flops | bytes accessed | tf_op | source)
XLA Modules:
  0.0 38.3 jit_solution(17925453290818433209)
XLA Ops:
  0.6 1.3 %shard_map.95 = (f32[4,24,128]{2,1,0:T(8,128)S(1)}, f32[48,128]{1,0:T(8,128)S(1)}, f32[48,128]{1,0:T(8,128)S(1)}, f32[4,128]{1,0:T(4,128)S(1)}, f32[16,128]{1,0:...) custom-call(s32[4]{0:T(128)} %send_hbm.1, f32[4,24,128]{2,1,0:T(8,128)} %loads_hbm.1, ...), custom_call_target="tpu_custom_call" | custom-call | tf_op jit(solution)/shard_map/pallas_call | solution.py:299
  2.0 0.5 %collective-permute-start = (f32[48,128]{1,0:T(8,128)S(1)}, f32[48,128]{1,0:T(8,128)S(1)}, u32[]{:S(2)}, u32[]{:S(2)}) collective-permute-start(f32[48,128]{1,0:T(8,128)S(1)} %get-tuple-element.26), channel_id=1, source_target_pairs={{0,8},{8,0},{16,24},{24,16},{1,9},{9,1},{17,25},{25,17},{2,10},{10... | collective-permute-start | bytes 73736 | tf_op jit(solution)/shard_map/ppermute | solution.py:265
  2.5 2.6 %collective-permute-start.1 = (f32[48,128]{1,0:T(8,128)S(1)}, f32[48,128]{1,0:T(8,128)S(1)}, u32[]{:S(2)}, u32[]{:S(2)}) collective-permute-start(f32[48,128]{1,0:T(8,128)S(1)} %get-tuple-element.27), channel_id=1, source_target_pairs={{0,24},{8,16},{16,8},{24,0},{1,25},{9,17},{17,9},{25,1},{2,26},{10... | collective-permute-start | bytes 73736 | tf_op jit(solution)/shard_map/ppermute | solution.py:270
  5.1 2.3 %shard_map.96 = (bf16[4,1024,256]{2,1,0:T(8,128)(2,1)S(1)}, bf16[128,512]{1,0:T(8,128)(2,1)S(1)}, f32[32,2,128]{2,1,0:T(2,128)}) custom-call(s32[4,4]{1,0:T(4,128)} %neighbors_hbm.1, s32[4,4]{1,0:T(4,128)} %mask_hbm.1, s32[4,128]{1,0:T(4,128)} %aggregate_ref.1, f32[4,4,128,128]{3,2,1,0:T(8,128)S(1)} %get-tuple-element.28.stiffness_ref, ...), custom_call_target="tpu_custom_call" | custom-call | tf_op jit(solution)/shard_map/pallas_call | solution.py:310
  7.4 0.0 collective-permute-done.near_ref
  7.5 0.0 collective-permute-done.1.far_ref
  7.5 0.5 %shard_map.97 = (f32[4,24,128]{2,1,0:T(8,128)S(1)}, f32[48,128]{1,0:T(8,128)S(1)}, f32[48,128]{1,0:T(8,128)S(1)}) custom-call(f32[4,24,128]{2,1,0:T(8,128)S(1)} %get-tuple-element.25.field_ref.field0_ref, f32[48,128]{1,0:T(8,128)S(1)} %collective-permute-done.near_ref, f32[48,128]{1,0:T(8,128)S(1)} %collective-permute-done.1.far_ref, ...), custom_call_target="tpu_custom_call" | custom-call | tf_op jit(solution)/shard_map/pallas_call | solution.py:323
  8.0 0.1 collective-permute-start.2
  8.1 0.9 %collective-permute-start.3 = (f32[48,128]{1,0:T(8,128)S(1)}, f32[48,128]{1,0:T(8,128)S(1)}, u32[]{:S(2)}, u32[]{:S(2)}) collective-permute-start(f32[48,128]{1,0:T(8,128)S(1)} %get-tuple-element.34), channel_id=1, source_target_pairs={{0,24},{8,16},{16,8},{24,0},{1,25},{9,17},{17,9},{25,1},{2,26},{10... | collective-permute-start | bytes 73736 | tf_op jit(solution)/shard_map/ppermute | solution.py:270
  9.0 5.5 %all-to-all-start = ((f32[32,2,128]{2,1,0:T(2,128)}), f32[32,2,128]{2,1,0:T(2,128)S(1)}, u32[]{:S(2)}, u32[]{:S(2)}) async-start(f32[32,2,128]{2,1,0:T(2,128)} %get-tuple-element.41), calls=%async_computation | async-start | bytes 65536 | tf_op jit(solution)/shard_map/all_to_all | solution.py:325
  14.5 0.0 collective-permute-done.2.refs_1_
  14.5 0.0 collective-permute-done.3.refs_2_
  14.5 0.5 %shard_map.98 = (f32[4,24,128]{2,1,0:T(8,128)S(1)}, f32[96,128]{1,0:T(8,128)S(1)}, f32[96,128]{1,0:T(8,128)S(1)}, f32[16,512]{1,0:T(8,128)S(1)}) custom-call(f32[4,24,128]{2,1,0:T(8,128)S(1)} %get-tuple-element.32.refs_0_.field1_ref, f32[48,128]{1,0:T(8,128)S(1)} %collective-permute-done.2.refs_1_, f32[48,128]{1,0:T(8,128)S(1)} %collective-permute-done.3.refs_2_, ...), custom_call_target="tpu_custom_call" | custom-call | tf_op jit(solution)/shard_map/pallas_call | solution.py:328
  15.0 0.0 copy-start
  15.0 0.3 collective-permute-start.4
  15.4 1.6 %collective-permute-start.5 = (f32[96,128]{1,0:T(8,128)S(1)}, f32[96,128]{1,0:T(8,128)S(1)}, u32[]{:S(2)}, u32[]{:S(2)}) collective-permute-start(f32[96,128]{1,0:T(8,128)S(1)} %get-tuple-element.39), channel_id=1, source_target_pairs={{0,24},{8,16},{16,8},{24,0},{1,25},{9,17},{17,9},{25,1},{2,26},{10... | collective-permute-start | bytes 147464 | tf_op jit(solution)/shard_map/ppermute | solution.py:270
  17.0 2.4 %collective-permute-start.6 = (f32[16,512]{1,0:T(8,128)S(1)}, f32[16,512]{1,0:T(8,128)S(1)}, u32[]{:S(2)}, u32[]{:S(2)}) collective-permute-start(f32[16,512]{1,0:T(8,128)S(1)} %get-tuple-element.42), channel_id=1, source_target_pairs={{0,4},{1,5},{2,6},{3,7},{4,0},{5,1},{6,2},{7,3},{8,12},{9,13},{10,... | collective-permute-start | bytes 98312 | tf_op jit(solution)/shard_map/ppermute | solution.py:265
  19.4 0.2 shard_map.99.early_ref
  19.6 2.2 %all-to-all-done = f32[32,2,128]{2,1,0:T(2,128)S(1)} async-done(((f32[32,2,128]{2,1,0:T(2,128)}), f32[32,2,128]{2,1,0:T(2,128)S(1)}, u32[]{:S(2)}, u32[]{:S(2)}) %all-to-all-start) | async-done | bytes 32800 | tf_op jit(solution)/shard_map/all_to_all | solution.py:325
  21.8 0.0 collective-permute-done.4.near_ref
  21.8 0.0 collective-permute-done.5.far_ref
  21.8 0.6 %shard_map.100 = (f32[4,24,128]{2,1,0:T(8,128)S(1)}, f32[24,128]{1,0:T(8,128)S(1)}) custom-call(f32[4,24,128]{2,1,0:T(8,128)S(1)} %get-tuple-element.36.field2_ref.field_ref, f32[96,128]{1,0:T(8,128)S(1)} %collective-permute-done.4.near_ref, f32[96,128]{1,0:T(8,128)S(1)} %collective-permute-done.5.far_ref, ...), custom_call_target="tpu_custom_call" | custom-call | tf_op jit(solution)/shard_map/pallas_call | solution.py:334
  22.4 0.0 collective-permute-done.6.after_ref
  22.5 0.7 %shard_map.101 = f32[32,3,4,128]{3,2,1,0:T(4,128)} custom-call(f32[3,24,128]{2,1,0:T(8,128)S(1)} %shard_map.99.early_ref, f32[24,128]{1,0:T(8,128)S(1)} %get-tuple-element.40.late_ref, f32[32,128]{1,0:T(8,128)S(1)} %bitcast.12, f32[16,512]{1,0:T(8,128)S(1)} %collective-permute-done.6.after_ref), custom_call_target="tpu_custom_call" | custom-call | tf_op jit(solution)/shard_map/pallas_call | solution.py:339
  23.2 4.3 %all-to-all-start.1 = ((f32[32,3,4,128]{3,2,1,0:T(4,128)}), f32[32,3,4,128]{3,2,1,0:T(4,128)S(1)}, u32[]{:S(2)}, u32[]{:S(2)}) async-start(f32[32,3,4,128]{3,2,1,0:T(4,128)} %shard_map.101), calls=%async_computation.1 | async-start | bytes 393216 | tf_op jit(solution)/shard_map/all_to_all | solution.py:340
  27.5 2.7 %collective-permute-start.10 = (f32[32,512]{1,0:T(8,128)S(1)}, f32[32,512]{1,0:T(8,128)S(1)}, u32[]{:S(2)}, u32[]{:S(2)}) collective-permute-start(f32[32,512]{1,0:T(8,128)S(1)} %constant_dynamic-update-slice_fusion.refs_0_), channel_id=1, source_target_pairs={{0,3},{1,2},{2,1},{3,0},{4,7},{5,6},{6,5},{7,4},{8,11},{9,10},{10,... | collective-permute-start | bytes 196616 | tf_op jit(solution)/shard_map/ppermute | solution.py:265
  30.2 0.6 %collective-permute-start.9 = (f32[32,512]{1,0:T(8,128)S(1)}, f32[32,512]{1,0:T(8,128)S(1)}, u32[]{:S(2)}, u32[]{:S(2)}) collective-permute-start(f32[32,512]{1,0:T(8,128)S(1)} %constant_dynamic-update-slice_fusion.refs_0_), channel_id=1, source_target_pairs={{0,2},{1,3},{2,0},{3,1},{4,6},{5,7},{6,4},{7,5},{8,10},{9,11},{10,... | collective-permute-start | bytes 196616 | tf_op jit(solution)/shard_map/ppermute | solution.py:265
  30.8 0.3 collective-permute-start.8
  31.0 5.0 %all-to-all-done.1 = f32[32,3,4,128]{3,2,1,0:T(4,128)S(1)} async-done(((f32[32,3,4,128]{3,2,1,0:T(4,128)}), f32[32,3,4,128]{3,2,1,0:T(4,128)S(1)}, u32[]{:S(2)}, u32[]{:S(2)}) %all-to-all-start.1) | async-done | bytes 196640 | tf_op jit(solution)/shard_map/all_to_all | solution.py:340
  36.0 0.2 collective-permute-start.7
  36.2 0.7 %shard_map.103 = (f32[4,24,128]{2,1,0:T(8,128)}, f32[4,24,128]{2,1,0:T(8,128)S(1)}) custom-call(f32[4,24,128]{2,1,0:T(8,128)S(1)} %get-tuple-element.25.field_ref.field0_ref, f32[4,24,128]{2,1,0:T(8,128)S(1)} %get-tuple-element.32.refs_0_.field1_ref, f32[4,24,128]{2,1,0:T(8,128)S(1)} %get-tuple-element.36.field2_ref.field_ref, ...), custom_call_target="tpu_custom_call" | custom-call | tf_op jit(solution)/shard_map/pallas_call | solution.py:341
  36.9 0.0 collective-permute-done.10.refs_3_
  36.9 0.0 collective-permute-done.9.refs_2_
  36.9 0.0 collective-permute-done.8.refs_1_
  36.9 0.0 copy-done
  36.9 0.1 shard_map.102
  37.1 0.3 collective-permute-done.7.other_ref
  37.3 1.0 %shard_map.104 = f32[4,24,128]{2,1,0:T(8,128)} custom-call(f32[12,512]{1,0:T(8,128)S(1)} %bitcast.15, f32[12,512]{1,0:T(8,128)S(1)} %collective-permute-done.7.other_ref, bf16[512,256]{1,0:T(8,128)(2,1)S(1)} %get-tuple-element.43.right_ref, bf16[128,512]{1,0:T(8,128)(2,1)S(1)} %get-tuple-element.44.places_ref, f32[4,24,128]{2,1,0:T(8,128)S(1)} %get-tuple-element.46.answer_ref), custom_call_target="tpu_custom_call" | custom-call | tf_op jit(solution)/shard_map/pallas_call | solution.py:351
  (7 shorter events, 0.1 us)
Async XLA Ops:
  2.0 5.5 %collective-permute-start = (f32[48,128]{1,0:T(8,128)S(1)}, f32[48,128]{1,0:T(8,128)S(1)}, u32[]{:S(2)}, u32[]{:S(2)}) collective-permute-start(f32[48,128]{1,0:T(8,128)S(1)} %get-tuple-element.26), channel_id=1, source_target_pairs={{0,8},{8,0},{16,24},{24,16},{1,9},{9,1},{17,25},{25,17},{2,10},{10... | collective-permute-start | bytes 73736 | tf_op jit(solution)/shard_map/ppermute | solution.py:265
  2.5 5.0 %collective-permute-start.1 = (f32[48,128]{1,0:T(8,128)S(1)}, f32[48,128]{1,0:T(8,128)S(1)}, u32[]{:S(2)}, u32[]{:S(2)}) collective-permute-start(f32[48,128]{1,0:T(8,128)S(1)} %get-tuple-element.27), channel_id=1, source_target_pairs={{0,24},{8,16},{16,8},{24,0},{1,25},{9,17},{17,9},{25,1},{2,26},{10... | collective-permute-start | bytes 73736 | tf_op jit(solution)/shard_map/ppermute | solution.py:270
  8.0 6.6 %collective-permute-start.2 = (f32[48,128]{1,0:T(8,128)S(1)}, f32[48,128]{1,0:T(8,128)S(1)}, u32[]{:S(2)}, u32[]{:S(2)}) collective-permute-start(f32[48,128]{1,0:T(8,128)S(1)} %get-tuple-element.33), channel_id=1, source_target_pairs={{0,8},{8,0},{16,24},{24,16},{1,9},{9,1},{17,25},{25,17},{2,10},{10... | collective-permute-start | bytes 73736 | tf_op jit(solution)/shard_map/ppermute | solution.py:265
  8.1 6.4 %collective-permute-start.3 = (f32[48,128]{1,0:T(8,128)S(1)}, f32[48,128]{1,0:T(8,128)S(1)}, u32[]{:S(2)}, u32[]{:S(2)}) collective-permute-start(f32[48,128]{1,0:T(8,128)S(1)} %get-tuple-element.34), channel_id=1, source_target_pairs={{0,24},{8,16},{16,8},{24,0},{1,25},{9,17},{17,9},{25,1},{2,26},{10... | collective-permute-start | bytes 73736 | tf_op jit(solution)/shard_map/ppermute | solution.py:270
  9.0 12.8 %all-to-all-start = ((f32[32,2,128]{2,1,0:T(2,128)}), f32[32,2,128]{2,1,0:T(2,128)S(1)}, u32[]{:S(2)}, u32[]{:S(2)}) async-start(f32[32,2,128]{2,1,0:T(2,128)} %get-tuple-element.41), calls=%async_computation | async-start | bytes 65536 | tf_op jit(solution)/shard_map/all_to_all | solution.py:325
  15.0 21.9 %copy-start = (s32[4,128]{1,0:T(4,128)S(1)}, s32[4,128]{1,0:T(4,128)}, u32[]{:S(2)}) copy-start(s32[4,128]{1,0:T(4,128)} %aggregate_ref.1) | copy-start | bytes 6148
  15.0 6.8 %collective-permute-start.4 = (f32[96,128]{1,0:T(8,128)S(1)}, f32[96,128]{1,0:T(8,128)S(1)}, u32[]{:S(2)}, u32[]{:S(2)}) collective-permute-start(f32[96,128]{1,0:T(8,128)S(1)} %get-tuple-element.38), channel_id=1, source_target_pairs={{0,8},{8,0},{16,24},{24,16},{1,9},{9,1},{17,25},{25,17},{2,10},{10... | collective-permute-start | bytes 147464 | tf_op jit(solution)/shard_map/ppermute | solution.py:265
  15.4 6.5 %collective-permute-start.5 = (f32[96,128]{1,0:T(8,128)S(1)}, f32[96,128]{1,0:T(8,128)S(1)}, u32[]{:S(2)}, u32[]{:S(2)}) collective-permute-start(f32[96,128]{1,0:T(8,128)S(1)} %get-tuple-element.39), channel_id=1, source_target_pairs={{0,24},{8,16},{16,8},{24,0},{1,25},{9,17},{17,9},{25,1},{2,26},{10... | collective-permute-start | bytes 147464 | tf_op jit(solution)/shard_map/ppermute | solution.py:270
  17.0 5.5 %collective-permute-start.6 = (f32[16,512]{1,0:T(8,128)S(1)}, f32[16,512]{1,0:T(8,128)S(1)}, u32[]{:S(2)}, u32[]{:S(2)}) collective-permute-start(f32[16,512]{1,0:T(8,128)S(1)} %get-tuple-element.42), channel_id=1, source_target_pairs={{0,4},{1,5},{2,6},{3,7},{4,0},{5,1},{6,2},{7,3},{8,12},{9,13},{10,... | collective-permute-start | bytes 98312 | tf_op jit(solution)/shard_map/ppermute | solution.py:265
  23.2 12.8 %all-to-all-start.1 = ((f32[32,3,4,128]{3,2,1,0:T(4,128)}), f32[32,3,4,128]{3,2,1,0:T(4,128)S(1)}, u32[]{:S(2)}, u32[]{:S(2)}) async-start(f32[32,3,4,128]{3,2,1,0:T(4,128)} %shard_map.101), calls=%async_computation.1 | async-start | bytes 393216 | tf_op jit(solution)/shard_map/all_to_all | solution.py:340
  27.5 9.4 %collective-permute-start.10 = (f32[32,512]{1,0:T(8,128)S(1)}, f32[32,512]{1,0:T(8,128)S(1)}, u32[]{:S(2)}, u32[]{:S(2)}) collective-permute-start(f32[32,512]{1,0:T(8,128)S(1)} %constant_dynamic-update-slice_fusion.refs_0_), channel_id=1, source_target_pairs={{0,3},{1,2},{2,1},{3,0},{4,7},{5,6},{6,5},{7,4},{8,11},{9,10},{10,... | collective-permute-start | bytes 196616 | tf_op jit(solution)/shard_map/ppermute | solution.py:265
  30.2 6.7 %collective-permute-start.9 = (f32[32,512]{1,0:T(8,128)S(1)}, f32[32,512]{1,0:T(8,128)S(1)}, u32[]{:S(2)}, u32[]{:S(2)}) collective-permute-start(f32[32,512]{1,0:T(8,128)S(1)} %constant_dynamic-update-slice_fusion.refs_0_), channel_id=1, source_target_pairs={{0,2},{1,3},{2,0},{3,1},{4,6},{5,7},{6,4},{7,5},{8,10},{9,11},{10,... | collective-permute-start | bytes 196616 | tf_op jit(solution)/shard_map/ppermute | solution.py:265
  30.8 6.1 %collective-permute-start.8 = (f32[32,512]{1,0:T(8,128)S(1)}, f32[32,512]{1,0:T(8,128)S(1)}, u32[]{:S(2)}, u32[]{:S(2)}) collective-permute-start(f32[32,512]{1,0:T(8,128)S(1)} %constant_dynamic-update-slice_fusion.refs_0_), channel_id=1, source_target_pairs={{0,1},{1,0},{2,3},{3,2},{4,5},{5,4},{6,7},{7,6},{8,9},{9,8},{10,11... | collective-permute-start | bytes 196616 | tf_op jit(solution)/shard_map/ppermute | solution.py:265
  36.0 1.3 %collective-permute-start.7 = (f32[12,512]{1,0:T(8,128)S(1)}, f32[12,512]{1,0:T(8,128)S(1)}, u32[]{:S(2)}, u32[]{:S(2)}) collective-permute-start(f32[12,512]{1,0:T(8,128)S(1)} %bitcast.14), channel_id=1, source_target_pairs={{0,8},{8,0},{16,24},{24,16},{1,9},{9,1},{17,25},{25,17},{2,10},{10... | collective-permute-start | bytes 73736 | tf_op jit(solution)/shard_map/ppermute | solution.py:265

commit v4 on v3

--- a/solution.py
+++ b/solution.py
@@ -60,17 +60,16 @@
 
 
 def start_kernel(
-    send_hbm, loads_hbm, diagonal_hbm, stiffness_hbm, inverse_hbm,
-    field_ref, near_ref, far_ref, diagonal_ref, choice_ref, stiffness_ref, inverse_ref,
+    send_hbm, loads_hbm, diagonal_hbm,
+    field_ref, near_ref, far_ref, diagonal_ref, choice_ref,
     loads_ref, send_ref, sems,
 ):
     blocks, _, size = loads_ref.shape
     ghosts = send_ref.shape[0] // 2
     copies = start_copies([
-        (send_hbm, send_ref), (diagonal_hbm, diagonal_ref), (loads_hbm, loads_ref), (stiffness_hbm, stiffness_ref),
-        (inverse_hbm, inverse_ref),
+        (send_hbm, send_ref), (diagonal_hbm, diagonal_ref), (loads_hbm, loads_ref)
     ], sems)
-    for copy in copies[:3]:
+    for copy in copies:
         copy.wait()
     odd = parity()
     for j in range(ghosts):
@@ -83,66 +82,88 @@
     for b in range(blocks):
         field_ref[b] = loads_ref[b] / diagonal_ref[b : b + 1, :]
     write_messages(choice_ref, field_ref, near_ref, far_ref)
-    for copy in copies[3:]:
-        copy.wait()
 
 
 def prepare_kernel(
-    neighbors_hbm, mask_hbm, aggregate_hbm, stiffness_ref, diagonal_ref, parts_ref, places_ref, peaks_ref,
-    total_ref, aggregate_ref, neighbors_ref, mask_ref, sems,
+    neighbors_hbm, mask_hbm, aggregate_hbm, inverse_hbm, stiffness_hbm, diagonal_ref,
+    inner_ref, outer_ref, places_ref, inverse_ref, peaks_hbm,
+    total_ref, live_ref, stiffness_ref, aggregate_ref, peaks_ref, neighbors_ref, mask_ref, sems,
 ):
     blocks, slots, size, _ = stiffness_ref.shape
     entries = total_ref.shape[0]
     ghosts = (entries - blocks) // 2
+    inside = blocks + ghosts
     copies = start_copies([
-        (neighbors_hbm, neighbors_ref), (mask_hbm, mask_ref), (aggregate_hbm, aggregate_ref)
+        (neighbors_hbm, neighbors_ref), (mask_hbm, mask_ref),
+        *((stiffness_hbm.at[b], stiffness_ref.at[b]) for b in range(blocks)),
+        (aggregate_hbm, aggregate_ref), (inverse_hbm, inverse_ref),
     ], sems)
-    for copy in copies:
-        copy.wait()
-    odd = parity()
-    peak = jnp.zeros((8, size), f32)
-    for b in range(blocks):
-        total_ref[...] = jnp.zeros_like(total_ref)
+    copies[0].wait()
+    copies[1].wait()
+    peak = jnp.zeros((1, size), f32)
+    for b in range(blocks):
+        copies[2 + b].wait()
         ratio = jnp.zeros((size, size), f32)
         for s in range(slots):
+            live = (stiffness_ref[b, s] * mask_ref[b, s].astype(f32)).T
+            live_ref[b, s] = live
+            ratio = ratio + jnp.abs(live)
+        peak = jnp.maximum(peak, jnp.sum(ratio, axis=0, keepdims=True) / diagonal_ref[b : b + 1, :])
+    peak = jnp.max(peak, axis=1, keepdims=True).reshape(1, 1, 1)
+    peaks_ref[...] = jnp.broadcast_to(peak, peaks_ref.shape)
+    sent = pltpu.make_async_copy(peaks_ref, peaks_hbm, sems.at[len(copies)])
+    sent.start()
+    odd = parity()
+    for b in range(blocks):
+        total_ref[...] = jnp.zeros_like(total_ref)
+        for s in range(slots):
             entry = neighbors_ref[b, s]
-            swapped = jnp.where(entry < blocks + ghosts, entry + ghosts, entry - ghosts)
+            swapped = jnp.where(entry < inside, entry + ghosts, entry - ghosts)
             entry = jnp.where((entry >= blocks) & (odd == 0), swapped, entry)
-            live = stiffness_ref[b, s] * mask_ref[b, s].astype(f32)
-            ratio = ratio + jnp.abs(live)
-            total_ref[entry] = total_ref[entry] + live.T
+            total_ref[entry] = total_ref[entry] + live_ref[b, s]
         for entry in range(entries):
-            parts_ref[b, entry * size : (entry + 1) * size, :] = beside(total_ref[entry])
-        rows = lax.dot_general(
-            jnp.ones((8, size), f32), ratio, TRANSPOSED,
-            precision=lax.Precision.HIGHEST, preferred_element_type=f32,
-        )
-        peak = jnp.maximum(peak, rows / diagonal_ref[b : b + 1, :])
-    peak = jnp.max(peak[:1], axis=1, keepdims=True).reshape(1, 1, 1)
-    peaks_ref[...] = jnp.broadcast_to(peak, peaks_ref.shape)
+            part = beside(total_ref[entry])
+            if entry < inside:
+                inner_ref[b, entry * size : (entry + 1) * size, :] = part
+            else:
+                outer_ref[b, (entry - inside) * size : (entry - inside + 1) * size, :] = part
+    for copy in copies[2 + blocks :]:
+        copy.wait()
     index = lax.broadcasted_iota(jnp.int32, (places_ref.shape[0], size), 0)
     for b in range(blocks):
         hit = index == aggregate_ref[b : b + 1, :]
         places_ref[:, b * size : (b + 1) * size] = hit.astype(f32).astype(bf16)
-
-
-def couple(field_ref, near_ref, far_ref, parts_ref, diagonal_ref, next_ref):
+    sent.wait()
+
+
+def products(fields, parts_ref, out_ref, start_ref=None):
+    extended = jnp.concatenate([stacked(field) for field in fields], axis=1)
+    blocks, comps, size = out_ref.shape
+    for b in range(blocks):
+        product = jnp.dot(extended, parts_ref[b], preferred_element_type=f32)
+        value = product[:comps, :size] + product[:comps, size:] + product[comps:, :size]
+        out_ref[b] = value if start_ref is None else start_ref[b] + value
+
+
+def inner_kernel(field_ref, near_ref, inner_ref, sum_ref):
     blocks, comps, size = field_ref.shape
-    ghosts = (parts_ref.shape[1] // size - blocks) // 2
+    ghosts = inner_ref.shape[1] // size - blocks
+    fields = [field_ref[b] for b in range(blocks)] + [near_ref[j * comps : (j + 1) * comps] for j in range(ghosts)]
+    products(fields, inner_ref, sum_ref)
+
+
+def couple(sum_ref, far_ref, outer_ref, diagonal_ref, next_ref):
+    blocks, comps, size = sum_ref.shape
+    ghosts = outer_ref.shape[1] // size
     me = lax.axis_index("wide")
     inside = jnp.where((me == 0) | (me == lax.axis_size("wide") - 1), 0.0, 1.0).astype(f32)
-    extended = [stacked(field_ref[b]) for b in range(blocks)]
-    extended += [stacked(near_ref[j * comps : (j + 1) * comps]) for j in range(ghosts)]
-    extended += [stacked(far_ref[j * comps : (j + 1) * comps] * inside) for j in range(ghosts)]
-    extended = jnp.concatenate(extended, axis=1)
-    for b in range(blocks):
-        product = jnp.dot(extended, parts_ref[b], preferred_element_type=f32)
-        coupled = product[:comps, :size] + product[:comps, size:] + product[comps:, :size]
-        next_ref[b] = coupled / diagonal_ref[b : b + 1, :]
-
-
-def step_kernel(field_ref, near_ref, far_ref, parts_ref, diagonal_ref, choice_ref, next_ref, near_out, far_out):
-    couple(field_ref, near_ref, far_ref, parts_ref, diagonal_ref, next_ref)
+    products([far_ref[j * comps : (j + 1) * comps] * inside for j in range(ghosts)], outer_ref, next_ref, sum_ref)
+    for b in range(blocks):
+        next_ref[b] = next_ref[b] / diagonal_ref[b : b + 1, :]
+
+
+def step_kernel(sum_ref, far_ref, outer_ref, diagonal_ref, choice_ref, next_ref, near_out, far_out):
+    couple(sum_ref, far_ref, outer_ref, diagonal_ref, next_ref)
     write_messages(choice_ref, next_ref, near_out, far_out)
 
 
@@ -170,8 +191,8 @@
         sums_ref[k] = value
 
 
-def last_step_kernel(field_ref, near_ref, far_ref, parts_ref, diagonal_ref, places_ref, next_ref, sums_ref):
-    couple(field_ref, near_ref, far_ref, parts_ref, diagonal_ref, next_ref)
+def last_step_kernel(sum_ref, far_ref, outer_ref, diagonal_ref, places_ref, next_ref, sums_ref):
+    couple(sum_ref, far_ref, outer_ref, diagonal_ref, next_ref)
     (sums_ref[...],) = restrict([next_ref], diagonal_ref, places_ref)
 
 
@@ -202,7 +223,7 @@
 
 
 def largest(peaks_ref):
-    return 1.0 + jnp.max(peaks_ref[...], axis=0, keepdims=True)
+    return 1.0 + jnp.max(peaks_ref[...], axis=0)[0:1, 0:128]
 
 
 def outgoing_kernel(early_ref, late_ref, peaks_ref, after_ref, outgoing_ref):
@@ -286,9 +307,9 @@
     field = like(blocks, comps, size)
     message = like(ghosts * comps, size)
 
-    def call(kernel, in_specs, out_shape, scratch=()):
+    def call(kernel, in_specs, out_shape, scratch=(), out_specs=None):
         return pl.pallas_call(
-            kernel, in_specs=in_specs, out_specs=jax.tree.map(lambda _: VMEM, out_shape), out_shape=out_shape,
+            kernel, in_specs=in_specs, out_specs=out_specs or jax.tree.map(lambda _: VMEM, out_shape), out_shape=out_shape,
             scratch_shapes=scratch, compiler_params=LIMIT,
         )
 
@@ -296,43 +317,45 @@
         far = swap_far(far)
         return swap(near, "wide", 1), far
 
-    field0, near, far, scale, choice, live, inverse = call(
-        start_kernel, [HBM] * 5,
+    field0, near, far, scale, choice = call(
+        start_kernel, [HBM] * 3,
+        (field, message, message, like(blocks, size), like(2 * ghosts * blocks, size)),
+        [
+            pltpu.VMEM(loads.shape, f32), pltpu.SMEM(send_list.shape, jnp.int32), pltpu.SemaphoreType.DMA((3,)),
+        ],
+    )(*from_hbm(send_list, loads, diagonal))
+    near, far = halo(near, far)
+    parts = like(blocks, (blocks + ghosts) * size, 2 * size, dtype=bf16)
+    peaks = like(wide * narrow, 1, 192)
+    inner, outer, places, inverse, peaks = call(
+        prepare_kernel, [HBM] * 5 + [VMEM],
         (
-            field, message, message, like(blocks, size), like(2 * ghosts * blocks, size), like(*stiffness.shape),
-            like(*coarse_inverse.shape),
+            parts, like(blocks, ghosts * size, 2 * size, dtype=bf16),
+            like(members, blocks * size, dtype=bf16), like(*coarse_inverse.shape), peaks,
         ),
         [
-            pltpu.VMEM(loads.shape, f32), pltpu.SMEM(send_list.shape, jnp.int32), pltpu.SemaphoreType.DMA((5,)),
+            pltpu.VMEM((entries, size, size), f32), pltpu.VMEM(stiffness.shape, f32), pltpu.VMEM(stiffness.shape, f32),
+            pltpu.VMEM(aggregate.shape, jnp.int32), pltpu.VMEM(peaks.shape, f32),
+            pltpu.SMEM(neighbors.shape, jnp.int32), pltpu.SMEM(slot_mask.shape, jnp.int32),
+            pltpu.SemaphoreType.DMA((5 + blocks,)),
         ],
-    )(*from_hbm(send_list, loads, diagonal, stiffness, coarse_inverse))
-    near, far = halo(near, far)
-    parts, places, peaks = call(
-        prepare_kernel, [HBM] * 3 + [VMEM] * 2,
-        (
-            like(blocks, entries * size, 2 * size, dtype=bf16), like(members, blocks * size, dtype=bf16),
-            like(wide * narrow, 2, size),
-        ),
-        [
-            pltpu.VMEM((entries, size, size), f32), pltpu.VMEM(aggregate.shape, jnp.int32),
-            pltpu.SMEM(neighbors.shape, jnp.int32), pltpu.SMEM(slot_mask.shape, jnp.int32),
-            pltpu.SemaphoreType.DMA((3,)),
-        ],
-    )(*from_hbm(neighbors, slot_mask, aggregate), live, scale)
-    step = call(step_kernel, [VMEM] * 6, (field, message, message))
-    field1, near, far = step(field0, near, far, parts, scale, choice)
+        (VMEM, VMEM, VMEM, VMEM, HBM),
+    )(*from_hbm(neighbors, slot_mask, aggregate, coarse_inverse, stiffness), scale)
+    within = call(inner_kernel, [VMEM] * 3, field)
+    field1, near, far = call(step_kernel, [VMEM] * 5, (field, message, message))(
+        within(field0, near, inner), far, outer, scale, choice
+    )
     near, far = halo(near, far)
     peaks = lax.all_to_all(peaks, AXES, 0, 0)
-    peaks = peaks[:, 0]
-    longer = like(2 * ghosts * comps, size)
-    field2, near, far, inverse = call(passing_step_kernel, [VMEM] * 7, (field, longer, longer, like(*coarse_inverse.shape)))(
-        field1, near, far, parts, scale, choice, inverse
+    longer = like(ghosts * comps, size)
+    field2, near, far, inverse = call(passing_step_kernel, [VMEM] * 6, (field, longer, longer, like(*coarse_inverse.shape)))(
+        within(field1, near, inner), far, outer, scale, choice, inverse
     )
     near, far = halo(near, far)
     early = call(restrict_kernel, [VMEM] * 5, like(3, comps, members))(field0, field1, field2, scale, places)
     arrived = swap(inverse, "narrow", narrow // 2)
-    field3, late = call(last_step_kernel, [VMEM] * 6, (field, like(comps, members)))(
-        field2, near, far, parts, scale, places
+    field3, late = call(last_step_kernel, [VMEM] * 5, (field, like(comps, members)))(
+        within(field2, near, inner), far, outer, scale, places
     )
 
     half = comps // 2

time: 38.6 us -> 38 us (0.984)
  waiting for transfers between devices: 7.47 us -> 6.5 us
    all_to_all x1, waiting for transfers between devices: 2.21 us -> 0.19 us  [shards(): peaks = lax.all_to_all(peaks, AXES, 0, 0)]
    ppermute x3, waiting for transfers between devices: 0.01 us -> 1.07 us  [swap_far(): lax.ppermute(value, 'wide', [(i, (i + 1 if i % 2 else i - 1) % count) for...]
    ppermute x3, starting transfers between devices: 5.19 us -> 4.43 us  [swap_far(): lax.ppermute(value, 'wide', [(i, (i + 1 if i % 2 else i - 1) % count) for...]
    all_to_all x1, starting transfers between devices: 5.5 us -> 6.22 us  [shards(): peaks = lax.all_to_all(peaks, AXES, 0, 0)]
    pallas_call x5 -> x8, Pallas kernels: 5.23 us -> 5.45 us  [the longest x1 2.64 us: shards(): call(prepare_kernel, [HBM] * 5 + [VMEM], (parts, like(blocks, ghosts * si...]
  transfers between devices with their start and end apart: 13 -> 13, of which waited for: 3 -> 4; matrix products, arithmetic and copies ran while one was open for 0% -> 0% of each run, Pallas kernels for 12% -> 14%
where the time goes in v4:
time: 38 us; the launch traced here: 37.7 us
  starting transfers between devices  22.2 us (58%)
  Pallas kernels  8.12 us (21%)
  waiting for transfers between devices  6.5 us (17%)
  between operations  0.82 us (2%)
    ppermute x8, starting transfers between devices, swap(): lax.ppermute(value, axis, [(i, i ^ bit) for i in range(lax.axis_size(axis...  7.12 us
    all_to_all x1, starting transfers between devices, shards(): peaks = lax.all_to_all(peaks, AXES, 0, 0)  6.22 us
    all_to_all x1, waiting for transfers between devices, shards(): incoming = lax.all_to_all(outgoing, AXES, 0, 0)  4.96 us
    all_to_all x1, starting transfers between devices, shards(): incoming = lax.all_to_all(outgoing, AXES, 0, 0)  4.44 us
    ppermute x3, starting transfers between devices, swap_far(): lax.ppermute(value, 'wide', [(i, (i + 1 if i % 2 else i - 1) % count) for...  4.43 us
    pallas_call x1, Pallas kernels, shards(): call(prepare_kernel, [HBM] * 5 + [VMEM], (parts, like(blocks, ghosts * si...  2.64 us
    ppermute x3, waiting for transfers between devices, swap_far(): lax.ppermute(value, 'wide', [(i, (i + 1 if i % 2 else i - 1) % count) for...  1.07 us
    pallas_call x1, Pallas kernels, shards(): call(coarse_kernel, [VMEM] * 5, field)(own, other, right, reads, answer)  0.96 us
  transfers between devices with their start and end apart: 13, of which 4 were waited for; matrix products, arithmetic and copies ran while one was open for 0% of the time, Pallas kernels for 14%

profile of v4, /device:TPU:0, one launch (start us, length us, event | category | flops | bytes accessed | tf_op | source)
XLA Modules:
  0.0 37.7 jit_solution(3359324204542196256)
XLA Ops:
  0.6 0.9 %shard_map.95 = (f32[4,24,128]{2,1,0:T(8,128)S(1)}, f32[48,128]{1,0:T(8,128)S(1)}, f32[48,128]{1,0:T(8,128)S(1)}, f32[4,128]{1,0:T(4,128)S(1)}, f32[16,128]{1,0:T(8,128)S(1)}) custom-call(s32[4]{0:T(128)} %send_hbm.1, f32[4,24,128]{2,1,0:T(8,128)} %loads_hbm.1, f32[4,128]{1,0:T(4,128)} %diagonal_hbm.1), custom_call_target="tpu_custom_call" | custom-call | tf_op jit(solution)/shard_map/pallas_call | solution.py:320
  1.5 0.5 %collective-permute-start = (f32[48,128]{1,0:T(8,128)S(1)}, f32[48,128]{1,0:T(8,128)S(1)}, u32[]{:S(2)}, u32[]{:S(2)}) collective-permute-start(f32[48,128]{1,0:T(8,128)S(1)} %get-tuple-element.26), channel_id=1, source_target_pairs={{0,8},{8,0},{16,24},{24,16},{1,9},{9,1},{17,25},{25,17},{2,10},{10... | collective-permute-start | bytes 73736 | tf_op jit(solution)/shard_map/ppermute | solution.py:286
  2.0 2.6 %collective-permute-start.1 = (f32[48,128]{1,0:T(8,128)S(1)}, f32[48,128]{1,0:T(8,128)S(1)}, u32[]{:S(2)}, u32[]{:S(2)}) collective-permute-start(f32[48,128]{1,0:T(8,128)S(1)} %get-tuple-element.29), channel_id=1, source_target_pairs={{0,24},{8,16},{16,8},{24,0},{1,25},{9,17},{17,9},{25,1},{2,26},{10... | collective-permute-start | bytes 73736 | tf_op jit(solution)/shard_map/ppermute | solution.py:291
  4.7 2.6 %shard_map.96 = (bf16[4,768,256]{2,1,0:T(8,128)(2,1)S(1)}, bf16[4,256,256]{2,1,0:T(8,128)(2,1)S(1)}, bf16[128,512]{1,0:T(8,128)(2,1)S(1)}, f32[16,512]{1,0:T(8,128)S(1)}, f32[32,1,192]{2,1,0:T(1,128)}) custom-call(s32[4,4]{1,0:T(4,128)} %neighbors_hbm.1, s32[4,4]{1,0:T(4,128)} %mask_hbm.1, s32[4,128]{1,0:T(4,128)} %aggregate_ref.1, f32[16,512]{1,0:T(8,128)} %inverse_hbm.1, ...), custom_call_target="tpu_custom_call" | custom-call | tf_op jit(solution)/shard_map/pallas_call | solution.py:330
  7.3 0.0 collective-permute-done.near_ref
  7.3 0.4 %shard_map.97.sum_ref = f32[4,24,128]{2,1,0:T(8,128)S(1)} custom-call(f32[4,24,128]{2,1,0:T(8,128)S(1)} %get-tuple-element.25.field_ref.field0_ref, f32[48,128]{1,0:T(8,128)S(1)} %collective-permute-done.near_ref, bf16[4,768,256]{2,1,0:T(8,128)(2,1)S(1)} %get-tuple-element.28.inner_ref), custom_call_target="tpu_custom_call" | custom-call | tf_op jit(solution)/shard_map/pallas_call | solution.py:346
  7.7 0.0 collective-permute-done.1.far_ref
  7.7 0.2 shard_map.98
  8.0 0.1 collective-permute-start.2
  8.1 0.2 collective-permute-start.3
  8.3 6.2 %all-to-all-start = ((f32[32,1,192]{2,1,0:T(1,128)}), f32[32,1,192]{2,1,0:T(1,128)S(1)}, u32[]{:S(2)}, u32[]{:S(2)}) async-start(f32[32,1,192]{2,1,0:T(1,128)} %get-tuple-element.41), calls=%async_computation | async-start | bytes 65536 | tf_op jit(solution)/shard_map/all_to_all | solution.py:349
  14.5 0.0 collective-permute-done.2.near_ref
  14.5 0.4 %shard_map.99.refs_0_ = f32[4,24,128]{2,1,0:T(8,128)S(1)} custom-call(f32[4,24,128]{2,1,0:T(8,128)S(1)} %get-tuple-element.32.field_ref.field1_ref, f32[48,128]{1,0:T(8,128)S(1)} %collective-permute-done.2.near_ref, bf16[4,768,256]{2,1,0:T(8,128)(2,1)S(1)} %get-tuple-element.28.inner_ref), custom_call_target="tpu_custom_call" | custom-call | tf_op jit(solution)/shard_map/pallas_call | solution.py:352
  14.9 0.0 collective-permute-done.3.refs_1_
  14.9 0.2 shard_map.100
  15.2 2.7 %collective-permute-start.6 = (f32[16,512]{1,0:T(8,128)S(1)}, f32[16,512]{1,0:T(8,128)S(1)}, u32[]{:S(2)}, u32[]{:S(2)}) collective-permute-start(f32[16,512]{1,0:T(8,128)S(1)} %get-tuple-element.42), channel_id=1, source_target_pairs={{0,4},{1,5},{2,6},{3,7},{4,0},{5,1},{6,2},{7,3},{8,12},{9,13},{10,... | collective-permute-start | bytes 98312 | tf_op jit(solution)/shard_map/ppermute | solution.py:286
  17.9 0.0 collective-permute-start.4
  17.9 1.6 %collective-permute-start.5 = (f32[48,128]{1,0:T(8,128)S(1)}, f32[48,128]{1,0:T(8,128)S(1)}, u32[]{:S(2)}, u32[]{:S(2)}) collective-permute-start(f32[48,128]{1,0:T(8,128)S(1)} %get-tuple-element.39), channel_id=1, source_target_pairs={{0,24},{8,16},{16,8},{24,0},{1,25},{9,17},{17,9},{25,1},{2,26},{10... | collective-permute-start | bytes 73736 | tf_op jit(solution)/shard_map/ppermute | solution.py:291
  19.5 0.2 shard_map.101.early_ref
  19.7 0.0 copy-start
  19.7 0.0 collective-permute-done.4.near_ref
  19.7 0.4 %shard_map.102.sum_ref = f32[4,24,128]{2,1,0:T(8,128)S(1)} custom-call(f32[4,24,128]{2,1,0:T(8,128)S(1)} %get-tuple-element.36.field2_ref.field_ref, f32[48,128]{1,0:T(8,128)S(1)} %collective-permute-done.4.near_ref, bf16[4,768,256]{2,1,0:T(8,128)(2,1)S(1)} %get-tuple-element.28.inner_ref), custom_call_target="tpu_custom_call" | custom-call | tf_op jit(solution)/shard_map/pallas_call | solution.py:358
  20.1 1.1 %collective-permute-done.5.far_ref = f32[48,128]{1,0:T(8,128)S(1)} collective-permute-done((f32[48,128]{1,0:T(8,128)S(1)}, f32[48,128]{1,0:T(8,128)S(1)}, u32[]{:S(2)}, u32[]{:S(2)}) %collective-permute-start.5) | collective-permute-done | bytes 24608 | tf_op jit(solution)/shard_map/ppermute | solution.py:291
  21.2 0.3 shard_map.103
  21.5 0.2 all-to-all-done.peaks_ref
  21.7 0.0 collective-permute-done.6.after_ref
  21.7 0.7 %shard_map.104 = f32[32,3,4,128]{3,2,1,0:T(4,128)} custom-call(f32[3,24,128]{2,1,0:T(8,128)S(1)} %shard_map.101.early_ref, f32[24,128]{1,0:T(8,128)S(1)} %get-tuple-element.40.late_ref, f32[32,1,192]{2,1,0:T(1,128)S(1)} %all-to-all-done.peaks_ref, f32[16,512]{1,0:T(8,128)S(1)} %collective-permute-done.6.after_ref), custom_call_target="tpu_custom_call" | custom-call | tf_op jit(solution)/shard_map/pallas_call | solution.py:362
  22.4 4.4 %all-to-all-start.1 = ((f32[32,3,4,128]{3,2,1,0:T(4,128)}), f32[32,3,4,128]{3,2,1,0:T(4,128)S(1)}, u32[]{:S(2)}, u32[]{:S(2)}) async-start(f32[32,3,4,128]{3,2,1,0:T(4,128)} %shard_map.104), calls=%async_computation.1 | async-start | bytes 393216 | tf_op jit(solution)/shard_map/all_to_all | solution.py:363
  26.9 2.7 %collective-permute-start.10 = (f32[32,512]{1,0:T(8,128)S(1)}, f32[32,512]{1,0:T(8,128)S(1)}, u32[]{:S(2)}, u32[]{:S(2)}) collective-permute-start(f32[32,512]{1,0:T(8,128)S(1)} %constant_dynamic-update-slice_fusion.refs_0_), channel_id=1, source_target_pairs={{0,3},{1,2},{2,1},{3,0},{4,7},{5,6},{6,5},{7,4},{8,11},{9,10},{10,... | collective-permute-start | bytes 196616 | tf_op jit(solution)/shard_map/ppermute | solution.py:286
  29.6 0.6 %collective-permute-start.9 = (f32[32,512]{1,0:T(8,128)S(1)}, f32[32,512]{1,0:T(8,128)S(1)}, u32[]{:S(2)}, u32[]{:S(2)}) collective-permute-start(f32[32,512]{1,0:T(8,128)S(1)} %constant_dynamic-update-slice_fusion.refs_0_), channel_id=1, source_target_pairs={{0,2},{1,3},{2,0},{3,1},{4,6},{5,7},{6,4},{7,5},{8,10},{9,11},{10,... | collective-permute-start | bytes 196616 | tf_op jit(solution)/shard_map/ppermute | solution.py:286
  30.2 0.3 collective-permute-start.8
  30.5 5.0 %all-to-all-done.1 = f32[32,3,4,128]{3,2,1,0:T(4,128)S(1)} async-done(((f32[32,3,4,128]{3,2,1,0:T(4,128)}), f32[32,3,4,128]{3,2,1,0:T(4,128)S(1)}, u32[]{:S(2)}, u32[]{:S(2)}) %all-to-all-start.1) | async-done | bytes 196640 | tf_op jit(solution)/shard_map/all_to_all | solution.py:363
  35.5 0.2 collective-permute-start.7
  35.7 0.7 %shard_map.106 = (f32[4,24,128]{2,1,0:T(8,128)}, f32[4,24,128]{2,1,0:T(8,128)S(1)}) custom-call(f32[4,24,128]{2,1,0:T(8,128)S(1)} %get-tuple-element.25.field_ref.field0_ref, f32[4,24,128]{2,1,0:T(8,128)S(1)} %get-tuple-element.32.field_ref.field1_ref, f32[4,24,128]{2,1,0:T(8,128)S(1)} %get-tuple-element.36.field2_ref.field_ref, ...), custom_call_target="tpu_custom_call" | custom-call | tf_op jit(solution)/shard_map/pallas_call | solution.py:364
  36.3 0.0 collective-permute-done.10.refs_3_
  36.3 0.0 collective-permute-done.9.refs_2_
  36.3 0.0 collective-permute-done.8.refs_1_
  36.4 0.0 copy-done
  36.4 0.1 shard_map.105
  36.5 0.3 collective-permute-done.7.other_ref
  36.8 1.0 %shard_map.107 = f32[4,24,128]{2,1,0:T(8,128)} custom-call(f32[12,512]{1,0:T(8,128)S(1)} %bitcast.10, f32[12,512]{1,0:T(8,128)S(1)} %collective-permute-done.7.other_ref, bf16[512,256]{1,0:T(8,128)(2,1)S(1)} %get-tuple-element.43.right_ref, bf16[128,512]{1,0:T(8,128)(2,1)S(1)} %get-tuple-element.44.places_ref, f32[4,24,128]{2,1,0:T(8,128)S(1)} %get-tuple-element.46.answer_ref), custom_call_target="tpu_custom_call" | custom-call | tf_op jit(solution)/shard_map/pallas_call | solution.py:374
  (6 shorter events, 0.1 us)
Async XLA Ops:
  1.5 5.8 %collective-permute-start = (f32[48,128]{1,0:T(8,128)S(1)}, f32[48,128]{1,0:T(8,128)S(1)}, u32[]{:S(2)}, u32[]{:S(2)}) collective-permute-start(f32[48,128]{1,0:T(8,128)S(1)} %get-tuple-element.26), channel_id=1, source_target_pairs={{0,8},{8,0},{16,24},{24,16},{1,9},{9,1},{17,25},{25,17},{2,10},{10... | collective-permute-start | bytes 73736 | tf_op jit(solution)/shard_map/ppermute | solution.py:286
  2.0 5.7 %collective-permute-start.1 = (f32[48,128]{1,0:T(8,128)S(1)}, f32[48,128]{1,0:T(8,128)S(1)}, u32[]{:S(2)}, u32[]{:S(2)}) collective-permute-start(f32[48,128]{1,0:T(8,128)S(1)} %get-tuple-element.29), channel_id=1, source_target_pairs={{0,24},{8,16},{16,8},{24,0},{1,25},{9,17},{17,9},{25,1},{2,26},{10... | collective-permute-start | bytes 73736 | tf_op jit(solution)/shard_map/ppermute | solution.py:291
  8.0 6.6 %collective-permute-start.2 = (f32[48,128]{1,0:T(8,128)S(1)}, f32[48,128]{1,0:T(8,128)S(1)}, u32[]{:S(2)}, u32[]{:S(2)}) collective-permute-start(f32[48,128]{1,0:T(8,128)S(1)} %get-tuple-element.33), channel_id=1, source_target_pairs={{0,8},{8,0},{16,24},{24,16},{1,9},{9,1},{17,25},{25,17},{2,10},{10... | collective-permute-start | bytes 73736 | tf_op jit(solution)/shard_map/ppermute | solution.py:286
  8.1 6.8 %collective-permute-start.3 = (f32[48,128]{1,0:T(8,128)S(1)}, f32[48,128]{1,0:T(8,128)S(1)}, u32[]{:S(2)}, u32[]{:S(2)}) collective-permute-start(f32[48,128]{1,0:T(8,128)S(1)} %get-tuple-element.34), channel_id=1, source_target_pairs={{0,24},{8,16},{16,8},{24,0},{1,25},{9,17},{17,9},{25,1},{2,26},{10... | collective-permute-start | bytes 73736 | tf_op jit(solution)/shard_map/ppermute | solution.py:291
  8.3 13.4 %all-to-all-start = ((f32[32,1,192]{2,1,0:T(1,128)}), f32[32,1,192]{2,1,0:T(1,128)S(1)}, u32[]{:S(2)}, u32[]{:S(2)}) async-start(f32[32,1,192]{2,1,0:T(1,128)} %get-tuple-element.41), calls=%async_computation | async-start | bytes 65536 | tf_op jit(solution)/shard_map/all_to_all | solution.py:349
  15.2 6.6 %collective-permute-start.6 = (f32[16,512]{1,0:T(8,128)S(1)}, f32[16,512]{1,0:T(8,128)S(1)}, u32[]{:S(2)}, u32[]{:S(2)}) collective-permute-start(f32[16,512]{1,0:T(8,128)S(1)} %get-tuple-element.42), channel_id=1, source_target_pairs={{0,4},{1,5},{2,6},{3,7},{4,0},{5,1},{6,2},{7,3},{8,12},{9,13},{10,... | collective-permute-start | bytes 98312 | tf_op jit(solution)/shard_map/ppermute | solution.py:286
  17.9 1.8 %collective-permute-start.4 = (f32[48,128]{1,0:T(8,128)S(1)}, f32[48,128]{1,0:T(8,128)S(1)}, u32[]{:S(2)}, u32[]{:S(2)}) collective-permute-start(f32[48,128]{1,0:T(8,128)S(1)} %get-tuple-element.38), channel_id=1, source_target_pairs={{0,8},{8,0},{16,24},{24,16},{1,9},{9,1},{17,25},{25,17},{2,10},{10... | collective-permute-start | bytes 73736 | tf_op jit(solution)/shard_map/ppermute | solution.py:286
  17.9 3.3 %collective-permute-start.5 = (f32[48,128]{1,0:T(8,128)S(1)}, f32[48,128]{1,0:T(8,128)S(1)}, u32[]{:S(2)}, u32[]{:S(2)}) collective-permute-start(f32[48,128]{1,0:T(8,128)S(1)} %get-tuple-element.39), channel_id=1, source_target_pairs={{0,24},{8,16},{16,8},{24,0},{1,25},{9,17},{17,9},{25,1},{2,26},{10... | collective-permute-start | bytes 73736 | tf_op jit(solution)/shard_map/ppermute | solution.py:291
  19.7 16.7 %copy-start = (s32[4,128]{1,0:T(4,128)S(1)}, s32[4,128]{1,0:T(4,128)}, u32[]{:S(2)}) copy-start(s32[4,128]{1,0:T(4,128)} %aggregate_ref.1) | copy-start | bytes 6148
  22.4 13.0 %all-to-all-start.1 = ((f32[32,3,4,128]{3,2,1,0:T(4,128)}), f32[32,3,4,128]{3,2,1,0:T(4,128)S(1)}, u32[]{:S(2)}, u32[]{:S(2)}) async-start(f32[32,3,4,128]{3,2,1,0:T(4,128)} %shard_map.104), calls=%async_computation.1 | async-start | bytes 393216 | tf_op jit(solution)/shard_map/all_to_all | solution.py:363
  26.9 9.4 %collective-permute-start.10 = (f32[32,512]{1,0:T(8,128)S(1)}, f32[32,512]{1,0:T(8,128)S(1)}, u32[]{:S(2)}, u32[]{:S(2)}) collective-permute-start(f32[32,512]{1,0:T(8,128)S(1)} %constant_dynamic-update-slice_fusion.refs_0_), channel_id=1, source_target_pairs={{0,3},{1,2},{2,1},{3,0},{4,7},{5,6},{6,5},{7,4},{8,11},{9,10},{10,... | collective-permute-start | bytes 196616 | tf_op jit(solution)/shard_map/ppermute | solution.py:286
  29.6 6.7 %collective-permute-start.9 = (f32[32,512]{1,0:T(8,128)S(1)}, f32[32,512]{1,0:T(8,128)S(1)}, u32[]{:S(2)}, u32[]{:S(2)}) collective-permute-start(f32[32,512]{1,0:T(8,128)S(1)} %constant_dynamic-update-slice_fusion.refs_0_), channel_id=1, source_target_pairs={{0,2},{1,3},{2,0},{3,1},{4,6},{5,7},{6,4},{7,5},{8,10},{9,11},{10,... | collective-permute-start | bytes 196616 | tf_op jit(solution)/shard_map/ppermute | solution.py:286
  30.2 6.1 %collective-permute-start.8 = (f32[32,512]{1,0:T(8,128)S(1)}, f32[32,512]{1,0:T(8,128)S(1)}, u32[]{:S(2)}, u32[]{:S(2)}) collective-permute-start(f32[32,512]{1,0:T(8,128)S(1)} %constant_dynamic-update-slice_fusion.refs_0_), channel_id=1, source_target_pairs={{0,1},{1,0},{2,3},{3,2},{4,5},{5,4},{6,7},{7,6},{8,9},{9,8},{10,11... | collective-permute-start | bytes 196616 | tf_op jit(solution)/shard_map/ppermute | solution.py:286
  35.5 1.3 %collective-permute-start.7 = (f32[12,512]{1,0:T(8,128)S(1)}, f32[12,512]{1,0:T(8,128)S(1)}, u32[]{:S(2)}, u32[]{:S(2)}) collective-permute-start(f32[12,512]{1,0:T(8,128)S(1)} %bitcast.9), channel_id=1, source_target_pairs={{0,8},{8,0},{16,24},{24,16},{1,9},{9,1},{17,25},{25,17},{2,10},{10... | collective-permute-start | bytes 73736 | tf_op jit(solution)/shard_map/ppermute | solution.py:286

commit v5 on v4

--- a/solution.py
+++ b/solution.py
@@ -222,14 +222,14 @@
     return less(remainder, applied(direction)), answer
 
 
-def largest(peaks_ref):
-    return 1.0 + jnp.max(peaks_ref[...], axis=0)[0:1, 0:128]
-
-
-def outgoing_kernel(early_ref, late_ref, peaks_ref, after_ref, outgoing_ref):
+def largest(peaks_ref, size):
+    return 1.0 + jnp.max(peaks_ref[...], axis=0)[0:1, :size]
+
+
+def outgoing_kernel(early_ref, late_ref, peaks_ref, outgoing_ref):
     targets, quarter, four, _ = outgoing_ref.shape
     half = quarter * four
-    on_residual, _ = coefficients(largest(peaks_ref))
+    on_residual, _ = coefficients(largest(peaks_ref, late_ref.shape[1]))
     sums = sum(c * f for c, f in zip(on_residual, [early_ref[0], early_ref[1], early_ref[2], late_ref[...]]))
     narrow = lax.axis_size("narrow")
     for target in range(targets):
@@ -239,7 +239,7 @@
 
 
 def finish_kernel(field0_ref, field1_ref, field2_ref, field3_ref, diagonal_ref, peaks_ref, residual_ref, answer_ref):
-    on_residual, on_answer = coefficients(largest(peaks_ref))
+    on_residual, on_answer = coefficients(largest(peaks_ref, diagonal_ref.shape[1]))
     for b in range(field0_ref.shape[0]):
         fields = [field0_ref[b], field1_ref[b], field2_ref[b], field3_ref[b]]
         residual_ref[b] = diagonal_ref[b : b + 1, :] * sum(c * f for c, f in zip(on_residual, fields))
@@ -282,6 +282,11 @@
     return [pltpu.with_memory_space_constraint(array, pltpu.HBM) for array in arrays]
 
 
+def longer(value, rows):
+    times = -(-rows // value.shape[0])
+    return jnp.concatenate([value] * times, axis=0)[:rows]
+
+
 def swap(value, axis, bit):
     return lax.ppermute(value, axis, [(i, i ^ bit) for i in range(lax.axis_size(axis))])
 
@@ -306,6 +311,8 @@
     unknowns = coarse_inverse.shape[1]
     field = like(blocks, comps, size)
     message = like(ghosts * comps, size)
+    further = like(ghosts * comps + 8, size)
+    furthest = like(3 * ghosts * comps // 2, size)
 
     def call(kernel, in_specs, out_shape, scratch=(), out_specs=None):
         return pl.pallas_call(
@@ -319,14 +326,14 @@
 
     field0, near, far, scale, choice = call(
         start_kernel, [HBM] * 3,
-        (field, message, message, like(blocks, size), like(2 * ghosts * blocks, size)),
+        (field, message, further, like(blocks, size), like(2 * ghosts * blocks, size)),
         [
             pltpu.VMEM(loads.shape, f32), pltpu.SMEM(send_list.shape, jnp.int32), pltpu.SemaphoreType.DMA((3,)),
         ],
     )(*from_hbm(send_list, loads, diagonal))
     near, far = halo(near, far)
     parts = like(blocks, (blocks + ghosts) * size, 2 * size, dtype=bf16)
-    peaks = like(wide * narrow, 1, 192)
+    peaks = like(wide * narrow, 1, 3 * size // 2)
     inner, outer, places, inverse, peaks = call(
         prepare_kernel, [HBM] * 5 + [VMEM],
         (
@@ -342,28 +349,30 @@
         (VMEM, VMEM, VMEM, VMEM, HBM),
     )(*from_hbm(neighbors, slot_mask, aggregate, coarse_inverse, stiffness), scale)
     within = call(inner_kernel, [VMEM] * 3, field)
-    field1, near, far = call(step_kernel, [VMEM] * 5, (field, message, message))(
+    field1, near, far = call(step_kernel, [VMEM] * 5, (field, message, further))(
         within(field0, near, inner), far, outer, scale, choice
     )
     near, far = halo(near, far)
     peaks = lax.all_to_all(peaks, AXES, 0, 0)
-    longer = like(ghosts * comps, size)
-    field2, near, far, inverse = call(passing_step_kernel, [VMEM] * 6, (field, longer, longer, like(*coarse_inverse.shape)))(
+    field2, near, far, inverse = call(passing_step_kernel, [VMEM] * 6, (field, message, furthest, like(*coarse_inverse.shape)))(
         within(field1, near, inner), far, outer, scale, choice, inverse
     )
     near, far = halo(near, far)
     early = call(restrict_kernel, [VMEM] * 5, like(3, comps, members))(field0, field1, field2, scale, places)
-    arrived = swap(inverse, "narrow", narrow // 2)
+    arrived = swap(longer(inverse, 3 * inverse.shape[0] // 2), "narrow", narrow // 2)[: inverse.shape[0]]
     field3, late = call(last_step_kernel, [VMEM] * 5, (field, like(comps, members)))(
         within(field2, near, inner), far, outer, scale, places
     )
 
     half = comps // 2
-    outgoing = call(outgoing_kernel, [VMEM] * 4, like(wide * narrow, half // 4, 4, members))(early, late, peaks, arrived)
+    outgoing = call(outgoing_kernel, [VMEM] * 3, like(wide * narrow, half // 4, 4, members))(early, late, peaks)
     incoming = lax.all_to_all(outgoing, AXES, 0, 0)
     residual, answer = call(finish_kernel, [VMEM] * 6, (field, field))(field0, field1, field2, field3, scale, peaks)
     inverse = jnp.concatenate([inverse, arrived], axis=0)
-    gathered = [inverse] + [swap(inverse, "narrow", offset) for offset in range(1, narrow // 2)]
+    gathered = [inverse]
+    for offset in range(1, narrow // 2):
+        sent = longer(inverse, 9 * inverse.shape[0] // 4) if offset == 1 else inverse
+        gathered.append(swap(sent, "narrow", offset)[: inverse.shape[0]])
     right, reads = call(
         inverse_kernel, [VMEM] * (1 + len(gathered)),
         (like(unknowns, 2 * members, dtype=bf16), like(members, blocks * size, dtype=bf16)),

time: 38 us -> 36.8 us (0.968)
  starting transfers between devices: 22.2 us -> 21 us
    all_to_all x1, starting transfers between devices: 4.44 us -> 3.27 us  [shards(): incoming = lax.all_to_all(outgoing, AXES, 0, 0)]
    ppermute x3, waiting for transfers between devices: 1.07 us -> 0.01 us  [swap_far(): lax.ppermute(value, 'wide', [(i, (i + 1 if i % 2 else i - 1) % count) for...]
    all_to_all x1, waiting for transfers between devices: 0.19 us -> 1.24 us  [shards(): peaks = lax.all_to_all(peaks, AXES, 0, 0)]
  transfers between devices with their start and end apart: 13 -> 13, of which waited for: 4 -> 4; matrix products, arithmetic and copies ran while one was open for 0% -> 0% of each run, Pallas kernels for 14% -> 17%
where the time goes in v5:
time: 36.8 us; the launch traced here: 36.5 us
  starting transfers between devices  21 us (57%)
  Pallas kernels  8.12 us (22%)
  waiting for transfers between devices  6.41 us (17%)
  between operations  0.87 us (2%)
    ppermute x8, starting transfers between devices, swap(): lax.ppermute(value, axis, [(i, i ^ bit) for i in range(lax.axis_size(axis...  7.5 us
    all_to_all x1, starting transfers between devices, shards(): peaks = lax.all_to_all(peaks, AXES, 0, 0)  5.95 us
    all_to_all x1, waiting for transfers between devices, shards(): incoming = lax.all_to_all(outgoing, AXES, 0, 0)  4.9 us
    ppermute x3, starting transfers between devices, swap_far(): lax.ppermute(value, 'wide', [(i, (i + 1 if i % 2 else i - 1) % count) for...  4.3 us
    all_to_all x1, starting transfers between devices, shards(): incoming = lax.all_to_all(outgoing, AXES, 0, 0)  3.27 us
    pallas_call x1, Pallas kernels, shards(): call(prepare_kernel, [HBM] * 5 + [VMEM], (parts, like(blocks, ghosts * si...  2.64 us
    all_to_all x1, waiting for transfers between devices, shards(): peaks = lax.all_to_all(peaks, AXES, 0, 0)  1.24 us
    pallas_call x1, Pallas kernels, shards(): call(coarse_kernel, [VMEM] * 5, field)(own, other, right, reads, answer)  0.96 us
  transfers between devices with their start and end apart: 13, of which 4 were waited for; matrix products, arithmetic and copies ran while one was open for 0% of the time, Pallas kernels for 17%

profile of v5, /device:TPU:0, one launch (start us, length us, event | category | flops | bytes accessed | tf_op | source)
XLA Modules:
  0.0 36.5 jit_solution(18116494794840556719)
XLA Ops:
  0.6 0.9 %shard_map.95 = (f32[4,24,128]{2,1,0:T(8,128)S(1)}, f32[48,128]{1,0:T(8,128)S(1)}, f32[56,128]{1,0:T(8,128)S(1)}, f32[4,128]{1,0:T(4,128)S(1)}, f32[16,128]{1,0:T(8,128)S(1)}) custom-call(s32[4]{0:T(128)} %send_hbm.1, f32[4,24,128]{2,1,0:T(8,128)} %loads_hbm.1, f32[4,128]{1,0:T(4,128)} %diagonal_hbm.1), custom_call_target="tpu_custom_call" | custom-call | tf_op jit(solution)/shard_map/pallas_call | solution.py:327
  1.5 2.5 %collective-permute-start.1 = (f32[56,128]{1,0:T(8,128)S(1)}, f32[56,128]{1,0:T(8,128)S(1)}, u32[]{:S(2)}, u32[]{:S(2)}) collective-permute-start(f32[56,128]{1,0:T(8,128)S(1)} %get-tuple-element.29), channel_id=1, source_target_pairs={{0,24},{8,16},{16,8},{24,0},{1,25},{9,17},{17,9},{25,1},{2,26},{10... | collective-permute-start | bytes 86024 | tf_op jit(solution)/shard_map/ppermute | solution.py:296
  4.0 0.7 %collective-permute-start = (f32[48,128]{1,0:T(8,128)S(1)}, f32[48,128]{1,0:T(8,128)S(1)}, u32[]{:S(2)}, u32[]{:S(2)}) collective-permute-start(f32[48,128]{1,0:T(8,128)S(1)} %get-tuple-element.26), channel_id=1, source_target_pairs={{0,8},{8,0},{16,24},{24,16},{1,9},{9,1},{17,25},{25,17},{2,10},{10... | collective-permute-start | bytes 73736 | tf_op jit(solution)/shard_map/ppermute | solution.py:291
  4.7 2.6 %shard_map.96 = (bf16[4,768,256]{2,1,0:T(8,128)(2,1)S(1)}, bf16[4,256,256]{2,1,0:T(8,128)(2,1)S(1)}, bf16[128,512]{1,0:T(8,128)(2,1)S(1)}, f32[16,512]{1,0:T(8,128)S(1)}, f32[32,1,192]{2,1,0:T(1,128)}) custom-call(s32[4,4]{1,0:T(4,128)} %neighbors_hbm.1, s32[4,4]{1,0:T(4,128)} %mask_hbm.1, s32[4,128]{1,0:T(4,128)} %aggregate_ref.1, f32[16,512]{1,0:T(8,128)} %inverse_hbm.1, ...), custom_call_target="tpu_custom_call" | custom-call | tf_op jit(solution)/shard_map/pallas_call | solution.py:337
  7.3 0.0 collective-permute-done.near_ref
  7.3 0.4 %shard_map.97.sum_ref = f32[4,24,128]{2,1,0:T(8,128)S(1)} custom-call(f32[4,24,128]{2,1,0:T(8,128)S(1)} %get-tuple-element.25.field_ref.field0_ref, f32[48,128]{1,0:T(8,128)S(1)} %collective-permute-done.near_ref, bf16[4,768,256]{2,1,0:T(8,128)(2,1)S(1)} %get-tuple-element.28.inner_ref), custom_call_target="tpu_custom_call" | custom-call | tf_op jit(solution)/shard_map/pallas_call | solution.py:353
  7.7 0.0 collective-permute-done.1.far_ref
  7.7 0.2 shard_map.98
  8.0 0.2 collective-permute-start.3
  8.1 0.4 %collective-permute-start.2 = (f32[48,128]{1,0:T(8,128)S(1)}, f32[48,128]{1,0:T(8,128)S(1)}, u32[]{:S(2)}, u32[]{:S(2)}) collective-permute-start(f32[48,128]{1,0:T(8,128)S(1)} %get-tuple-element.33), channel_id=1, source_target_pairs={{0,8},{8,0},{16,24},{24,16},{1,9},{9,1},{17,25},{25,17},{2,10},{10... | collective-permute-start | bytes 73736 | tf_op jit(solution)/shard_map/ppermute | solution.py:291
  8.5 5.9 %all-to-all-start = ((f32[32,1,192]{2,1,0:T(1,128)}), f32[32,1,192]{2,1,0:T(1,128)S(1)}, u32[]{:S(2)}, u32[]{:S(2)}) async-start(f32[32,1,192]{2,1,0:T(1,128)} %get-tuple-element.41), calls=%async_computation | async-start | bytes 65536 | tf_op jit(solution)/shard_map/all_to_all | solution.py:356
  14.5 0.0 collective-permute-done.2.near_ref
  14.5 0.4 %shard_map.99.refs_0_ = f32[4,24,128]{2,1,0:T(8,128)S(1)} custom-call(f32[4,24,128]{2,1,0:T(8,128)S(1)} %get-tuple-element.32.field_ref.field1_ref, f32[48,128]{1,0:T(8,128)S(1)} %collective-permute-done.2.near_ref, bf16[4,768,256]{2,1,0:T(8,128)(2,1)S(1)} %get-tuple-element.28.inner_ref), custom_call_target="tpu_custom_call" | custom-call | tf_op jit(solution)/shard_map/pallas_call | solution.py:358
  14.9 0.0 collective-permute-done.3.refs_1_
  14.9 0.2 shard_map.100
  15.1 0.3 collective-permute-start.4
  15.4 1.6 %collective-permute-start.5 = (f32[72,128]{1,0:T(8,128)S(1)}, f32[72,128]{1,0:T(8,128)S(1)}, u32[]{:S(2)}, u32[]{:S(2)}) collective-permute-start(f32[72,128]{1,0:T(8,128)S(1)} %get-tuple-element.39), channel_id=1, source_target_pairs={{0,24},{8,16},{16,8},{24,0},{1,25},{9,17},{17,9},{25,1},{2,26},{10... | collective-permute-start | bytes 110600 | tf_op jit(solution)/shard_map/ppermute | solution.py:296
  17.1 2.4 %collective-permute-start.7 = (f32[24,512]{1,0:T(8,128)S(1)}, f32[24,512]{1,0:T(8,128)S(1)}, u32[]{:S(2)}, u32[]{:S(2)}) collective-permute-start(f32[24,512]{1,0:T(8,128)S(1)} %pad_maximum_fusion.1), channel_id=1, source_target_pairs={{0,4},{1,5},{2,6},{3,7},{4,0},{5,1},{6,2},{7,3},{8,12},{9,13},{10,... | collective-permute-start | bytes 147464 | tf_op jit(solution)/shard_map/ppermute | solution.py:291
  19.5 0.2 shard_map.101.early_ref
  19.7 0.0 collective-permute-done.4.near_ref
  19.7 0.4 %shard_map.102.sum_ref = f32[4,24,128]{2,1,0:T(8,128)S(1)} custom-call(f32[4,24,128]{2,1,0:T(8,128)S(1)} %get-tuple-element.36.field2_ref.field_ref, f32[48,128]{1,0:T(8,128)S(1)} %collective-permute-done.4.near_ref, bf16[4,768,256]{2,1,0:T(8,128)(2,1)S(1)} %get-tuple-element.28.inner_ref), custom_call_target="tpu_custom_call" | custom-call | tf_op jit(solution)/shard_map/pallas_call | solution.py:364
  20.1 0.0 copy-start
  20.1 0.0 collective-permute-done.5.far_ref
  20.1 0.4 shard_map.103
  20.4 1.2 %all-to-all-done.peaks_ref = f32[32,1,192]{2,1,0:T(1,128)S(1)} async-done(((f32[32,1,192]{2,1,0:T(1,128)}), f32[32,1,192]{2,1,0:T(1,128)S(1)}, u32[]{:S(2)}, u32[]{:S(2)}) %all-to-all-start) | async-done | bytes 24608 | tf_op jit(solution)/shard_map/all_to_all | solution.py:356
  21.7 0.7 %shard_map.104 = f32[32,3,4,128]{3,2,1,0:T(4,128)} custom-call(f32[3,24,128]{2,1,0:T(8,128)S(1)} %shard_map.101.early_ref, f32[24,128]{1,0:T(8,128)S(1)} %get-tuple-element.40.late_ref, f32[32,1,192]{2,1,0:T(1,128)S(1)} %all-to-all-done.peaks_ref), custom_call_target="tpu_custom_call" | custom-call | tf_op jit(solution)/shard_map/pallas_call | solution.py:368
  22.4 3.3 %all-to-all-start.1 = ((f32[32,3,4,128]{3,2,1,0:T(4,128)}), f32[32,3,4,128]{3,2,1,0:T(4,128)S(1)}, u32[]{:S(2)}, u32[]{:S(2)}) async-start(f32[32,3,4,128]{3,2,1,0:T(4,128)} %shard_map.104), calls=%async_computation.1 | async-start | bytes 393216 | tf_op jit(solution)/shard_map/all_to_all | solution.py:369
  25.7 0.0 collective-permute-done.7
  25.8 1.8 %collective-permute-start.8 = (f32[72,512]{1,0:T(8,128)S(1)}, f32[72,512]{1,0:T(8,128)S(1)}, u32[]{:S(2)}, u32[]{:S(2)}) collective-permute-start(f32[72,512]{1,0:T(8,128)S(1)} %slice.18), channel_id=1, source_target_pairs={{0,1},{1,0},{2,3},{3,2},{4,5},{5,4},{6,7},{7,6},{8,9},{9,8},{10,11... | collective-permute-start | bytes 442376 | tf_op jit(solution)/shard_map/ppermute | solution.py:291
  27.6 1.5 %collective-permute-start.10 = (f32[32,512]{1,0:T(8,128)S(1)}, f32[32,512]{1,0:T(8,128)S(1)}, u32[]{:S(2)}, u32[]{:S(2)}) collective-permute-start(f32[32,512]{1,0:T(8,128)S(1)} %pad_maximum_fusion.refs_0_), channel_id=1, source_target_pairs={{0,3},{1,2},{2,1},{3,0},{4,7},{5,6},{6,5},{7,4},{8,11},{9,10},{10,... | collective-permute-start | bytes 196616 | tf_op jit(solution)/shard_map/ppermute | solution.py:291
  29.1 0.3 collective-permute-start.9
  29.3 4.9 %all-to-all-done.1 = f32[32,3,4,128]{3,2,1,0:T(4,128)S(1)} async-done(((f32[32,3,4,128]{3,2,1,0:T(4,128)}), f32[32,3,4,128]{3,2,1,0:T(4,128)S(1)}, u32[]{:S(2)}, u32[]{:S(2)}) %all-to-all-start.1) | async-done | bytes 196640 | tf_op jit(solution)/shard_map/all_to_all | solution.py:369
  34.3 0.2 collective-permute-start.6
  34.5 0.7 %shard_map.106 = (f32[4,24,128]{2,1,0:T(8,128)}, f32[4,24,128]{2,1,0:T(8,128)S(1)}) custom-call(f32[4,24,128]{2,1,0:T(8,128)S(1)} %get-tuple-element.25.field_ref.field0_ref, f32[4,24,128]{2,1,0:T(8,128)S(1)} %get-tuple-element.32.field_ref.field1_ref, f32[4,24,128]{2,1,0:T(8,128)S(1)} %get-tuple-element.36.field2_ref.field_ref, ...), custom_call_target="tpu_custom_call" | custom-call | tf_op jit(solution)/shard_map/pallas_call | solution.py:370
  35.1 0.1 collective-permute-done.8
  35.2 0.0 collective-permute-done.10.refs_3_
  35.2 0.0 collective-permute-done.9.refs_2_
  35.2 0.0 copy-done
  35.2 0.1 shard_map.105
  35.4 0.2 collective-permute-done.6.other_ref
  35.6 1.0 %shard_map.107 = f32[4,24,128]{2,1,0:T(8,128)} custom-call(f32[12,512]{1,0:T(8,128)S(1)} %bitcast.10, f32[12,512]{1,0:T(8,128)S(1)} %collective-permute-done.6.other_ref, bf16[512,256]{1,0:T(8,128)(2,1)S(1)} %get-tuple-element.43.right_ref, bf16[128,512]{1,0:T(8,128)(2,1)S(1)} %get-tuple-element.44.places_ref, f32[4,24,128]{2,1,0:T(8,128)S(1)} %get-tuple-element.46.answer_ref), custom_call_target="tpu_custom_call" | custom-call | tf_op jit(solution)/shard_map/pallas_call | solution.py:383
  (13 shorter events, 0.1 us)
Async XLA Ops:
  1.5 6.2 %collective-permute-start.1 = (f32[56,128]{1,0:T(8,128)S(1)}, f32[56,128]{1,0:T(8,128)S(1)}, u32[]{:S(2)}, u32[]{:S(2)}) collective-permute-start(f32[56,128]{1,0:T(8,128)S(1)} %get-tuple-element.29), channel_id=1, source_target_pairs={{0,24},{8,16},{16,8},{24,0},{1,25},{9,17},{17,9},{25,1},{2,26},{10... | collective-permute-start | bytes 86024 | tf_op jit(solution)/shard_map/ppermute | solution.py:296
  4.0 3.3 %collective-permute-start = (f32[48,128]{1,0:T(8,128)S(1)}, f32[48,128]{1,0:T(8,128)S(1)}, u32[]{:S(2)}, u32[]{:S(2)}) collective-permute-start(f32[48,128]{1,0:T(8,128)S(1)} %get-tuple-element.26), channel_id=1, source_target_pairs={{0,8},{8,0},{16,24},{24,16},{1,9},{9,1},{17,25},{25,17},{2,10},{10... | collective-permute-start | bytes 73736 | tf_op jit(solution)/shard_map/ppermute | solution.py:291
  8.0 6.9 %collective-permute-start.3 = (f32[56,128]{1,0:T(8,128)S(1)}, f32[56,128]{1,0:T(8,128)S(1)}, u32[]{:S(2)}, u32[]{:S(2)}) collective-permute-start(f32[56,128]{1,0:T(8,128)S(1)} %get-tuple-element.34), channel_id=1, source_target_pairs={{0,24},{8,16},{16,8},{24,0},{1,25},{9,17},{17,9},{25,1},{2,26},{10... | collective-permute-start | bytes 86024 | tf_op jit(solution)/shard_map/ppermute | solution.py:296
  8.1 6.4 %collective-permute-start.2 = (f32[48,128]{1,0:T(8,128)S(1)}, f32[48,128]{1,0:T(8,128)S(1)}, u32[]{:S(2)}, u32[]{:S(2)}) collective-permute-start(f32[48,128]{1,0:T(8,128)S(1)} %get-tuple-element.33), channel_id=1, source_target_pairs={{0,8},{8,0},{16,24},{24,16},{1,9},{9,1},{17,25},{25,17},{2,10},{10... | collective-permute-start | bytes 73736 | tf_op jit(solution)/shard_map/ppermute | solution.py:291
  8.5 13.1 %all-to-all-start = ((f32[32,1,192]{2,1,0:T(1,128)}), f32[32,1,192]{2,1,0:T(1,128)S(1)}, u32[]{:S(2)}, u32[]{:S(2)}) async-start(f32[32,1,192]{2,1,0:T(1,128)} %get-tuple-element.41), calls=%async_computation | async-start | bytes 65536 | tf_op jit(solution)/shard_map/all_to_all | solution.py:356
  15.1 4.5 %collective-permute-start.4 = (f32[48,128]{1,0:T(8,128)S(1)}, f32[48,128]{1,0:T(8,128)S(1)}, u32[]{:S(2)}, u32[]{:S(2)}) collective-permute-start(f32[48,128]{1,0:T(8,128)S(1)} %get-tuple-element.38), channel_id=1, source_target_pairs={{0,8},{8,0},{16,24},{24,16},{1,9},{9,1},{17,25},{25,17},{2,10},{10... | collective-permute-start | bytes 73736 | tf_op jit(solution)/shard_map/ppermute | solution.py:291
  15.4 4.6 %collective-permute-start.5 = (f32[72,128]{1,0:T(8,128)S(1)}, f32[72,128]{1,0:T(8,128)S(1)}, u32[]{:S(2)}, u32[]{:S(2)}) collective-permute-start(f32[72,128]{1,0:T(8,128)S(1)} %get-tuple-element.39), channel_id=1, source_target_pairs={{0,24},{8,16},{16,8},{24,0},{1,25},{9,17},{17,9},{25,1},{2,26},{10... | collective-permute-start | bytes 110600 | tf_op jit(solution)/shard_map/ppermute | solution.py:296
  17.1 8.6 %collective-permute-start.7 = (f32[24,512]{1,0:T(8,128)S(1)}, f32[24,512]{1,0:T(8,128)S(1)}, u32[]{:S(2)}, u32[]{:S(2)}) collective-permute-start(f32[24,512]{1,0:T(8,128)S(1)} %pad_maximum_fusion.1), channel_id=1, source_target_pairs={{0,4},{1,5},{2,6},{3,7},{4,0},{5,1},{6,2},{7,3},{8,12},{9,13},{10,... | collective-permute-start | bytes 147464 | tf_op jit(solution)/shard_map/ppermute | solution.py:291
  20.1 15.2 %copy-start = (s32[4,128]{1,0:T(4,128)S(1)}, s32[4,128]{1,0:T(4,128)}, u32[]{:S(2)}) copy-start(s32[4,128]{1,0:T(4,128)} %aggregate_ref.1) | copy-start | bytes 6148
  22.4 11.8 %all-to-all-start.1 = ((f32[32,3,4,128]{3,2,1,0:T(4,128)}), f32[32,3,4,128]{3,2,1,0:T(4,128)S(1)}, u32[]{:S(2)}, u32[]{:S(2)}) async-start(f32[32,3,4,128]{3,2,1,0:T(4,128)} %shard_map.104), calls=%async_computation.1 | async-start | bytes 393216 | tf_op jit(solution)/shard_map/all_to_all | solution.py:369
  25.8 9.5 %collective-permute-start.8 = (f32[72,512]{1,0:T(8,128)S(1)}, f32[72,512]{1,0:T(8,128)S(1)}, u32[]{:S(2)}, u32[]{:S(2)}) collective-permute-start(f32[72,512]{1,0:T(8,128)S(1)} %slice.18), channel_id=1, source_target_pairs={{0,1},{1,0},{2,3},{3,2},{4,5},{5,4},{6,7},{7,6},{8,9},{9,8},{10,11... | collective-permute-start | bytes 442376 | tf_op jit(solution)/shard_map/ppermute | solution.py:291
  27.6 7.6 %collective-permute-start.10 = (f32[32,512]{1,0:T(8,128)S(1)}, f32[32,512]{1,0:T(8,128)S(1)}, u32[]{:S(2)}, u32[]{:S(2)}) collective-permute-start(f32[32,512]{1,0:T(8,128)S(1)} %pad_maximum_fusion.refs_0_), channel_id=1, source_target_pairs={{0,3},{1,2},{2,1},{3,0},{4,7},{5,6},{6,5},{7,4},{8,11},{9,10},{10,... | collective-permute-start | bytes 196616 | tf_op jit(solution)/shard_map/ppermute | solution.py:291
  29.1 6.2 %collective-permute-start.9 = (f32[32,512]{1,0:T(8,128)S(1)}, f32[32,512]{1,0:T(8,128)S(1)}, u32[]{:S(2)}, u32[]{:S(2)}) collective-permute-start(f32[32,512]{1,0:T(8,128)S(1)} %pad_maximum_fusion.refs_0_), channel_id=1, source_target_pairs={{0,2},{1,3},{2,0},{3,1},{4,6},{5,7},{6,4},{7,5},{8,10},{9,11},{10,... | collective-permute-start | bytes 196616 | tf_op jit(solution)/shard_map/ppermute | solution.py:291
  34.3 1.3 %collective-permute-start.6 = (f32[12,512]{1,0:T(8,128)S(1)}, f32[12,512]{1,0:T(8,128)S(1)}, u32[]{:S(2)}, u32[]{:S(2)}) collective-permute-start(f32[12,512]{1,0:T(8,128)S(1)} %bitcast.9), channel_id=1, source_target_pairs={{0,8},{8,0},{16,24},{24,16},{1,9},{9,1},{17,25},{25,17},{2,10},{10... | collective-permute-start | bytes 73736 | tf_op jit(solution)/shard_map/ppermute | solution.py:291

commit v6 on v5

--- a/solution.py
+++ b/solution.py
@@ -60,16 +60,17 @@
 
 
 def start_kernel(
-    send_hbm, loads_hbm, diagonal_hbm,
-    field_ref, near_ref, far_ref, diagonal_ref, choice_ref,
-    loads_ref, send_ref, sems,
+    send_hbm, loads_hbm, diagonal_hbm, mask_hbm, stiffness_hbm,
+    field_ref, near_ref, far_ref, diagonal_ref, choice_ref, live_ref, stiffness_ref,
+    loads_ref, send_ref, mask_ref, sems,
 ):
     blocks, _, size = loads_ref.shape
     ghosts = send_ref.shape[0] // 2
     copies = start_copies([
-        (send_hbm, send_ref), (diagonal_hbm, diagonal_ref), (loads_hbm, loads_ref)
+        (send_hbm, send_ref), (diagonal_hbm, diagonal_ref), (loads_hbm, loads_ref), (mask_hbm, mask_ref),
+        (stiffness_hbm, stiffness_ref),
     ], sems)
-    for copy in copies:
+    for copy in copies[:4]:
         copy.wait()
     odd = parity()
     for j in range(ghosts):
@@ -82,37 +83,40 @@
     for b in range(blocks):
         field_ref[b] = loads_ref[b] / diagonal_ref[b : b + 1, :]
     write_messages(choice_ref, field_ref, near_ref, far_ref)
+    slots = mask_ref.shape[1]
+    for b in range(blocks):
+        for s in range(slots):
+            row = b * slots + s
+            live_ref[row : row + 1, :] = jnp.full((1, size), mask_ref[b, s].astype(f32), f32)
+    copies[4].wait()
 
 
 def prepare_kernel(
-    neighbors_hbm, mask_hbm, aggregate_hbm, inverse_hbm, stiffness_hbm, diagonal_ref,
+    neighbors_hbm, aggregate_hbm, inverse_hbm, stiffness_ref, live_ref, diagonal_ref,
     inner_ref, outer_ref, places_ref, inverse_ref, peaks_hbm,
-    total_ref, live_ref, stiffness_ref, aggregate_ref, peaks_ref, neighbors_ref, mask_ref, sems,
+    total_ref, turned_ref, aggregate_ref, peaks_ref, neighbors_ref, sems,
 ):
     blocks, slots, size, _ = stiffness_ref.shape
     entries = total_ref.shape[0]
     ghosts = (entries - blocks) // 2
     inside = blocks + ghosts
     copies = start_copies([
-        (neighbors_hbm, neighbors_ref), (mask_hbm, mask_ref),
-        *((stiffness_hbm.at[b], stiffness_ref.at[b]) for b in range(blocks)),
-        (aggregate_hbm, aggregate_ref), (inverse_hbm, inverse_ref),
+        (neighbors_hbm, neighbors_ref), (aggregate_hbm, aggregate_ref), (inverse_hbm, inverse_ref)
     ], sems)
-    copies[0].wait()
-    copies[1].wait()
     peak = jnp.zeros((1, size), f32)
     for b in range(blocks):
-        copies[2 + b].wait()
         ratio = jnp.zeros((size, size), f32)
         for s in range(slots):
-            live = (stiffness_ref[b, s] * mask_ref[b, s].astype(f32)).T
-            live_ref[b, s] = live
-            ratio = ratio + jnp.abs(live)
+            row = b * slots + s
+            turned = (stiffness_ref[b, s] * live_ref[row : row + 1, :]).T
+            turned_ref[b, s] = turned
+            ratio = ratio + jnp.abs(turned)
         peak = jnp.maximum(peak, jnp.sum(ratio, axis=0, keepdims=True) / diagonal_ref[b : b + 1, :])
     peak = jnp.max(peak, axis=1, keepdims=True).reshape(1, 1, 1)
     peaks_ref[...] = jnp.broadcast_to(peak, peaks_ref.shape)
     sent = pltpu.make_async_copy(peaks_ref, peaks_hbm, sems.at[len(copies)])
     sent.start()
+    copies[0].wait()
     odd = parity()
     for b in range(blocks):
         total_ref[...] = jnp.zeros_like(total_ref)
@@ -120,14 +124,14 @@
             entry = neighbors_ref[b, s]
             swapped = jnp.where(entry < inside, entry + ghosts, entry - ghosts)
             entry = jnp.where((entry >= blocks) & (odd == 0), swapped, entry)
-            total_ref[entry] = total_ref[entry] + live_ref[b, s]
+            total_ref[entry] = total_ref[entry] + turned_ref[b, s]
         for entry in range(entries):
             part = beside(total_ref[entry])
             if entry < inside:
                 inner_ref[b, entry * size : (entry + 1) * size, :] = part
             else:
                 outer_ref[b, (entry - inside) * size : (entry - inside + 1) * size, :] = part
-    for copy in copies[2 + blocks :]:
+    for copy in copies[1:]:
         copy.wait()
     index = lax.broadcasted_iota(jnp.int32, (places_ref.shape[0], size), 0)
     for b in range(blocks):
@@ -324,30 +328,33 @@
         far = swap_far(far)
         return swap(near, "wide", 1), far
 
-    field0, near, far, scale, choice = call(
-        start_kernel, [HBM] * 3,
-        (field, message, further, like(blocks, size), like(2 * ghosts * blocks, size)),
+    field0, near, far, scale, choice, live, matrix = call(
+        start_kernel, [HBM] * 5,
+        (
+            field, message, further, like(blocks, size), like(2 * ghosts * blocks, size), like(blocks * slots, size),
+            like(*stiffness.shape),
+        ),
         [
-            pltpu.VMEM(loads.shape, f32), pltpu.SMEM(send_list.shape, jnp.int32), pltpu.SemaphoreType.DMA((3,)),
+            pltpu.VMEM(loads.shape, f32), pltpu.SMEM(send_list.shape, jnp.int32),
+            pltpu.SMEM(slot_mask.shape, jnp.int32), pltpu.SemaphoreType.DMA((5,)),
         ],
-    )(*from_hbm(send_list, loads, diagonal))
+    )(*from_hbm(send_list, loads, diagonal, slot_mask, stiffness))
     near, far = halo(near, far)
     parts = like(blocks, (blocks + ghosts) * size, 2 * size, dtype=bf16)
     peaks = like(wide * narrow, 1, 3 * size // 2)
     inner, outer, places, inverse, peaks = call(
-        prepare_kernel, [HBM] * 5 + [VMEM],
+        prepare_kernel, [HBM] * 3 + [VMEM] * 3,
         (
             parts, like(blocks, ghosts * size, 2 * size, dtype=bf16),
             like(members, blocks * size, dtype=bf16), like(*coarse_inverse.shape), peaks,
         ),
         [
-            pltpu.VMEM((entries, size, size), f32), pltpu.VMEM(stiffness.shape, f32), pltpu.VMEM(stiffness.shape, f32),
+            pltpu.VMEM((entries, size, size), f32), pltpu.VMEM(stiffness.shape, f32),
             pltpu.VMEM(aggregate.shape, jnp.int32), pltpu.VMEM(peaks.shape, f32),
-            pltpu.SMEM(neighbors.shape, jnp.int32), pltpu.SMEM(slot_mask.shape, jnp.int32),
-            pltpu.SemaphoreType.DMA((5 + blocks,)),
+            pltpu.SMEM(neighbors.shape, jnp.int32), pltpu.SemaphoreType.DMA((4,)),
         ],
         (VMEM, VMEM, VMEM, VMEM, HBM),
-    )(*from_hbm(neighbors, slot_mask, aggregate, coarse_inverse, stiffness), scale)
+    )(*from_hbm(neighbors, aggregate, coarse_inverse), matrix, live, scale)
     within = call(inner_kernel, [VMEM] * 3, field)
     field1, near, far = call(step_kernel, [VMEM] * 5, (field, message, further))(
         within(field0, near, inner), far, outer, scale, choice

time: 36.8 us -> 36.2 us (0.984)
  Pallas kernels: 8.12 us -> 7.52 us
    all_to_all x1, starting transfers between devices: 5.95 us -> 4.92 us  [shards(): peaks = lax.all_to_all(peaks, AXES, 0, 0)]
    ppermute x3, starting transfers between devices: 4.3 us -> 5.32 us  [swap_far(): lax.ppermute(value, 'wide', [(i, (i + 1 if i % 2 else i - 1) % count) for...]
    pallas_call x2, Pallas kernels: 3.53 us -> 2.93 us  [the longest x1 1.62 us: shards(): call(prepare_kernel, [HBM] * 3 + [VMEM] * 3, (parts, like(blocks, ghosts...]
  transfers between devices with their start and end apart: 13 -> 13, of which waited for: 4 -> 4; matrix products, arithmetic and copies ran while one was open for 0% -> 0% of each run, Pallas kernels for 17% -> 14%
where the time goes in v6:
time: 36.2 us; the launch traced here: 35.9 us
  starting transfers between devices  21 us (58%)
  Pallas kernels  7.52 us (21%)
  waiting for transfers between devices  6.41 us (18%)
  between operations  0.87 us (2%)
    ppermute x8, starting transfers between devices, swap(): lax.ppermute(value, axis, [(i, i ^ bit) for i in range(lax.axis_size(axis...  7.5 us
    ppermute x3, starting transfers between devices, swap_far(): lax.ppermute(value, 'wide', [(i, (i + 1 if i % 2 else i - 1) % count) for...  5.32 us
    all_to_all x1, starting transfers between devices, shards(): peaks = lax.all_to_all(peaks, AXES, 0, 0)  4.92 us
    all_to_all x1, waiting for transfers between devices, shards(): incoming = lax.all_to_all(outgoing, AXES, 0, 0)  4.9 us
    all_to_all x1, starting transfers between devices, shards(): incoming = lax.all_to_all(outgoing, AXES, 0, 0)  3.27 us
    pallas_call x1, Pallas kernels, shards(): call(prepare_kernel, [HBM] * 3 + [VMEM] * 3, (parts, like(blocks, ghosts...  1.62 us
    pallas_call x1, Pallas kernels, shards(): call(start_kernel, [HBM] * 5, (field, message, further, like(blocks, size...  1.32 us
    all_to_all x1, waiting for transfers between devices, shards(): peaks = lax.all_to_all(peaks, AXES, 0, 0)  1.24 us
  transfers between devices with their start and end apart: 13, of which 4 were waited for; matrix products, arithmetic and copies ran while one was open for 0% of the time, Pallas kernels for 14%

profile of v6, /device:TPU:0, one launch (start us, length us, event | category | flops | bytes accessed | tf_op | source)
XLA Modules:
  0.0 35.9 jit_solution(5410370341045625519)
XLA Ops:
  0.6 1.3 %shard_map.95 = (f32[4,24,128]{2,1,0:T(8,128)S(1)}, f32[48,128]{1,0:T(8,128)S(1)}, f32[56,128]{1,0:T(8,128)S(1)}, f32[4,128]{1,0:T(4,128)S(1)}, f32[16,128]{1,0:...) custom-call(s32[4]{0:T(128)} %send_hbm.1, f32[4,24,128]{2,1,0:T(8,128)} %loads_hbm.1, ...), custom_call_target="tpu_custom_call" | custom-call | tf_op jit(solution)/shard_map/pallas_call | solution.py:331
  2.0 2.5 %collective-permute-start.1 = (f32[56,128]{1,0:T(8,128)S(1)}, f32[56,128]{1,0:T(8,128)S(1)}, u32[]{:S(2)}, u32[]{:S(2)}) collective-permute-start(f32[56,128]{1,0:T(8,128)S(1)} %get-tuple-element.33), channel_id=1, source_target_pairs={{0,24},{8,16},{16,8},{24,0},{1,25},{9,17},{17,9},{25,1},{2,26},{10... | collective-permute-start | bytes 86024 | tf_op jit(solution)/shard_map/ppermute | solution.py:300
  4.4 0.7 %collective-permute-start = (f32[48,128]{1,0:T(8,128)S(1)}, f32[48,128]{1,0:T(8,128)S(1)}, u32[]{:S(2)}, u32[]{:S(2)}) collective-permute-start(f32[48,128]{1,0:T(8,128)S(1)} %get-tuple-element.28), channel_id=1, source_target_pairs={{0,8},{8,0},{16,24},{24,16},{1,9},{9,1},{17,25},{25,17},{2,10},{10... | collective-permute-start | bytes 73736 | tf_op jit(solution)/shard_map/ppermute | solution.py:295
  5.1 1.6 %shard_map.96 = (bf16[4,768,256]{2,1,0:T(8,128)(2,1)S(1)}, bf16[4,256,256]{2,1,0:T(8,128)(2,1)S(1)}, bf16[128,512]{1,0:T(8,128)(2,1)S(1)}, f32[16,512]{1,0:T(8,128)S(1)}, f32[32,1,192]{2,1,0:T(1,128)}) custom-call(s32[4,4]{1,0:T(4,128)} %neighbors_hbm.1, s32[4,128]{1,0:T(4,128)} %aggregate_ref.1, f32[16,512]{1,0:T(8,128)} %inverse_hbm.1, ...), custom_call_target="tpu_custom_call" | custom-call | tf_op jit(solution)/shard_map/pallas_call | solution.py:345
  6.7 0.0 collective-permute-done.near_ref
  6.7 0.4 %shard_map.97.sum_ref = f32[4,24,128]{2,1,0:T(8,128)S(1)} custom-call(f32[4,24,128]{2,1,0:T(8,128)S(1)} %get-tuple-element.27.field_ref.field0_ref, f32[48,128]{1,0:T(8,128)S(1)} %collective-permute-done.near_ref, bf16[4,768,256]{2,1,0:T(8,128)(2,1)S(1)} %get-tuple-element.32.inner_ref), custom_call_target="tpu_custom_call" | custom-call | tf_op jit(solution)/shard_map/pallas_call | solution.py:360
  7.1 0.0 collective-permute-done.1.far_ref
  7.1 0.2 shard_map.98
  7.4 1.2 %collective-permute-start.3 = (f32[56,128]{1,0:T(8,128)S(1)}, f32[56,128]{1,0:T(8,128)S(1)}, u32[]{:S(2)}, u32[]{:S(2)}) collective-permute-start(f32[56,128]{1,0:T(8,128)S(1)} %get-tuple-element.38), channel_id=1, source_target_pairs={{0,24},{8,16},{16,8},{24,0},{1,25},{9,17},{17,9},{25,1},{2,26},{10... | collective-permute-start | bytes 86024 | tf_op jit(solution)/shard_map/ppermute | solution.py:300
  8.6 0.4 %collective-permute-start.2 = (f32[48,128]{1,0:T(8,128)S(1)}, f32[48,128]{1,0:T(8,128)S(1)}, u32[]{:S(2)}, u32[]{:S(2)}) collective-permute-start(f32[48,128]{1,0:T(8,128)S(1)} %get-tuple-element.37), channel_id=1, source_target_pairs={{0,8},{8,0},{16,24},{24,16},{1,9},{9,1},{17,25},{25,17},{2,10},{10... | collective-permute-start | bytes 73736 | tf_op jit(solution)/shard_map/ppermute | solution.py:295
  9.0 4.9 %all-to-all-start = ((f32[32,1,192]{2,1,0:T(1,128)}), f32[32,1,192]{2,1,0:T(1,128)S(1)}, u32[]{:S(2)}, u32[]{:S(2)}) async-start(f32[32,1,192]{2,1,0:T(1,128)} %get-tuple-element.45), calls=%async_computation | async-start | bytes 65536 | tf_op jit(solution)/shard_map/all_to_all | solution.py:363
  13.9 0.0 collective-permute-done.2.near_ref
  13.9 0.4 %shard_map.99.refs_0_ = f32[4,24,128]{2,1,0:T(8,128)S(1)} custom-call(f32[4,24,128]{2,1,0:T(8,128)S(1)} %get-tuple-element.36.field_ref.field1_ref, f32[48,128]{1,0:T(8,128)S(1)} %collective-permute-done.2.near_ref, bf16[4,768,256]{2,1,0:T(8,128)(2,1)S(1)} %get-tuple-element.32.inner_ref), custom_call_target="tpu_custom_call" | custom-call | tf_op jit(solution)/shard_map/pallas_call | solution.py:365
  14.3 0.0 collective-permute-done.3.refs_1_
  14.3 0.2 shard_map.100
  14.5 0.3 collective-permute-start.4
  14.9 1.6 %collective-permute-start.5 = (f32[72,128]{1,0:T(8,128)S(1)}, f32[72,128]{1,0:T(8,128)S(1)}, u32[]{:S(2)}, u32[]{:S(2)}) collective-permute-start(f32[72,128]{1,0:T(8,128)S(1)} %get-tuple-element.43), channel_id=1, source_target_pairs={{0,24},{8,16},{16,8},{24,0},{1,25},{9,17},{17,9},{25,1},{2,26},{10... | collective-permute-start | bytes 110600 | tf_op jit(solution)/shard_map/ppermute | solution.py:300
  16.5 2.4 %collective-permute-start.7 = (f32[24,512]{1,0:T(8,128)S(1)}, f32[24,512]{1,0:T(8,128)S(1)}, u32[]{:S(2)}, u32[]{:S(2)}) collective-permute-start(f32[24,512]{1,0:T(8,128)S(1)} %pad_maximum_fusion.1), channel_id=1, source_target_pairs={{0,4},{1,5},{2,6},{3,7},{4,0},{5,1},{6,2},{7,3},{8,12},{9,13},{10,... | collective-permute-start | bytes 147464 | tf_op jit(solution)/shard_map/ppermute | solution.py:295
  18.9 0.2 shard_map.101.early_ref
  19.1 0.0 collective-permute-done.4.near_ref
  19.1 0.4 %shard_map.102.sum_ref = f32[4,24,128]{2,1,0:T(8,128)S(1)} custom-call(f32[4,24,128]{2,1,0:T(8,128)S(1)} %get-tuple-element.40.field2_ref.field_ref, f32[48,128]{1,0:T(8,128)S(1)} %collective-permute-done.4.near_ref, bf16[4,768,256]{2,1,0:T(8,128)(2,1)S(1)} %get-tuple-element.32.inner_ref), custom_call_target="tpu_custom_call" | custom-call | tf_op jit(solution)/shard_map/pallas_call | solution.py:371
  19.5 0.0 copy-start
  19.5 0.0 collective-permute-done.5.far_ref
  19.5 0.4 shard_map.103
  19.8 1.2 %all-to-all-done.peaks_ref = f32[32,1,192]{2,1,0:T(1,128)S(1)} async-done(((f32[32,1,192]{2,1,0:T(1,128)}), f32[32,1,192]{2,1,0:T(1,128)S(1)}, u32[]{:S(2)}, u32[]{:S(2)}) %all-to-all-start) | async-done | bytes 24608 | tf_op jit(solution)/shard_map/all_to_all | solution.py:363
  21.1 0.7 %shard_map.104 = f32[32,3,4,128]{3,2,1,0:T(4,128)} custom-call(f32[3,24,128]{2,1,0:T(8,128)S(1)} %shard_map.101.early_ref, f32[24,128]{1,0:T(8,128)S(1)} %get-tuple-element.44.late_ref, f32[32,1,192]{2,1,0:T(1,128)S(1)} %all-to-all-done.peaks_ref), custom_call_target="tpu_custom_call" | custom-call | tf_op jit(solution)/shard_map/pallas_call | solution.py:375
  21.8 3.3 %all-to-all-start.1 = ((f32[32,3,4,128]{3,2,1,0:T(4,128)}), f32[32,3,4,128]{3,2,1,0:T(4,128)S(1)}, u32[]{:S(2)}, u32[]{:S(2)}) async-start(f32[32,3,4,128]{3,2,1,0:T(4,128)} %shard_map.104), calls=%async_computation.1 | async-start | bytes 393216 | tf_op jit(solution)/shard_map/all_to_all | solution.py:376
  25.1 0.0 collective-permute-done.7
  25.2 1.8 %collective-permute-start.8 = (f32[72,512]{1,0:T(8,128)S(1)}, f32[72,512]{1,0:T(8,128)S(1)}, u32[]{:S(2)}, u32[]{:S(2)}) collective-permute-start(f32[72,512]{1,0:T(8,128)S(1)} %slice.18), channel_id=1, source_target_pairs={{0,1},{1,0},{2,3},{3,2},{4,5},{5,4},{6,7},{7,6},{8,9},{9,8},{10,11... | collective-permute-start | bytes 442376 | tf_op jit(solution)/shard_map/ppermute | solution.py:295
  27.0 1.5 %collective-permute-start.10 = (f32[32,512]{1,0:T(8,128)S(1)}, f32[32,512]{1,0:T(8,128)S(1)}, u32[]{:S(2)}, u32[]{:S(2)}) collective-permute-start(f32[32,512]{1,0:T(8,128)S(1)} %pad_maximum_fusion.refs_0_), channel_id=1, source_target_pairs={{0,3},{1,2},{2,1},{3,0},{4,7},{5,6},{6,5},{7,4},{8,11},{9,10},{10,... | collective-permute-start | bytes 196616 | tf_op jit(solution)/shard_map/ppermute | solution.py:295
  28.5 0.3 collective-permute-start.9
  28.7 4.9 %all-to-all-done.1 = f32[32,3,4,128]{3,2,1,0:T(4,128)S(1)} async-done(((f32[32,3,4,128]{3,2,1,0:T(4,128)}), f32[32,3,4,128]{3,2,1,0:T(4,128)S(1)}, u32[]{:S(2)}, u32[]{:S(2)}) %all-to-all-start.1) | async-done | bytes 196640 | tf_op jit(solution)/shard_map/all_to_all | solution.py:376
  33.7 0.2 collective-permute-start.6
  33.9 0.7 %shard_map.106 = (f32[4,24,128]{2,1,0:T(8,128)}, f32[4,24,128]{2,1,0:T(8,128)S(1)}) custom-call(f32[4,24,128]{2,1,0:T(8,128)S(1)} %get-tuple-element.27.field_ref.field0_ref, f32[4,24,128]{2,1,0:T(8,128)S(1)} %get-tuple-element.36.field_ref.field1_ref, f32[4,24,128]{2,1,0:T(8,128)S(1)} %get-tuple-element.40.field2_ref.field_ref, ...), custom_call_target="tpu_custom_call" | custom-call | tf_op jit(solution)/shard_map/pallas_call | solution.py:377
  34.5 0.1 collective-permute-done.8
  34.6 0.0 collective-permute-done.10.refs_3_
  34.6 0.0 collective-permute-done.9.refs_2_
  34.6 0.0 copy-done
  34.6 0.1 shard_map.105
  34.8 0.2 collective-permute-done.6.other_ref
  35.0 1.0 %shard_map.107 = f32[4,24,128]{2,1,0:T(8,128)} custom-call(f32[12,512]{1,0:T(8,128)S(1)} %bitcast.10, f32[12,512]{1,0:T(8,128)S(1)} %collective-permute-done.6.other_ref, bf16[512,256]{1,0:T(8,128)(2,1)S(1)} %get-tuple-element.47.right_ref, bf16[128,512]{1,0:T(8,128)(2,1)S(1)} %get-tuple-element.48.places_ref, f32[4,24,128]{2,1,0:T(8,128)S(1)} %get-tuple-element.50.answer_ref), custom_call_target="tpu_custom_call" | custom-call | tf_op jit(solution)/shard_map/pallas_call | solution.py:390
  (13 shorter events, 0.1 us)
Async XLA Ops:
  2.0 5.2 %collective-permute-start.1 = (f32[56,128]{1,0:T(8,128)S(1)}, f32[56,128]{1,0:T(8,128)S(1)}, u32[]{:S(2)}, u32[]{:S(2)}) collective-permute-start(f32[56,128]{1,0:T(8,128)S(1)} %get-tuple-element.33), channel_id=1, source_target_pairs={{0,24},{8,16},{16,8},{24,0},{1,25},{9,17},{17,9},{25,1},{2,26},{10... | collective-permute-start | bytes 86024 | tf_op jit(solution)/shard_map/ppermute | solution.py:300
  4.4 2.3 %collective-permute-start = (f32[48,128]{1,0:T(8,128)S(1)}, f32[48,128]{1,0:T(8,128)S(1)}, u32[]{:S(2)}, u32[]{:S(2)}) collective-permute-start(f32[48,128]{1,0:T(8,128)S(1)} %get-tuple-element.28), channel_id=1, source_target_pairs={{0,8},{8,0},{16,24},{24,16},{1,9},{9,1},{17,25},{25,17},{2,10},{10... | collective-permute-start | bytes 73736 | tf_op jit(solution)/shard_map/ppermute | solution.py:295
  7.4 6.9 %collective-permute-start.3 = (f32[56,128]{1,0:T(8,128)S(1)}, f32[56,128]{1,0:T(8,128)S(1)}, u32[]{:S(2)}, u32[]{:S(2)}) collective-permute-start(f32[56,128]{1,0:T(8,128)S(1)} %get-tuple-element.38), channel_id=1, source_target_pairs={{0,24},{8,16},{16,8},{24,0},{1,25},{9,17},{17,9},{25,1},{2,26},{10... | collective-permute-start | bytes 86024 | tf_op jit(solution)/shard_map/ppermute | solution.py:300
  8.6 5.3 %collective-permute-start.2 = (f32[48,128]{1,0:T(8,128)S(1)}, f32[48,128]{1,0:T(8,128)S(1)}, u32[]{:S(2)}, u32[]{:S(2)}) collective-permute-start(f32[48,128]{1,0:T(8,128)S(1)} %get-tuple-element.37), channel_id=1, source_target_pairs={{0,8},{8,0},{16,24},{24,16},{1,9},{9,1},{17,25},{25,17},{2,10},{10... | collective-permute-start | bytes 73736 | tf_op jit(solution)/shard_map/ppermute | solution.py:295
  9.0 12.1 %all-to-all-start = ((f32[32,1,192]{2,1,0:T(1,128)}), f32[32,1,192]{2,1,0:T(1,128)S(1)}, u32[]{:S(2)}, u32[]{:S(2)}) async-start(f32[32,1,192]{2,1,0:T(1,128)} %get-tuple-element.45), calls=%async_computation | async-start | bytes 65536 | tf_op jit(solution)/shard_map/all_to_all | solution.py:363
  14.5 4.5 %collective-permute-start.4 = (f32[48,128]{1,0:T(8,128)S(1)}, f32[48,128]{1,0:T(8,128)S(1)}, u32[]{:S(2)}, u32[]{:S(2)}) collective-permute-start(f32[48,128]{1,0:T(8,128)S(1)} %get-tuple-element.42), channel_id=1, source_target_pairs={{0,8},{8,0},{16,24},{24,16},{1,9},{9,1},{17,25},{25,17},{2,10},{10... | collective-permute-start | bytes 73736 | tf_op jit(solution)/shard_map/ppermute | solution.py:295
  14.9 4.6 %collective-permute-start.5 = (f32[72,128]{1,0:T(8,128)S(1)}, f32[72,128]{1,0:T(8,128)S(1)}, u32[]{:S(2)}, u32[]{:S(2)}) collective-permute-start(f32[72,128]{1,0:T(8,128)S(1)} %get-tuple-element.43), channel_id=1, source_target_pairs={{0,24},{8,16},{16,8},{24,0},{1,25},{9,17},{17,9},{25,1},{2,26},{10... | collective-permute-start | bytes 110600 | tf_op jit(solution)/shard_map/ppermute | solution.py:300
  16.5 8.6 %collective-permute-start.7 = (f32[24,512]{1,0:T(8,128)S(1)}, f32[24,512]{1,0:T(8,128)S(1)}, u32[]{:S(2)}, u32[]{:S(2)}) collective-permute-start(f32[24,512]{1,0:T(8,128)S(1)} %pad_maximum_fusion.1), channel_id=1, source_target_pairs={{0,4},{1,5},{2,6},{3,7},{4,0},{5,1},{6,2},{7,3},{8,12},{9,13},{10,... | collective-permute-start | bytes 147464 | tf_op jit(solution)/shard_map/ppermute | solution.py:295
  19.5 15.2 %copy-start = (s32[4,128]{1,0:T(4,128)S(1)}, s32[4,128]{1,0:T(4,128)}, u32[]{:S(2)}) copy-start(s32[4,128]{1,0:T(4,128)} %aggregate_ref.1) | copy-start | bytes 6148
  21.8 11.8 %all-to-all-start.1 = ((f32[32,3,4,128]{3,2,1,0:T(4,128)}), f32[32,3,4,128]{3,2,1,0:T(4,128)S(1)}, u32[]{:S(2)}, u32[]{:S(2)}) async-start(f32[32,3,4,128]{3,2,1,0:T(4,128)} %shard_map.104), calls=%async_computation.1 | async-start | bytes 393216 | tf_op jit(solution)/shard_map/all_to_all | solution.py:376
  25.2 9.5 %collective-permute-start.8 = (f32[72,512]{1,0:T(8,128)S(1)}, f32[72,512]{1,0:T(8,128)S(1)}, u32[]{:S(2)}, u32[]{:S(2)}) collective-permute-start(f32[72,512]{1,0:T(8,128)S(1)} %slice.18), channel_id=1, source_target_pairs={{0,1},{1,0},{2,3},{3,2},{4,5},{5,4},{6,7},{7,6},{8,9},{9,8},{10,11... | collective-permute-start | bytes 442376 | tf_op jit(solution)/shard_map/ppermute | solution.py:295
  27.0 7.6 %collective-permute-start.10 = (f32[32,512]{1,0:T(8,128)S(1)}, f32[32,512]{1,0:T(8,128)S(1)}, u32[]{:S(2)}, u32[]{:S(2)}) collective-permute-start(f32[32,512]{1,0:T(8,128)S(1)} %pad_maximum_fusion.refs_0_), channel_id=1, source_target_pairs={{0,3},{1,2},{2,1},{3,0},{4,7},{5,6},{6,5},{7,4},{8,11},{9,10},{10,... | collective-permute-start | bytes 196616 | tf_op jit(solution)/shard_map/ppermute | solution.py:295
  28.5 6.2 %collective-permute-start.9 = (f32[32,512]{1,0:T(8,128)S(1)}, f32[32,512]{1,0:T(8,128)S(1)}, u32[]{:S(2)}, u32[]{:S(2)}) collective-permute-start(f32[32,512]{1,0:T(8,128)S(1)} %pad_maximum_fusion.refs_0_), channel_id=1, source_target_pairs={{0,2},{1,3},{2,0},{3,1},{4,6},{5,7},{6,4},{7,5},{8,10},{9,11},{10,... | collective-permute-start | bytes 196616 | tf_op jit(solution)/shard_map/ppermute | solution.py:295
  33.7 1.3 %collective-permute-start.6 = (f32[12,512]{1,0:T(8,128)S(1)}, f32[12,512]{1,0:T(8,128)S(1)}, u32[]{:S(2)}, u32[]{:S(2)}) collective-permute-start(f32[12,512]{1,0:T(8,128)S(1)} %bitcast.9), channel_id=1, source_target_pairs={{0,8},{8,0},{16,24},{24,16},{1,9},{9,1},{17,25},{25,17},{2,10},{10... | collective-permute-start | bytes 73736 | tf_op jit(solution)/shard_map/ppermute | solution.py:295

commit v7 on v6

--- a/solution.py
+++ b/solution.py
@@ -226,14 +226,14 @@
     return less(remainder, applied(direction)), answer
 
 
-def largest(peaks_ref, size):
-    return 1.0 + jnp.max(peaks_ref[...], axis=0)[0:1, :size]
+def largest(peaks_ref):
+    return 1.0 + jnp.max(peaks_ref[...], axis=0)[0:1]
 
 
 def outgoing_kernel(early_ref, late_ref, peaks_ref, outgoing_ref):
     targets, quarter, four, _ = outgoing_ref.shape
     half = quarter * four
-    on_residual, _ = coefficients(largest(peaks_ref, late_ref.shape[1]))
+    on_residual, _ = coefficients(largest(peaks_ref))
     sums = sum(c * f for c, f in zip(on_residual, [early_ref[0], early_ref[1], early_ref[2], late_ref[...]]))
     narrow = lax.axis_size("narrow")
     for target in range(targets):
@@ -243,7 +243,7 @@
 
 
 def finish_kernel(field0_ref, field1_ref, field2_ref, field3_ref, diagonal_ref, peaks_ref, residual_ref, answer_ref):
-    on_residual, on_answer = coefficients(largest(peaks_ref, diagonal_ref.shape[1]))
+    on_residual, on_answer = coefficients(largest(peaks_ref))
     for b in range(field0_ref.shape[0]):
         fields = [field0_ref[b], field1_ref[b], field2_ref[b], field3_ref[b]]
         residual_ref[b] = diagonal_ref[b : b + 1, :] * sum(c * f for c, f in zip(on_residual, fields))
@@ -316,7 +316,6 @@
     field = like(blocks, comps, size)
     message = like(ghosts * comps, size)
     further = like(ghosts * comps + 8, size)
-    furthest = like(3 * ghosts * comps // 2, size)
 
     def call(kernel, in_specs, out_shape, scratch=(), out_specs=None):
         return pl.pallas_call(
@@ -341,7 +340,7 @@
     )(*from_hbm(send_list, loads, diagonal, slot_mask, stiffness))
     near, far = halo(near, far)
     parts = like(blocks, (blocks + ghosts) * size, 2 * size, dtype=bf16)
-    peaks = like(wide * narrow, 1, 3 * size // 2)
+    peaks = like(wide * narrow, 1, size)
     inner, outer, places, inverse, peaks = call(
         prepare_kernel, [HBM] * 3 + [VMEM] * 3,
         (
@@ -361,12 +360,12 @@
     )
     near, far = halo(near, far)
     peaks = lax.all_to_all(peaks, AXES, 0, 0)
-    field2, near, far, inverse = call(passing_step_kernel, [VMEM] * 6, (field, message, furthest, like(*coarse_inverse.shape)))(
+    field2, near, far, inverse = call(passing_step_kernel, [VMEM] * 6, (field, message, message, like(*coarse_inverse.shape)))(
         within(field1, near, inner), far, outer, scale, choice, inverse
     )
     near, far = halo(near, far)
     early = call(restrict_kernel, [VMEM] * 5, like(3, comps, members))(field0, field1, field2, scale, places)
-    arrived = swap(longer(inverse, 3 * inverse.shape[0] // 2), "narrow", narrow // 2)[: inverse.shape[0]]
+    arrived = swap(inverse, "narrow", narrow // 2)
     field3, late = call(last_step_kernel, [VMEM] * 5, (field, like(comps, members)))(
         within(field2, near, inner), far, outer, scale, places
     )

time: 36.2 us -> 36 us (level)
  transfers between devices with their start and end apart: 13 -> 13, of which waited for: 4 -> 4; matrix products, arithmetic and copies ran while one was open for 0% -> 0% of each run, Pallas kernels for 14% -> 13%
where the time goes in v7:
time: 36 us; the launch traced here: 35.8 us
  starting transfers between devices  21.3 us (59%)
  Pallas kernels  7.19 us (20%)
  waiting for transfers between devices  6.27 us (17%)
  between operations  0.87 us (2%)
    ppermute x8, starting transfers between devices, swap(): lax.ppermute(value, axis, [(i, i ^ bit) for i in range(lax.axis_size(axis...  7.5 us
    ppermute x3, starting transfers between devices, swap_far(): lax.ppermute(value, 'wide', [(i, (i + 1 if i % 2 else i - 1) % count) for...  5.66 us
    all_to_all x1, waiting for transfers between devices, shards(): incoming = lax.all_to_all(outgoing, AXES, 0, 0)  4.9 us
    all_to_all x1, starting transfers between devices, shards(): peaks = lax.all_to_all(peaks, AXES, 0, 0)  4.89 us
    all_to_all x1, starting transfers between devices, shards(): incoming = lax.all_to_all(outgoing, AXES, 0, 0)  3.28 us
    pallas_call x1, Pallas kernels, shards(): call(start_kernel, [HBM] * 5, (field, message, further, like(blocks, size...  1.32 us
    pallas_call x1, Pallas kernels, shards(): call(prepare_kernel, [HBM] * 3 + [VMEM] * 3, (parts, like(blocks, ghosts...  1.28 us
    all_to_all x1, waiting for transfers between devices, shards(): peaks = lax.all_to_all(peaks, AXES, 0, 0)  1.1 us
  transfers between devices with their start and end apart: 13, of which 4 were waited for; matrix products, arithmetic and copies ran while one was open for 0% of the time, Pallas kernels for 13%

profile of v7, /device:TPU:0, one launch (start us, length us, event | category | flops | bytes accessed | tf_op | source)
XLA Modules:
  0.0 35.8 jit_solution(13743159993762443189)
XLA Ops:
  0.6 1.3 %shard_map.95 = (f32[4,24,128]{2,1,0:T(8,128)S(1)}, f32[48,128]{1,0:T(8,128)S(1)}, f32[56,128]{1,0:T(8,128)S(1)}, f32[4,128]{1,0:T(4,128)S(1)}, f32[16,128]{1,0:...) custom-call(s32[4]{0:T(128)} %send_hbm.1, f32[4,24,128]{2,1,0:T(8,128)} %loads_hbm.1, ...), custom_call_target="tpu_custom_call" | custom-call | tf_op jit(solution)/shard_map/pallas_call | solution.py:330
  2.0 2.5 %collective-permute-start.1 = (f32[56,128]{1,0:T(8,128)S(1)}, f32[56,128]{1,0:T(8,128)S(1)}, u32[]{:S(2)}, u32[]{:S(2)}) collective-permute-start(f32[56,128]{1,0:T(8,128)S(1)} %get-tuple-element.33), channel_id=1, source_target_pairs={{0,24},{8,16},{16,8},{24,0},{1,25},{9,17},{17,9},{25,1},{2,26},{10... | collective-permute-start | bytes 86024 | tf_op jit(solution)/shard_map/ppermute | solution.py:300
  4.4 0.7 %collective-permute-start = (f32[48,128]{1,0:T(8,128)S(1)}, f32[48,128]{1,0:T(8,128)S(1)}, u32[]{:S(2)}, u32[]{:S(2)}) collective-permute-start(f32[48,128]{1,0:T(8,128)S(1)} %get-tuple-element.28), channel_id=1, source_target_pairs={{0,8},{8,0},{16,24},{24,16},{1,9},{9,1},{17,25},{25,17},{2,10},{10... | collective-permute-start | bytes 73736 | tf_op jit(solution)/shard_map/ppermute | solution.py:295
  5.1 1.3 %shard_map.96 = (bf16[4,768,256]{2,1,0:T(8,128)(2,1)S(1)}, bf16[4,256,256]{2,1,0:T(8,128)(2,1)S(1)}, bf16[128,512]{1,0:T(8,128)(2,1)S(1)}, f32[16,512]{1,0:T(8,128)S(1)}, f32[32,1,128]{2,1,0:T(1,128)}) custom-call(s32[4,4]{1,0:T(4,128)} %neighbors_hbm.1, s32[4,128]{1,0:T(4,128)} %aggregate_ref.1, f32[16,512]{1,0:T(8,128)} %inverse_hbm.1, ...), custom_call_target="tpu_custom_call" | custom-call | tf_op jit(solution)/shard_map/pallas_call | solution.py:344
  6.4 0.0 collective-permute-done.near_ref
  6.4 0.4 %shard_map.97.sum_ref = f32[4,24,128]{2,1,0:T(8,128)S(1)} custom-call(f32[4,24,128]{2,1,0:T(8,128)S(1)} %get-tuple-element.27.field_ref.field0_ref, f32[48,128]{1,0:T(8,128)S(1)} %collective-permute-done.near_ref, bf16[4,768,256]{2,1,0:T(8,128)(2,1)S(1)} %get-tuple-element.32.inner_ref), custom_call_target="tpu_custom_call" | custom-call | tf_op jit(solution)/shard_map/pallas_call | solution.py:359
  6.8 0.0 collective-permute-done.1.far_ref
  6.8 0.2 shard_map.98
  7.0 1.6 %collective-permute-start.3 = (f32[56,128]{1,0:T(8,128)S(1)}, f32[56,128]{1,0:T(8,128)S(1)}, u32[]{:S(2)}, u32[]{:S(2)}) collective-permute-start(f32[56,128]{1,0:T(8,128)S(1)} %get-tuple-element.38), channel_id=1, source_target_pairs={{0,24},{8,16},{16,8},{24,0},{1,25},{9,17},{17,9},{25,1},{2,26},{10... | collective-permute-start | bytes 86024 | tf_op jit(solution)/shard_map/ppermute | solution.py:300
  8.6 0.4 %collective-permute-start.2 = (f32[48,128]{1,0:T(8,128)S(1)}, f32[48,128]{1,0:T(8,128)S(1)}, u32[]{:S(2)}, u32[]{:S(2)}) collective-permute-start(f32[48,128]{1,0:T(8,128)S(1)} %get-tuple-element.37), channel_id=1, source_target_pairs={{0,8},{8,0},{16,24},{24,16},{1,9},{9,1},{17,25},{25,17},{2,10},{10... | collective-permute-start | bytes 73736 | tf_op jit(solution)/shard_map/ppermute | solution.py:295
  9.0 4.9 %all-to-all-start = ((f32[32,1,128]{2,1,0:T(1,128)}), f32[32,1,128]{2,1,0:T(1,128)S(1)}, u32[]{:S(2)}, u32[]{:S(2)}) async-start(f32[32,1,128]{2,1,0:T(1,128)} %get-tuple-element.45), calls=%async_computation | async-start | bytes 32768 | tf_op jit(solution)/shard_map/all_to_all | solution.py:362
  13.9 0.0 collective-permute-done.2.near_ref
  13.9 0.4 %shard_map.99.refs_0_ = f32[4,24,128]{2,1,0:T(8,128)S(1)} custom-call(f32[4,24,128]{2,1,0:T(8,128)S(1)} %get-tuple-element.36.field_ref.field1_ref, f32[48,128]{1,0:T(8,128)S(1)} %collective-permute-done.2.near_ref, bf16[4,768,256]{2,1,0:T(8,128)(2,1)S(1)} %get-tuple-element.32.inner_ref), custom_call_target="tpu_custom_call" | custom-call | tf_op jit(solution)/shard_map/pallas_call | solution.py:364
  14.3 0.0 collective-permute-done.3.refs_1_
  14.3 0.2 shard_map.100
  14.5 0.3 collective-permute-start.4
  14.8 1.6 %collective-permute-start.5 = (f32[48,128]{1,0:T(8,128)S(1)}, f32[48,128]{1,0:T(8,128)S(1)}, u32[]{:S(2)}, u32[]{:S(2)}) collective-permute-start(f32[48,128]{1,0:T(8,128)S(1)} %get-tuple-element.43), channel_id=1, source_target_pairs={{0,24},{8,16},{16,8},{24,0},{1,25},{9,17},{17,9},{25,1},{2,26},{10... | collective-permute-start | bytes 73736 | tf_op jit(solution)/shard_map/ppermute | solution.py:300
  16.5 2.4 %collective-permute-start.7 = (f32[16,512]{1,0:T(8,128)S(1)}, f32[16,512]{1,0:T(8,128)S(1)}, u32[]{:S(2)}, u32[]{:S(2)}) collective-permute-start(f32[16,512]{1,0:T(8,128)S(1)} %get-tuple-element.46), channel_id=1, source_target_pairs={{0,4},{1,5},{2,6},{3,7},{4,0},{5,1},{6,2},{7,3},{8,12},{9,13},{10,... | collective-permute-start | bytes 98312 | tf_op jit(solution)/shard_map/ppermute | solution.py:295
  18.8 0.2 shard_map.101.early_ref
  19.0 0.0 collective-permute-done.4.near_ref
  19.1 0.4 %shard_map.102.sum_ref = f32[4,24,128]{2,1,0:T(8,128)S(1)} custom-call(f32[4,24,128]{2,1,0:T(8,128)S(1)} %get-tuple-element.40.field2_ref.field_ref, f32[48,128]{1,0:T(8,128)S(1)} %collective-permute-done.4.near_ref, bf16[4,768,256]{2,1,0:T(8,128)(2,1)S(1)} %get-tuple-element.32.inner_ref), custom_call_target="tpu_custom_call" | custom-call | tf_op jit(solution)/shard_map/pallas_call | solution.py:370
  19.4 0.0 copy-start
  19.5 0.0 collective-permute-done.5.far_ref
  19.5 0.4 shard_map.103
  19.8 1.1 %all-to-all-done.peaks_ref = f32[32,1,128]{2,1,0:T(1,128)S(1)} async-done(((f32[32,1,128]{2,1,0:T(1,128)}), f32[32,1,128]{2,1,0:T(1,128)S(1)}, u32[]{:S(2)}, u32[]{:S(2)}) %all-to-all-start) | async-done | bytes 16416 | tf_op jit(solution)/shard_map/all_to_all | solution.py:362
  20.9 0.7 %shard_map.104 = f32[32,3,4,128]{3,2,1,0:T(4,128)} custom-call(f32[3,24,128]{2,1,0:T(8,128)S(1)} %shard_map.101.early_ref, f32[24,128]{1,0:T(8,128)S(1)} %get-tuple-element.44.late_ref, f32[32,1,128]{2,1,0:T(1,128)S(1)} %all-to-all-done.peaks_ref), custom_call_target="tpu_custom_call" | custom-call | tf_op jit(solution)/shard_map/pallas_call | solution.py:374
  21.6 3.3 %all-to-all-start.1 = ((f32[32,3,4,128]{3,2,1,0:T(4,128)}), f32[32,3,4,128]{3,2,1,0:T(4,128)S(1)}, u32[]{:S(2)}, u32[]{:S(2)}) async-start(f32[32,3,4,128]{3,2,1,0:T(4,128)} %shard_map.104), calls=%async_computation.1 | async-start | bytes 393216 | tf_op jit(solution)/shard_map/all_to_all | solution.py:375
  24.9 0.0 collective-permute-done.7
  25.0 1.8 %collective-permute-start.8 = (f32[72,512]{1,0:T(8,128)S(1)}, f32[72,512]{1,0:T(8,128)S(1)}, u32[]{:S(2)}, u32[]{:S(2)}) collective-permute-start(f32[72,512]{1,0:T(8,128)S(1)} %slice.9), channel_id=1, source_target_pairs={{0,1},{1,0},{2,3},{3,2},{4,5},{5,4},{6,7},{7,6},{8,9},{9,8},{10,11... | collective-permute-start | bytes 442376 | tf_op jit(solution)/shard_map/ppermute | solution.py:295
  26.8 1.5 %collective-permute-start.10 = (f32[32,512]{1,0:T(8,128)S(1)}, f32[32,512]{1,0:T(8,128)S(1)}, u32[]{:S(2)}, u32[]{:S(2)}) collective-permute-start(f32[32,512]{1,0:T(8,128)S(1)} %constant_dynamic-update-slice_fusion.refs_0_), channel_id=1, source_target_pairs={{0,3},{1,2},{2,1},{3,0},{4,7},{5,6},{6,5},{7,4},{8,11},{9,10},{10,... | collective-permute-start | bytes 196616 | tf_op jit(solution)/shard_map/ppermute | solution.py:295
  28.3 0.3 collective-permute-start.9
  28.6 4.9 %all-to-all-done.1 = f32[32,3,4,128]{3,2,1,0:T(4,128)S(1)} async-done(((f32[32,3,4,128]{3,2,1,0:T(4,128)}), f32[32,3,4,128]{3,2,1,0:T(4,128)S(1)}, u32[]{:S(2)}, u32[]{:S(2)}) %all-to-all-start.1) | async-done | bytes 196640 | tf_op jit(solution)/shard_map/all_to_all | solution.py:375
  33.5 0.2 collective-permute-start.6
  33.7 0.7 %shard_map.106 = (f32[4,24,128]{2,1,0:T(8,128)}, f32[4,24,128]{2,1,0:T(8,128)S(1)}) custom-call(f32[4,24,128]{2,1,0:T(8,128)S(1)} %get-tuple-element.27.field_ref.field0_ref, f32[4,24,128]{2,1,0:T(8,128)S(1)} %get-tuple-element.36.field_ref.field1_ref, f32[4,24,128]{2,1,0:T(8,128)S(1)} %get-tuple-element.40.field2_ref.field_ref, ...), custom_call_target="tpu_custom_call" | custom-call | tf_op jit(solution)/shard_map/pallas_call | solution.py:376
  34.4 0.1 collective-permute-done.8
  34.5 0.0 collective-permute-done.10.refs_3_
  34.5 0.0 collective-permute-done.9.refs_2_
  34.5 0.0 copy-done
  34.5 0.1 shard_map.105
  34.6 0.2 collective-permute-done.6.other_ref
  34.8 1.0 %shard_map.107 = f32[4,24,128]{2,1,0:T(8,128)} custom-call(f32[12,512]{1,0:T(8,128)S(1)} %bitcast.10, f32[12,512]{1,0:T(8,128)S(1)} %collective-permute-done.6.other_ref, bf16[512,256]{1,0:T(8,128)(2,1)S(1)} %get-tuple-element.47.right_ref, bf16[128,512]{1,0:T(8,128)(2,1)S(1)} %get-tuple-element.48.places_ref, f32[4,24,128]{2,1,0:T(8,128)S(1)} %get-tuple-element.50.answer_ref), custom_call_target="tpu_custom_call" | custom-call | tf_op jit(solution)/shard_map/pallas_call | solution.py:389
  (12 shorter events, 0.1 us)
Async XLA Ops:
  2.0 4.8 %collective-permute-start.1 = (f32[56,128]{1,0:T(8,128)S(1)}, f32[56,128]{1,0:T(8,128)S(1)}, u32[]{:S(2)}, u32[]{:S(2)}) collective-permute-start(f32[56,128]{1,0:T(8,128)S(1)} %get-tuple-element.33), channel_id=1, source_target_pairs={{0,24},{8,16},{16,8},{24,0},{1,25},{9,17},{17,9},{25,1},{2,26},{10... | collective-permute-start | bytes 86024 | tf_op jit(solution)/shard_map/ppermute | solution.py:300
  4.4 2.0 %collective-permute-start = (f32[48,128]{1,0:T(8,128)S(1)}, f32[48,128]{1,0:T(8,128)S(1)}, u32[]{:S(2)}, u32[]{:S(2)}) collective-permute-start(f32[48,128]{1,0:T(8,128)S(1)} %get-tuple-element.28), channel_id=1, source_target_pairs={{0,8},{8,0},{16,24},{24,16},{1,9},{9,1},{17,25},{25,17},{2,10},{10... | collective-permute-start | bytes 73736 | tf_op jit(solution)/shard_map/ppermute | solution.py:295
  7.0 7.3 %collective-permute-start.3 = (f32[56,128]{1,0:T(8,128)S(1)}, f32[56,128]{1,0:T(8,128)S(1)}, u32[]{:S(2)}, u32[]{:S(2)}) collective-permute-start(f32[56,128]{1,0:T(8,128)S(1)} %get-tuple-element.38), channel_id=1, source_target_pairs={{0,24},{8,16},{16,8},{24,0},{1,25},{9,17},{17,9},{25,1},{2,26},{10... | collective-permute-start | bytes 86024 | tf_op jit(solution)/shard_map/ppermute | solution.py:300
  8.6 5.3 %collective-permute-start.2 = (f32[48,128]{1,0:T(8,128)S(1)}, f32[48,128]{1,0:T(8,128)S(1)}, u32[]{:S(2)}, u32[]{:S(2)}) collective-permute-start(f32[48,128]{1,0:T(8,128)S(1)} %get-tuple-element.37), channel_id=1, source_target_pairs={{0,8},{8,0},{16,24},{24,16},{1,9},{9,1},{17,25},{25,17},{2,10},{10... | collective-permute-start | bytes 73736 | tf_op jit(solution)/shard_map/ppermute | solution.py:295
  9.0 11.9 %all-to-all-start = ((f32[32,1,128]{2,1,0:T(1,128)}), f32[32,1,128]{2,1,0:T(1,128)S(1)}, u32[]{:S(2)}, u32[]{:S(2)}) async-start(f32[32,1,128]{2,1,0:T(1,128)} %get-tuple-element.45), calls=%async_computation | async-start | bytes 32768 | tf_op jit(solution)/shard_map/all_to_all | solution.py:362
  14.5 4.5 %collective-permute-start.4 = (f32[48,128]{1,0:T(8,128)S(1)}, f32[48,128]{1,0:T(8,128)S(1)}, u32[]{:S(2)}, u32[]{:S(2)}) collective-permute-start(f32[48,128]{1,0:T(8,128)S(1)} %get-tuple-element.42), channel_id=1, source_target_pairs={{0,8},{8,0},{16,24},{24,16},{1,9},{9,1},{17,25},{25,17},{2,10},{10... | collective-permute-start | bytes 73736 | tf_op jit(solution)/shard_map/ppermute | solution.py:295
  14.8 4.6 %collective-permute-start.5 = (f32[48,128]{1,0:T(8,128)S(1)}, f32[48,128]{1,0:T(8,128)S(1)}, u32[]{:S(2)}, u32[]{:S(2)}) collective-permute-start(f32[48,128]{1,0:T(8,128)S(1)} %get-tuple-element.43), channel_id=1, source_target_pairs={{0,24},{8,16},{16,8},{24,0},{1,25},{9,17},{17,9},{25,1},{2,26},{10... | collective-permute-start | bytes 73736 | tf_op jit(solution)/shard_map/ppermute | solution.py:300
  16.5 8.5 %collective-permute-start.7 = (f32[16,512]{1,0:T(8,128)S(1)}, f32[16,512]{1,0:T(8,128)S(1)}, u32[]{:S(2)}, u32[]{:S(2)}) collective-permute-start(f32[16,512]{1,0:T(8,128)S(1)} %get-tuple-element.46), channel_id=1, source_target_pairs={{0,4},{1,5},{2,6},{3,7},{4,0},{5,1},{6,2},{7,3},{8,12},{9,13},{10,... | collective-permute-start | bytes 98312 | tf_op jit(solution)/shard_map/ppermute | solution.py:295
  19.4 15.0 %copy-start = (s32[4,128]{1,0:T(4,128)S(1)}, s32[4,128]{1,0:T(4,128)}, u32[]{:S(2)}) copy-start(s32[4,128]{1,0:T(4,128)} %aggregate_ref.1) | copy-start | bytes 6148
  21.6 11.8 %all-to-all-start.1 = ((f32[32,3,4,128]{3,2,1,0:T(4,128)}), f32[32,3,4,128]{3,2,1,0:T(4,128)S(1)}, u32[]{:S(2)}, u32[]{:S(2)}) async-start(f32[32,3,4,128]{3,2,1,0:T(4,128)} %shard_map.104), calls=%async_computation.1 | async-start | bytes 393216 | tf_op jit(solution)/shard_map/all_to_all | solution.py:375
  25.0 9.5 %collective-permute-start.8 = (f32[72,512]{1,0:T(8,128)S(1)}, f32[72,512]{1,0:T(8,128)S(1)}, u32[]{:S(2)}, u32[]{:S(2)}) collective-permute-start(f32[72,512]{1,0:T(8,128)S(1)} %slice.9), channel_id=1, source_target_pairs={{0,1},{1,0},{2,3},{3,2},{4,5},{5,4},{6,7},{7,6},{8,9},{9,8},{10,11... | collective-permute-start | bytes 442376 | tf_op jit(solution)/shard_map/ppermute | solution.py:295
  26.8 7.6 %collective-permute-start.10 = (f32[32,512]{1,0:T(8,128)S(1)}, f32[32,512]{1,0:T(8,128)S(1)}, u32[]{:S(2)}, u32[]{:S(2)}) collective-permute-start(f32[32,512]{1,0:T(8,128)S(1)} %constant_dynamic-update-slice_fusion.refs_0_), channel_id=1, source_target_pairs={{0,3},{1,2},{2,1},{3,0},{4,7},{5,6},{6,5},{7,4},{8,11},{9,10},{10,... | collective-permute-start | bytes 196616 | tf_op jit(solution)/shard_map/ppermute | solution.py:295
  28.3 6.2 %collective-permute-start.9 = (f32[32,512]{1,0:T(8,128)S(1)}, f32[32,512]{1,0:T(8,128)S(1)}, u32[]{:S(2)}, u32[]{:S(2)}) collective-permute-start(f32[32,512]{1,0:T(8,128)S(1)} %constant_dynamic-update-slice_fusion.refs_0_), channel_id=1, source_target_pairs={{0,2},{1,3},{2,0},{3,1},{4,6},{5,7},{6,4},{7,5},{8,10},{9,11},{10,... | collective-permute-start | bytes 196616 | tf_op jit(solution)/shard_map/ppermute | solution.py:295
  33.5 1.3 %collective-permute-start.6 = (f32[12,512]{1,0:T(8,128)S(1)}, f32[12,512]{1,0:T(8,128)S(1)}, u32[]{:S(2)}, u32[]{:S(2)}) collective-permute-start(f32[12,512]{1,0:T(8,128)S(1)} %bitcast.9), channel_id=1, source_target_pairs={{0,8},{8,0},{16,24},{24,16},{1,9},{9,1},{17,25},{25,17},{2,10},{10... | collective-permute-start | bytes 73736 | tf_op jit(solution)/shard_map/ppermute | solution.py:295

commit v8 on v7

--- a/solution.py
+++ b/solution.py
@@ -67,10 +67,10 @@
     blocks, _, size = loads_ref.shape
     ghosts = send_ref.shape[0] // 2
     copies = start_copies([
+        *((stiffness_hbm.at[b], stiffness_ref.at[b]) for b in range(blocks)),
         (send_hbm, send_ref), (diagonal_hbm, diagonal_ref), (loads_hbm, loads_ref), (mask_hbm, mask_ref),
-        (stiffness_hbm, stiffness_ref),
     ], sems)
-    for copy in copies[:4]:
+    for copy in copies[blocks:]:
         copy.wait()
     odd = parity()
     for j in range(ghosts):
@@ -88,7 +88,8 @@
         for s in range(slots):
             row = b * slots + s
             live_ref[row : row + 1, :] = jnp.full((1, size), mask_ref[b, s].astype(f32), f32)
-    copies[4].wait()
+    for copy in copies[:blocks]:
+        copy.wait()
 
 
 def prepare_kernel(
@@ -156,18 +157,22 @@
     products(fields, inner_ref, sum_ref)
 
 
-def couple(sum_ref, far_ref, outer_ref, diagonal_ref, next_ref):
+def couple(sum_ref, far_ref, outer_ref, next_ref):
     blocks, comps, size = sum_ref.shape
     ghosts = outer_ref.shape[1] // size
     me = lax.axis_index("wide")
     inside = jnp.where((me == 0) | (me == lax.axis_size("wide") - 1), 0.0, 1.0).astype(f32)
     products([far_ref[j * comps : (j + 1) * comps] * inside for j in range(ghosts)], outer_ref, next_ref, sum_ref)
-    for b in range(blocks):
-        next_ref[b] = next_ref[b] / diagonal_ref[b : b + 1, :]
+
+
+def over_diagonal(field_ref, diagonal_ref):
+    for b in range(field_ref.shape[0]):
+        field_ref[b] = field_ref[b] / diagonal_ref[b : b + 1, :]
 
 
 def step_kernel(sum_ref, far_ref, outer_ref, diagonal_ref, choice_ref, next_ref, near_out, far_out):
-    couple(sum_ref, far_ref, outer_ref, diagonal_ref, next_ref)
+    couple(sum_ref, far_ref, outer_ref, next_ref)
+    over_diagonal(next_ref, diagonal_ref)
     write_messages(choice_ref, next_ref, near_out, far_out)
 
 
@@ -181,7 +186,7 @@
     blocks, comps, size = fields[0].shape
     values = []
     for b in range(blocks):
-        scale = diagonal_ref[b : b + 1, :]
+        scale = 1.0 if diagonal_ref is None else diagonal_ref[b : b + 1, :]
         values.append(jnp.concatenate([stacked(field[b] * scale) for field in fields], axis=0))
     product = lax.dot_general(
         jnp.concatenate(values, axis=1), places_ref[...], TRANSPOSED, preferred_element_type=f32
@@ -196,8 +201,9 @@
 
 
 def last_step_kernel(sum_ref, far_ref, outer_ref, diagonal_ref, places_ref, next_ref, sums_ref):
-    couple(sum_ref, far_ref, outer_ref, diagonal_ref, next_ref)
-    (sums_ref[...],) = restrict([next_ref], diagonal_ref, places_ref)
+    couple(sum_ref, far_ref, outer_ref, next_ref)
+    (sums_ref[...],) = restrict([next_ref], None, places_ref)
+    over_diagonal(next_ref, diagonal_ref)
 
 
 def coefficients(upper):
@@ -335,7 +341,7 @@
         ),
         [
             pltpu.VMEM(loads.shape, f32), pltpu.SMEM(send_list.shape, jnp.int32),
-            pltpu.SMEM(slot_mask.shape, jnp.int32), pltpu.SemaphoreType.DMA((5,)),
+            pltpu.SMEM(slot_mask.shape, jnp.int32), pltpu.SemaphoreType.DMA((4 + blocks,)),
         ],
     )(*from_hbm(send_list, loads, diagonal, slot_mask, stiffness))
     near, far = halo(near, far)

time: 36 us -> 36 us (level)
  no operation moved by 1% of the time
where the time goes in v8:
time: 36 us; the launch traced here: 35.7 us
  starting transfers between devices  21.3 us (59%)
  Pallas kernels  7.14 us (20%)
  waiting for transfers between devices  6.28 us (17%)
  between operations  0.87 us (2%)
    ppermute x8, starting transfers between devices, swap(): lax.ppermute(value, axis, [(i, i ^ bit) for i in range(lax.axis_size(axis...  7.5 us
    ppermute x3, starting transfers between devices, swap_far(): lax.ppermute(value, 'wide', [(i, (i + 1 if i % 2 else i - 1) % count) for...  5.66 us
    all_to_all x1, waiting for transfers between devices, shards(): incoming = lax.all_to_all(outgoing, AXES, 0, 0)  4.9 us
    all_to_all x1, starting transfers between devices, shards(): peaks = lax.all_to_all(peaks, AXES, 0, 0)  4.89 us
    all_to_all x1, starting transfers between devices, shards(): incoming = lax.all_to_all(outgoing, AXES, 0, 0)  3.28 us
    pallas_call x1, Pallas kernels, shards(): call(prepare_kernel, [HBM] * 3 + [VMEM] * 3, (parts, like(blocks, ghosts...  1.28 us
    pallas_call x1, Pallas kernels, shards(): call(start_kernel, [HBM] * 5, (field, message, further, like(blocks, size...  1.27 us
    all_to_all x1, waiting for transfers between devices, shards(): peaks = lax.all_to_all(peaks, AXES, 0, 0)  1.11 us
  transfers between devices with their start and end apart: 13, of which 4 were waited for; matrix products, arithmetic and copies ran while one was open for 0% of the time, Pallas kernels for 13%

profile of v8, /device:TPU:0, one launch (start us, length us, event | category | flops | bytes accessed | tf_op | source)
XLA Modules:
  0.0 35.7 jit_solution(1918420572469627230)
XLA Ops:
  0.6 1.3 %shard_map.95 = (f32[4,24,128]{2,1,0:T(8,128)S(1)}, f32[48,128]{1,0:T(8,128)S(1)}, f32[56,128]{1,0:T(8,128)S(1)}, f32[4,128]{1,0:T(4,128)S(1)}, f32[16,128]{1,0:...) custom-call(s32[4]{0:T(128)} %send_hbm.1, f32[4,24,128]{2,1,0:T(8,128)} %loads_hbm.1, ...), custom_call_target="tpu_custom_call" | custom-call | tf_op jit(solution)/shard_map/pallas_call | solution.py:336
  1.9 2.5 %collective-permute-start.1 = (f32[56,128]{1,0:T(8,128)S(1)}, f32[56,128]{1,0:T(8,128)S(1)}, u32[]{:S(2)}, u32[]{:S(2)}) collective-permute-start(f32[56,128]{1,0:T(8,128)S(1)} %get-tuple-element.33), channel_id=1, source_target_pairs={{0,24},{8,16},{16,8},{24,0},{1,25},{9,17},{17,9},{25,1},{2,26},{10... | collective-permute-start | bytes 86024 | tf_op jit(solution)/shard_map/ppermute | solution.py:306
  4.4 0.7 %collective-permute-start = (f32[48,128]{1,0:T(8,128)S(1)}, f32[48,128]{1,0:T(8,128)S(1)}, u32[]{:S(2)}, u32[]{:S(2)}) collective-permute-start(f32[48,128]{1,0:T(8,128)S(1)} %get-tuple-element.28), channel_id=1, source_target_pairs={{0,8},{8,0},{16,24},{24,16},{1,9},{9,1},{17,25},{25,17},{2,10},{10... | collective-permute-start | bytes 73736 | tf_op jit(solution)/shard_map/ppermute | solution.py:301
  5.1 1.3 %shard_map.96 = (bf16[4,768,256]{2,1,0:T(8,128)(2,1)S(1)}, bf16[4,256,256]{2,1,0:T(8,128)(2,1)S(1)}, bf16[128,512]{1,0:T(8,128)(2,1)S(1)}, f32[16,512]{1,0:T(8,128)S(1)}, f32[32,1,128]{2,1,0:T(1,128)}) custom-call(s32[4,4]{1,0:T(4,128)} %neighbors_hbm.1, s32[4,128]{1,0:T(4,128)} %aggregate_ref.1, f32[16,512]{1,0:T(8,128)} %inverse_hbm.1, ...), custom_call_target="tpu_custom_call" | custom-call | tf_op jit(solution)/shard_map/pallas_call | solution.py:350
  6.3 0.0 collective-permute-done.near_ref
  6.3 0.4 %shard_map.97.sum_ref = f32[4,24,128]{2,1,0:T(8,128)S(1)} custom-call(f32[4,24,128]{2,1,0:T(8,128)S(1)} %get-tuple-element.27.field_ref.field0_ref, f32[48,128]{1,0:T(8,128)S(1)} %collective-permute-done.near_ref, bf16[4,768,256]{2,1,0:T(8,128)(2,1)S(1)} %get-tuple-element.32.inner_ref), custom_call_target="tpu_custom_call" | custom-call | tf_op jit(solution)/shard_map/pallas_call | solution.py:365
  6.7 0.0 collective-permute-done.1.far_ref
  6.8 0.2 shard_map.98
  7.0 1.6 %collective-permute-start.3 = (f32[56,128]{1,0:T(8,128)S(1)}, f32[56,128]{1,0:T(8,128)S(1)}, u32[]{:S(2)}, u32[]{:S(2)}) collective-permute-start(f32[56,128]{1,0:T(8,128)S(1)} %get-tuple-element.38), channel_id=1, source_target_pairs={{0,24},{8,16},{16,8},{24,0},{1,25},{9,17},{17,9},{25,1},{2,26},{10... | collective-permute-start | bytes 86024 | tf_op jit(solution)/shard_map/ppermute | solution.py:306
  8.5 0.4 %collective-permute-start.2 = (f32[48,128]{1,0:T(8,128)S(1)}, f32[48,128]{1,0:T(8,128)S(1)}, u32[]{:S(2)}, u32[]{:S(2)}) collective-permute-start(f32[48,128]{1,0:T(8,128)S(1)} %get-tuple-element.37), channel_id=1, source_target_pairs={{0,8},{8,0},{16,24},{24,16},{1,9},{9,1},{17,25},{25,17},{2,10},{10... | collective-permute-start | bytes 73736 | tf_op jit(solution)/shard_map/ppermute | solution.py:301
  8.9 4.9 %all-to-all-start = ((f32[32,1,128]{2,1,0:T(1,128)}), f32[32,1,128]{2,1,0:T(1,128)S(1)}, u32[]{:S(2)}, u32[]{:S(2)}) async-start(f32[32,1,128]{2,1,0:T(1,128)} %get-tuple-element.45), calls=%async_computation | async-start | bytes 32768 | tf_op jit(solution)/shard_map/all_to_all | solution.py:368
  13.8 0.0 collective-permute-done.2.near_ref
  13.8 0.4 %shard_map.99.refs_0_ = f32[4,24,128]{2,1,0:T(8,128)S(1)} custom-call(f32[4,24,128]{2,1,0:T(8,128)S(1)} %get-tuple-element.36.field_ref.field1_ref, f32[48,128]{1,0:T(8,128)S(1)} %collective-permute-done.2.near_ref, bf16[4,768,256]{2,1,0:T(8,128)(2,1)S(1)} %get-tuple-element.32.inner_ref), custom_call_target="tpu_custom_call" | custom-call | tf_op jit(solution)/shard_map/pallas_call | solution.py:370
  14.2 0.0 collective-permute-done.3.refs_1_
  14.2 0.2 shard_map.100
  14.5 0.3 collective-permute-start.4
  14.8 1.6 %collective-permute-start.5 = (f32[48,128]{1,0:T(8,128)S(1)}, f32[48,128]{1,0:T(8,128)S(1)}, u32[]{:S(2)}, u32[]{:S(2)}) collective-permute-start(f32[48,128]{1,0:T(8,128)S(1)} %get-tuple-element.43), channel_id=1, source_target_pairs={{0,24},{8,16},{16,8},{24,0},{1,25},{9,17},{17,9},{25,1},{2,26},{10... | collective-permute-start | bytes 73736 | tf_op jit(solution)/shard_map/ppermute | solution.py:306
  16.4 2.4 %collective-permute-start.7 = (f32[16,512]{1,0:T(8,128)S(1)}, f32[16,512]{1,0:T(8,128)S(1)}, u32[]{:S(2)}, u32[]{:S(2)}) collective-permute-start(f32[16,512]{1,0:T(8,128)S(1)} %get-tuple-element.46), channel_id=1, source_target_pairs={{0,4},{1,5},{2,6},{3,7},{4,0},{5,1},{6,2},{7,3},{8,12},{9,13},{10,... | collective-permute-start | bytes 98312 | tf_op jit(solution)/shard_map/ppermute | solution.py:301
  18.8 0.2 shard_map.101.early_ref
  19.0 0.0 collective-permute-done.4.near_ref
  19.0 0.4 %shard_map.102.sum_ref = f32[4,24,128]{2,1,0:T(8,128)S(1)} custom-call(f32[4,24,128]{2,1,0:T(8,128)S(1)} %get-tuple-element.40.field2_ref.field_ref, f32[48,128]{1,0:T(8,128)S(1)} %collective-permute-done.4.near_ref, bf16[4,768,256]{2,1,0:T(8,128)(2,1)S(1)} %get-tuple-element.32.inner_ref), custom_call_target="tpu_custom_call" | custom-call | tf_op jit(solution)/shard_map/pallas_call | solution.py:376
  19.4 0.0 copy-start
  19.4 0.0 collective-permute-done.5.far_ref
  19.4 0.3 shard_map.103
  19.8 1.1 %all-to-all-done.peaks_ref = f32[32,1,128]{2,1,0:T(1,128)S(1)} async-done(((f32[32,1,128]{2,1,0:T(1,128)}), f32[32,1,128]{2,1,0:T(1,128)S(1)}, u32[]{:S(2)}, u32[]{:S(2)}) %all-to-all-start) | async-done | bytes 16416 | tf_op jit(solution)/shard_map/all_to_all | solution.py:368
  20.9 0.7 %shard_map.104 = f32[32,3,4,128]{3,2,1,0:T(4,128)} custom-call(f32[3,24,128]{2,1,0:T(8,128)S(1)} %shard_map.101.early_ref, f32[24,128]{1,0:T(8,128)S(1)} %get-tuple-element.44.late_ref, f32[32,1,128]{2,1,0:T(1,128)S(1)} %all-to-all-done.peaks_ref), custom_call_target="tpu_custom_call" | custom-call | tf_op jit(solution)/shard_map/pallas_call | solution.py:380
  21.6 3.3 %all-to-all-start.1 = ((f32[32,3,4,128]{3,2,1,0:T(4,128)}), f32[32,3,4,128]{3,2,1,0:T(4,128)S(1)}, u32[]{:S(2)}, u32[]{:S(2)}) async-start(f32[32,3,4,128]{3,2,1,0:T(4,128)} %shard_map.104), calls=%async_computation.1 | async-start | bytes 393216 | tf_op jit(solution)/shard_map/all_to_all | solution.py:381
  24.9 0.0 collective-permute-done.7
  24.9 1.8 %collective-permute-start.8 = (f32[72,512]{1,0:T(8,128)S(1)}, f32[72,512]{1,0:T(8,128)S(1)}, u32[]{:S(2)}, u32[]{:S(2)}) collective-permute-start(f32[72,512]{1,0:T(8,128)S(1)} %slice.9), channel_id=1, source_target_pairs={{0,1},{1,0},{2,3},{3,2},{4,5},{5,4},{6,7},{7,6},{8,9},{9,8},{10,11... | collective-permute-start | bytes 442376 | tf_op jit(solution)/shard_map/ppermute | solution.py:301
  26.8 1.5 %collective-permute-start.10 = (f32[32,512]{1,0:T(8,128)S(1)}, f32[32,512]{1,0:T(8,128)S(1)}, u32[]{:S(2)}, u32[]{:S(2)}) collective-permute-start(f32[32,512]{1,0:T(8,128)S(1)} %constant_dynamic-update-slice_fusion.refs_0_), channel_id=1, source_target_pairs={{0,3},{1,2},{2,1},{3,0},{4,7},{5,6},{6,5},{7,4},{8,11},{9,10},{10,... | collective-permute-start | bytes 196616 | tf_op jit(solution)/shard_map/ppermute | solution.py:301
  28.2 0.3 collective-permute-start.9
  28.5 4.9 %all-to-all-done.1 = f32[32,3,4,128]{3,2,1,0:T(4,128)S(1)} async-done(((f32[32,3,4,128]{3,2,1,0:T(4,128)}), f32[32,3,4,128]{3,2,1,0:T(4,128)S(1)}, u32[]{:S(2)}, u32[]{:S(2)}) %all-to-all-start.1) | async-done | bytes 196640 | tf_op jit(solution)/shard_map/all_to_all | solution.py:381
  33.5 0.2 collective-permute-start.6
  33.7 0.7 %shard_map.106 = (f32[4,24,128]{2,1,0:T(8,128)}, f32[4,24,128]{2,1,0:T(8,128)S(1)}) custom-call(f32[4,24,128]{2,1,0:T(8,128)S(1)} %get-tuple-element.27.field_ref.field0_ref, f32[4,24,128]{2,1,0:T(8,128)S(1)} %get-tuple-element.36.field_ref.field1_ref, f32[4,24,128]{2,1,0:T(8,128)S(1)} %get-tuple-element.40.field2_ref.field_ref, ...), custom_call_target="tpu_custom_call" | custom-call | tf_op jit(solution)/shard_map/pallas_call | solution.py:382
  34.3 0.1 collective-permute-done.8
  34.4 0.0 collective-permute-done.10.refs_3_
  34.4 0.0 collective-permute-done.9.refs_2_
  34.4 0.0 copy-done
  34.4 0.1 shard_map.105
  34.6 0.2 collective-permute-done.6.other_ref
  34.8 1.0 %shard_map.107 = f32[4,24,128]{2,1,0:T(8,128)} custom-call(f32[12,512]{1,0:T(8,128)S(1)} %bitcast.10, f32[12,512]{1,0:T(8,128)S(1)} %collective-permute-done.6.other_ref, bf16[512,256]{1,0:T(8,128)(2,1)S(1)} %get-tuple-element.47.right_ref, bf16[128,512]{1,0:T(8,128)(2,1)S(1)} %get-tuple-element.48.places_ref, f32[4,24,128]{2,1,0:T(8,128)S(1)} %get-tuple-element.50.answer_ref), custom_call_target="tpu_custom_call" | custom-call | tf_op jit(solution)/shard_map/pallas_call | solution.py:395
  (12 shorter events, 0.1 us)
Async XLA Ops:
  1.9 4.8 %collective-permute-start.1 = (f32[56,128]{1,0:T(8,128)S(1)}, f32[56,128]{1,0:T(8,128)S(1)}, u32[]{:S(2)}, u32[]{:S(2)}) collective-permute-start(f32[56,128]{1,0:T(8,128)S(1)} %get-tuple-element.33), channel_id=1, source_target_pairs={{0,24},{8,16},{16,8},{24,0},{1,25},{9,17},{17,9},{25,1},{2,26},{10... | collective-permute-start | bytes 86024 | tf_op jit(solution)/shard_map/ppermute | solution.py:306
  4.4 2.0 %collective-permute-start = (f32[48,128]{1,0:T(8,128)S(1)}, f32[48,128]{1,0:T(8,128)S(1)}, u32[]{:S(2)}, u32[]{:S(2)}) collective-permute-start(f32[48,128]{1,0:T(8,128)S(1)} %get-tuple-element.28), channel_id=1, source_target_pairs={{0,8},{8,0},{16,24},{24,16},{1,9},{9,1},{17,25},{25,17},{2,10},{10... | collective-permute-start | bytes 73736 | tf_op jit(solution)/shard_map/ppermute | solution.py:301
  7.0 7.3 %collective-permute-start.3 = (f32[56,128]{1,0:T(8,128)S(1)}, f32[56,128]{1,0:T(8,128)S(1)}, u32[]{:S(2)}, u32[]{:S(2)}) collective-permute-start(f32[56,128]{1,0:T(8,128)S(1)} %get-tuple-element.38), channel_id=1, source_target_pairs={{0,24},{8,16},{16,8},{24,0},{1,25},{9,17},{17,9},{25,1},{2,26},{10... | collective-permute-start | bytes 86024 | tf_op jit(solution)/shard_map/ppermute | solution.py:306
  8.5 5.3 %collective-permute-start.2 = (f32[48,128]{1,0:T(8,128)S(1)}, f32[48,128]{1,0:T(8,128)S(1)}, u32[]{:S(2)}, u32[]{:S(2)}) collective-permute-start(f32[48,128]{1,0:T(8,128)S(1)} %get-tuple-element.37), channel_id=1, source_target_pairs={{0,8},{8,0},{16,24},{24,16},{1,9},{9,1},{17,25},{25,17},{2,10},{10... | collective-permute-start | bytes 73736 | tf_op jit(solution)/shard_map/ppermute | solution.py:301
  8.9 11.9 %all-to-all-start = ((f32[32,1,128]{2,1,0:T(1,128)}), f32[32,1,128]{2,1,0:T(1,128)S(1)}, u32[]{:S(2)}, u32[]{:S(2)}) async-start(f32[32,1,128]{2,1,0:T(1,128)} %get-tuple-element.45), calls=%async_computation | async-start | bytes 32768 | tf_op jit(solution)/shard_map/all_to_all | solution.py:368
  14.5 4.5 %collective-permute-start.4 = (f32[48,128]{1,0:T(8,128)S(1)}, f32[48,128]{1,0:T(8,128)S(1)}, u32[]{:S(2)}, u32[]{:S(2)}) collective-permute-start(f32[48,128]{1,0:T(8,128)S(1)} %get-tuple-element.42), channel_id=1, source_target_pairs={{0,8},{8,0},{16,24},{24,16},{1,9},{9,1},{17,25},{25,17},{2,10},{10... | collective-permute-start | bytes 73736 | tf_op jit(solution)/shard_map/ppermute | solution.py:301
  14.8 4.6 %collective-permute-start.5 = (f32[48,128]{1,0:T(8,128)S(1)}, f32[48,128]{1,0:T(8,128)S(1)}, u32[]{:S(2)}, u32[]{:S(2)}) collective-permute-start(f32[48,128]{1,0:T(8,128)S(1)} %get-tuple-element.43), channel_id=1, source_target_pairs={{0,24},{8,16},{16,8},{24,0},{1,25},{9,17},{17,9},{25,1},{2,26},{10... | collective-permute-start | bytes 73736 | tf_op jit(solution)/shard_map/ppermute | solution.py:306
  16.4 8.5 %collective-permute-start.7 = (f32[16,512]{1,0:T(8,128)S(1)}, f32[16,512]{1,0:T(8,128)S(1)}, u32[]{:S(2)}, u32[]{:S(2)}) collective-permute-start(f32[16,512]{1,0:T(8,128)S(1)} %get-tuple-element.46), channel_id=1, source_target_pairs={{0,4},{1,5},{2,6},{3,7},{4,0},{5,1},{6,2},{7,3},{8,12},{9,13},{10,... | collective-permute-start | bytes 98312 | tf_op jit(solution)/shard_map/ppermute | solution.py:301
  19.4 15.0 %copy-start = (s32[4,128]{1,0:T(4,128)S(1)}, s32[4,128]{1,0:T(4,128)}, u32[]{:S(2)}) copy-start(s32[4,128]{1,0:T(4,128)} %aggregate_ref.1) | copy-start | bytes 6148
  21.6 11.8 %all-to-all-start.1 = ((f32[32,3,4,128]{3,2,1,0:T(4,128)}), f32[32,3,4,128]{3,2,1,0:T(4,128)S(1)}, u32[]{:S(2)}, u32[]{:S(2)}) async-start(f32[32,3,4,128]{3,2,1,0:T(4,128)} %shard_map.104), calls=%async_computation.1 | async-start | bytes 393216 | tf_op jit(solution)/shard_map/all_to_all | solution.py:381
  24.9 9.5 %collective-permute-start.8 = (f32[72,512]{1,0:T(8,128)S(1)}, f32[72,512]{1,0:T(8,128)S(1)}, u32[]{:S(2)}, u32[]{:S(2)}) collective-permute-start(f32[72,512]{1,0:T(8,128)S(1)} %slice.9), channel_id=1, source_target_pairs={{0,1},{1,0},{2,3},{3,2},{4,5},{5,4},{6,7},{7,6},{8,9},{9,8},{10,11... | collective-permute-start | bytes 442376 | tf_op jit(solution)/shard_map/ppermute | solution.py:301
  26.8 7.6 %collective-permute-start.10 = (f32[32,512]{1,0:T(8,128)S(1)}, f32[32,512]{1,0:T(8,128)S(1)}, u32[]{:S(2)}, u32[]{:S(2)}) collective-permute-start(f32[32,512]{1,0:T(8,128)S(1)} %constant_dynamic-update-slice_fusion.refs_0_), channel_id=1, source_target_pairs={{0,3},{1,2},{2,1},{3,0},{4,7},{5,6},{6,5},{7,4},{8,11},{9,10},{10,... | collective-permute-start | bytes 196616 | tf_op jit(solution)/shard_map/ppermute | solution.py:301
  28.2 6.2 %collective-permute-start.9 = (f32[32,512]{1,0:T(8,128)S(1)}, f32[32,512]{1,0:T(8,128)S(1)}, u32[]{:S(2)}, u32[]{:S(2)}) collective-permute-start(f32[32,512]{1,0:T(8,128)S(1)} %constant_dynamic-update-slice_fusion.refs_0_), channel_id=1, source_target_pairs={{0,2},{1,3},{2,0},{3,1},{4,6},{5,7},{6,4},{7,5},{8,10},{9,11},{10,... | collective-permute-start | bytes 196616 | tf_op jit(solution)/shard_map/ppermute | solution.py:301
  33.5 1.3 %collective-permute-start.6 = (f32[12,512]{1,0:T(8,128)S(1)}, f32[12,512]{1,0:T(8,128)S(1)}, u32[]{:S(2)}, u32[]{:S(2)}) collective-permute-start(f32[12,512]{1,0:T(8,128)S(1)} %bitcast.9), channel_id=1, source_target_pairs={{0,8},{8,0},{16,24},{24,16},{1,9},{9,1},{17,25},{25,17},{2,10},{10... | collective-permute-start | bytes 73736 | tf_op jit(solution)/shard_map/ppermute | solution.py:301

commit v9 on v8

--- a/solution.py
+++ b/solution.py
@@ -256,7 +256,7 @@
         answer_ref[b] = sum(c * f for c, f in zip(on_answer, fields))
 
 
-def inverse_kernel(aggregate_ref, *refs):
+def inverse_kernel(aggregate_ref, ahead_ref, *refs):
     *gathered, right_ref, places_ref = refs
     members = places_ref.shape[0]
     blocks, size = aggregate_ref.shape
@@ -381,14 +381,12 @@
     incoming = lax.all_to_all(outgoing, AXES, 0, 0)
     residual, answer = call(finish_kernel, [VMEM] * 6, (field, field))(field0, field1, field2, field3, scale, peaks)
     inverse = jnp.concatenate([inverse, arrived], axis=0)
-    gathered = [inverse]
-    for offset in range(1, narrow // 2):
-        sent = longer(inverse, 9 * inverse.shape[0] // 4) if offset == 1 else inverse
-        gathered.append(swap(sent, "narrow", offset)[: inverse.shape[0]])
+    gathered = [inverse] + [swap(inverse, "narrow", offset) for offset in range(1, narrow // 2)]
+    ahead = swap(longer(inverse, 9 * inverse.shape[0] // 4), "wide", 1)
     right, reads = call(
-        inverse_kernel, [VMEM] * (1 + len(gathered)),
+        inverse_kernel, [VMEM] * (2 + len(gathered)),
         (like(unknowns, 2 * members, dtype=bf16), like(members, blocks * size, dtype=bf16)),
-    )(aggregate, *gathered)
+    )(aggregate, ahead, *gathered)
     own = incoming.reshape(wide, narrow, half, members).sum(axis=1)
     own = own.transpose(1, 0, 2).reshape(half, wide * members)
     other = swap(own, "wide", 1)

time: 36 us -> 36 us (level)
    ppermute x8 -> x9, starting transfers between devices: 7.5 us -> 7.75 us  [swap(): lax.ppermute(value, axis, [(i, i ^ bit) for i in range(lax.axis_size(axis...]
  transfers between devices with their start and end apart: 13 -> 14, of which waited for: 4 -> 3; matrix products, arithmetic and copies ran while one was open for 0% -> 0% of each run, Pallas kernels for 13% -> 13%
where the time goes in v9:
time: 36 us; the launch traced here: 35.7 us
  starting transfers between devices  21.6 us (60%)
  Pallas kernels  7.14 us (20%)
  waiting for transfers between devices  6.03 us (17%)
  between operations  0.87 us (2%)
    ppermute x9, starting transfers between devices, swap(): lax.ppermute(value, axis, [(i, i ^ bit) for i in range(lax.axis_size(axis...  7.75 us
    ppermute x3, starting transfers between devices, swap_far(): lax.ppermute(value, 'wide', [(i, (i + 1 if i % 2 else i - 1) % count) for...  5.66 us
    all_to_all x1, starting transfers between devices, shards(): peaks = lax.all_to_all(peaks, AXES, 0, 0)  4.89 us
    all_to_all x1, waiting for transfers between devices, shards(): incoming = lax.all_to_all(outgoing, AXES, 0, 0)  4.65 us
    all_to_all x1, starting transfers between devices, shards(): incoming = lax.all_to_all(outgoing, AXES, 0, 0)  3.28 us
    pallas_call x1, Pallas kernels, shards(): call(prepare_kernel, [HBM] * 3 + [VMEM] * 3, (parts, like(blocks, ghosts...  1.28 us
    pallas_call x1, Pallas kernels, shards(): call(start_kernel, [HBM] * 5, (field, message, further, like(blocks, size...  1.27 us
    all_to_all x1, waiting for transfers between devices, shards(): peaks = lax.all_to_all(peaks, AXES, 0, 0)  1.1 us
  transfers between devices with their start and end apart: 14, of which 3 were waited for; matrix products, arithmetic and copies ran while one was open for 0% of the time, Pallas kernels for 13%

profile of v9, /device:TPU:0, one launch (start us, length us, event | category | flops | bytes accessed | tf_op | source)
XLA Modules:
  0.0 35.7 jit_solution(4795579278076662061)
XLA Ops:
  0.6 1.3 %shard_map.95 = (f32[4,24,128]{2,1,0:T(8,128)S(1)}, f32[48,128]{1,0:T(8,128)S(1)}, f32[56,128]{1,0:T(8,128)S(1)}, f32[4,128]{1,0:T(4,128)S(1)}, f32[16,128]{1,0:...) custom-call(s32[4]{0:T(128)} %send_hbm.1, f32[4,24,128]{2,1,0:T(8,128)} %loads_hbm.1, ...), custom_call_target="tpu_custom_call" | custom-call | tf_op jit(solution)/shard_map/pallas_call | solution.py:336
  1.9 2.5 %collective-permute-start.1 = (f32[56,128]{1,0:T(8,128)S(1)}, f32[56,128]{1,0:T(8,128)S(1)}, u32[]{:S(2)}, u32[]{:S(2)}) collective-permute-start(f32[56,128]{1,0:T(8,128)S(1)} %get-tuple-element.33), channel_id=1, source_target_pairs={{0,24},{8,16},{16,8},{24,0},{1,25},{9,17},{17,9},{25,1},{2,26},{10... | collective-permute-start | bytes 86024 | tf_op jit(solution)/shard_map/ppermute | solution.py:306
  4.4 0.7 %collective-permute-start = (f32[48,128]{1,0:T(8,128)S(1)}, f32[48,128]{1,0:T(8,128)S(1)}, u32[]{:S(2)}, u32[]{:S(2)}) collective-permute-start(f32[48,128]{1,0:T(8,128)S(1)} %get-tuple-element.28), channel_id=1, source_target_pairs={{0,8},{8,0},{16,24},{24,16},{1,9},{9,1},{17,25},{25,17},{2,10},{10... | collective-permute-start | bytes 73736 | tf_op jit(solution)/shard_map/ppermute | solution.py:301
  5.1 1.3 %shard_map.96 = (bf16[4,768,256]{2,1,0:T(8,128)(2,1)S(1)}, bf16[4,256,256]{2,1,0:T(8,128)(2,1)S(1)}, bf16[128,512]{1,0:T(8,128)(2,1)S(1)}, f32[16,512]{1,0:T(8,128)S(1)}, f32[32,1,128]{2,1,0:T(1,128)}) custom-call(s32[4,4]{1,0:T(4,128)} %neighbors_hbm.1, s32[4,128]{1,0:T(4,128)} %aggregate_ref.1, f32[16,512]{1,0:T(8,128)} %inverse_hbm.1, ...), custom_call_target="tpu_custom_call" | custom-call | tf_op jit(solution)/shard_map/pallas_call | solution.py:350
  6.3 0.0 collective-permute-done.near_ref
  6.3 0.4 %shard_map.97.sum_ref = f32[4,24,128]{2,1,0:T(8,128)S(1)} custom-call(f32[4,24,128]{2,1,0:T(8,128)S(1)} %get-tuple-element.27.field_ref.field0_ref, f32[48,128]{1,0:T(8,128)S(1)} %collective-permute-done.near_ref, bf16[4,768,256]{2,1,0:T(8,128)(2,1)S(1)} %get-tuple-element.32.inner_ref), custom_call_target="tpu_custom_call" | custom-call | tf_op jit(solution)/shard_map/pallas_call | solution.py:365
  6.7 0.0 collective-permute-done.1.far_ref
  6.8 0.2 shard_map.98
  7.0 1.6 %collective-permute-start.3 = (f32[56,128]{1,0:T(8,128)S(1)}, f32[56,128]{1,0:T(8,128)S(1)}, u32[]{:S(2)}, u32[]{:S(2)}) collective-permute-start(f32[56,128]{1,0:T(8,128)S(1)} %get-tuple-element.38), channel_id=1, source_target_pairs={{0,24},{8,16},{16,8},{24,0},{1,25},{9,17},{17,9},{25,1},{2,26},{10... | collective-permute-start | bytes 86024 | tf_op jit(solution)/shard_map/ppermute | solution.py:306
  8.5 0.4 %collective-permute-start.2 = (f32[48,128]{1,0:T(8,128)S(1)}, f32[48,128]{1,0:T(8,128)S(1)}, u32[]{:S(2)}, u32[]{:S(2)}) collective-permute-start(f32[48,128]{1,0:T(8,128)S(1)} %get-tuple-element.37), channel_id=1, source_target_pairs={{0,8},{8,0},{16,24},{24,16},{1,9},{9,1},{17,25},{25,17},{2,10},{10... | collective-permute-start | bytes 73736 | tf_op jit(solution)/shard_map/ppermute | solution.py:301
  8.9 4.9 %all-to-all-start = ((f32[32,1,128]{2,1,0:T(1,128)}), f32[32,1,128]{2,1,0:T(1,128)S(1)}, u32[]{:S(2)}, u32[]{:S(2)}) async-start(f32[32,1,128]{2,1,0:T(1,128)} %get-tuple-element.45), calls=%async_computation | async-start | bytes 32768 | tf_op jit(solution)/shard_map/all_to_all | solution.py:368
  13.8 0.0 collective-permute-done.2.near_ref
  13.8 0.4 %shard_map.99.refs_0_ = f32[4,24,128]{2,1,0:T(8,128)S(1)} custom-call(f32[4,24,128]{2,1,0:T(8,128)S(1)} %get-tuple-element.36.field_ref.field1_ref, f32[48,128]{1,0:T(8,128)S(1)} %collective-permute-done.2.near_ref, bf16[4,768,256]{2,1,0:T(8,128)(2,1)S(1)} %get-tuple-element.32.inner_ref), custom_call_target="tpu_custom_call" | custom-call | tf_op jit(solution)/shard_map/pallas_call | solution.py:370
  14.2 0.0 collective-permute-done.3.refs_1_
  14.2 0.2 shard_map.100
  14.5 0.3 collective-permute-start.4
  14.8 1.6 %collective-permute-start.5 = (f32[48,128]{1,0:T(8,128)S(1)}, f32[48,128]{1,0:T(8,128)S(1)}, u32[]{:S(2)}, u32[]{:S(2)}) collective-permute-start(f32[48,128]{1,0:T(8,128)S(1)} %get-tuple-element.43), channel_id=1, source_target_pairs={{0,24},{8,16},{16,8},{24,0},{1,25},{9,17},{17,9},{25,1},{2,26},{10... | collective-permute-start | bytes 73736 | tf_op jit(solution)/shard_map/ppermute | solution.py:306
  16.4 2.4 %collective-permute-start.7 = (f32[16,512]{1,0:T(8,128)S(1)}, f32[16,512]{1,0:T(8,128)S(1)}, u32[]{:S(2)}, u32[]{:S(2)}) collective-permute-start(f32[16,512]{1,0:T(8,128)S(1)} %get-tuple-element.46), channel_id=1, source_target_pairs={{0,4},{1,5},{2,6},{3,7},{4,0},{5,1},{6,2},{7,3},{8,12},{9,13},{10,... | collective-permute-start | bytes 98312 | tf_op jit(solution)/shard_map/ppermute | solution.py:301
  18.8 0.2 shard_map.101.early_ref
  19.0 0.0 collective-permute-done.4.near_ref
  19.0 0.4 %shard_map.102.sum_ref = f32[4,24,128]{2,1,0:T(8,128)S(1)} custom-call(f32[4,24,128]{2,1,0:T(8,128)S(1)} %get-tuple-element.40.field2_ref.field_ref, f32[48,128]{1,0:T(8,128)S(1)} %collective-permute-done.4.near_ref, bf16[4,768,256]{2,1,0:T(8,128)(2,1)S(1)} %get-tuple-element.32.inner_ref), custom_call_target="tpu_custom_call" | custom-call | tf_op jit(solution)/shard_map/pallas_call | solution.py:376
  19.4 0.0 copy-start
  19.4 0.0 collective-permute-done.5.far_ref
  19.4 0.3 shard_map.103
  19.8 1.1 %all-to-all-done.peaks_ref = f32[32,1,128]{2,1,0:T(1,128)S(1)} async-done(((f32[32,1,128]{2,1,0:T(1,128)}), f32[32,1,128]{2,1,0:T(1,128)S(1)}, u32[]{:S(2)}, u32[]{:S(2)}) %all-to-all-start) | async-done | bytes 16416 | tf_op jit(solution)/shard_map/all_to_all | solution.py:368
  20.9 0.7 %shard_map.104 = f32[32,3,4,128]{3,2,1,0:T(4,128)} custom-call(f32[3,24,128]{2,1,0:T(8,128)S(1)} %shard_map.101.early_ref, f32[24,128]{1,0:T(8,128)S(1)} %get-tuple-element.44.late_ref, f32[32,1,128]{2,1,0:T(1,128)S(1)} %all-to-all-done.peaks_ref), custom_call_target="tpu_custom_call" | custom-call | tf_op jit(solution)/shard_map/pallas_call | solution.py:380
  21.6 3.3 %all-to-all-start.1 = ((f32[32,3,4,128]{3,2,1,0:T(4,128)}), f32[32,3,4,128]{3,2,1,0:T(4,128)S(1)}, u32[]{:S(2)}, u32[]{:S(2)}) async-start(f32[32,3,4,128]{3,2,1,0:T(4,128)} %shard_map.104), calls=%async_computation.1 | async-start | bytes 393216 | tf_op jit(solution)/shard_map/all_to_all | solution.py:381
  24.9 0.0 collective-permute-done.7
  25.0 0.3 collective-permute-start.8
  25.3 2.6 %collective-permute-start.11 = (f32[32,512]{1,0:T(8,128)S(1)}, f32[32,512]{1,0:T(8,128)S(1)}, u32[]{:S(2)}, u32[]{:S(2)}) collective-permute-start(f32[32,512]{1,0:T(8,128)S(1)} %get-tuple-element.52.refs_0_), channel_id=1, source_target_pairs={{0,3},{1,2},{2,1},{3,0},{4,7},{5,6},{6,5},{7,4},{8,11},{9,10},{10,... | collective-permute-start | bytes 196616 | tf_op jit(solution)/shard_map/ppermute | solution.py:301
  27.9 0.6 %collective-permute-start.10 = (f32[32,512]{1,0:T(8,128)S(1)}, f32[32,512]{1,0:T(8,128)S(1)}, u32[]{:S(2)}, u32[]{:S(2)}) collective-permute-start(f32[32,512]{1,0:T(8,128)S(1)} %get-tuple-element.52.refs_0_), channel_id=1, source_target_pairs={{0,2},{1,3},{2,0},{3,1},{4,6},{5,7},{6,4},{7,5},{8,10},{9,11},{10,... | collective-permute-start | bytes 196616 | tf_op jit(solution)/shard_map/ppermute | solution.py:301
  28.4 0.3 collective-permute-start.9
  28.8 4.6 %all-to-all-done.1 = f32[32,3,4,128]{3,2,1,0:T(4,128)S(1)} async-done(((f32[32,3,4,128]{3,2,1,0:T(4,128)}), f32[32,3,4,128]{3,2,1,0:T(4,128)S(1)}, u32[]{:S(2)}, u32[]{:S(2)}) %all-to-all-start.1) | async-done | bytes 196640 | tf_op jit(solution)/shard_map/all_to_all | solution.py:381
  33.5 0.2 collective-permute-start.6
  33.7 0.7 %shard_map.106 = (f32[4,24,128]{2,1,0:T(8,128)}, f32[4,24,128]{2,1,0:T(8,128)S(1)}) custom-call(f32[4,24,128]{2,1,0:T(8,128)S(1)} %get-tuple-element.27.field_ref.field0_ref, f32[4,24,128]{2,1,0:T(8,128)S(1)} %get-tuple-element.36.field_ref.field1_ref, f32[4,24,128]{2,1,0:T(8,128)S(1)} %get-tuple-element.40.field2_ref.field_ref, ...), custom_call_target="tpu_custom_call" | custom-call | tf_op jit(solution)/shard_map/pallas_call | solution.py:382
  34.3 0.0 collective-permute-done.11.refs_3_
  34.3 0.0 collective-permute-done.10.refs_2_
  34.3 0.0 collective-permute-done.9.refs_1_
  34.3 0.0 collective-permute-done.8.ahead_ref
  34.4 0.0 copy-done
  34.4 0.1 shard_map.105
  34.5 0.2 collective-permute-done.6.other_ref
  34.8 1.0 %shard_map.107 = f32[4,24,128]{2,1,0:T(8,128)} custom-call(f32[12,512]{1,0:T(8,128)S(1)} %bitcast.10, f32[12,512]{1,0:T(8,128)S(1)} %collective-permute-done.6.other_ref, bf16[512,256]{1,0:T(8,128)(2,1)S(1)} %get-tuple-element.47.right_ref, bf16[128,512]{1,0:T(8,128)(2,1)S(1)} %get-tuple-element.48.places_ref, f32[4,24,128]{2,1,0:T(8,128)S(1)} %get-tuple-element.50.answer_ref), custom_call_target="tpu_custom_call" | custom-call | tf_op jit(solution)/shard_map/pallas_call | solution.py:393
  (10 shorter events, 0.1 us)
Async XLA Ops:
  1.9 4.8 %collective-permute-start.1 = (f32[56,128]{1,0:T(8,128)S(1)}, f32[56,128]{1,0:T(8,128)S(1)}, u32[]{:S(2)}, u32[]{:S(2)}) collective-permute-start(f32[56,128]{1,0:T(8,128)S(1)} %get-tuple-element.33), channel_id=1, source_target_pairs={{0,24},{8,16},{16,8},{24,0},{1,25},{9,17},{17,9},{25,1},{2,26},{10... | collective-permute-start | bytes 86024 | tf_op jit(solution)/shard_map/ppermute | solution.py:306
  4.4 2.0 %collective-permute-start = (f32[48,128]{1,0:T(8,128)S(1)}, f32[48,128]{1,0:T(8,128)S(1)}, u32[]{:S(2)}, u32[]{:S(2)}) collective-permute-start(f32[48,128]{1,0:T(8,128)S(1)} %get-tuple-element.28), channel_id=1, source_target_pairs={{0,8},{8,0},{16,24},{24,16},{1,9},{9,1},{17,25},{25,17},{2,10},{10... | collective-permute-start | bytes 73736 | tf_op jit(solution)/shard_map/ppermute | solution.py:301
  7.0 7.3 %collective-permute-start.3 = (f32[56,128]{1,0:T(8,128)S(1)}, f32[56,128]{1,0:T(8,128)S(1)}, u32[]{:S(2)}, u32[]{:S(2)}) collective-permute-start(f32[56,128]{1,0:T(8,128)S(1)} %get-tuple-element.38), channel_id=1, source_target_pairs={{0,24},{8,16},{16,8},{24,0},{1,25},{9,17},{17,9},{25,1},{2,26},{10... | collective-permute-start | bytes 86024 | tf_op jit(solution)/shard_map/ppermute | solution.py:306
  8.5 5.3 %collective-permute-start.2 = (f32[48,128]{1,0:T(8,128)S(1)}, f32[48,128]{1,0:T(8,128)S(1)}, u32[]{:S(2)}, u32[]{:S(2)}) collective-permute-start(f32[48,128]{1,0:T(8,128)S(1)} %get-tuple-element.37), channel_id=1, source_target_pairs={{0,8},{8,0},{16,24},{24,16},{1,9},{9,1},{17,25},{25,17},{2,10},{10... | collective-permute-start | bytes 73736 | tf_op jit(solution)/shard_map/ppermute | solution.py:301
  8.9 11.9 %all-to-all-start = ((f32[32,1,128]{2,1,0:T(1,128)}), f32[32,1,128]{2,1,0:T(1,128)S(1)}, u32[]{:S(2)}, u32[]{:S(2)}) async-start(f32[32,1,128]{2,1,0:T(1,128)} %get-tuple-element.45), calls=%async_computation | async-start | bytes 32768 | tf_op jit(solution)/shard_map/all_to_all | solution.py:368
  14.5 4.5 %collective-permute-start.4 = (f32[48,128]{1,0:T(8,128)S(1)}, f32[48,128]{1,0:T(8,128)S(1)}, u32[]{:S(2)}, u32[]{:S(2)}) collective-permute-start(f32[48,128]{1,0:T(8,128)S(1)} %get-tuple-element.42), channel_id=1, source_target_pairs={{0,8},{8,0},{16,24},{24,16},{1,9},{9,1},{17,25},{25,17},{2,10},{10... | collective-permute-start | bytes 73736 | tf_op jit(solution)/shard_map/ppermute | solution.py:301
  14.8 4.6 %collective-permute-start.5 = (f32[48,128]{1,0:T(8,128)S(1)}, f32[48,128]{1,0:T(8,128)S(1)}, u32[]{:S(2)}, u32[]{:S(2)}) collective-permute-start(f32[48,128]{1,0:T(8,128)S(1)} %get-tuple-element.43), channel_id=1, source_target_pairs={{0,24},{8,16},{16,8},{24,0},{1,25},{9,17},{17,9},{25,1},{2,26},{10... | collective-permute-start | bytes 73736 | tf_op jit(solution)/shard_map/ppermute | solution.py:306
  16.4 8.5 %collective-permute-start.7 = (f32[16,512]{1,0:T(8,128)S(1)}, f32[16,512]{1,0:T(8,128)S(1)}, u32[]{:S(2)}, u32[]{:S(2)}) collective-permute-start(f32[16,512]{1,0:T(8,128)S(1)} %get-tuple-element.46), channel_id=1, source_target_pairs={{0,4},{1,5},{2,6},{3,7},{4,0},{5,1},{6,2},{7,3},{8,12},{9,13},{10,... | collective-permute-start | bytes 98312 | tf_op jit(solution)/shard_map/ppermute | solution.py:301
  19.4 15.0 %copy-start = (s32[4,128]{1,0:T(4,128)S(1)}, s32[4,128]{1,0:T(4,128)}, u32[]{:S(2)}) copy-start(s32[4,128]{1,0:T(4,128)} %aggregate_ref.1) | copy-start | bytes 6148
  21.6 11.8 %all-to-all-start.1 = ((f32[32,3,4,128]{3,2,1,0:T(4,128)}), f32[32,3,4,128]{3,2,1,0:T(4,128)S(1)}, u32[]{:S(2)}, u32[]{:S(2)}) async-start(f32[32,3,4,128]{3,2,1,0:T(4,128)} %shard_map.104), calls=%async_computation.1 | async-start | bytes 393216 | tf_op jit(solution)/shard_map/all_to_all | solution.py:381
  25.0 9.4 %collective-permute-start.8 = (f32[72,512]{1,0:T(8,128)S(1)}, f32[72,512]{1,0:T(8,128)S(1)}, u32[]{:S(2)}, u32[]{:S(2)}) collective-permute-start(f32[72,512]{1,0:T(8,128)S(1)} %slice.5), channel_id=1, source_target_pairs={{0,8},{8,0},{16,24},{24,16},{1,9},{9,1},{17,25},{25,17},{2,10},{10... | collective-permute-start | bytes 442376 | tf_op jit(solution)/shard_map/ppermute | solution.py:301
  25.3 9.1 %collective-permute-start.11 = (f32[32,512]{1,0:T(8,128)S(1)}, f32[32,512]{1,0:T(8,128)S(1)}, u32[]{:S(2)}, u32[]{:S(2)}) collective-permute-start(f32[32,512]{1,0:T(8,128)S(1)} %get-tuple-element.52.refs_0_), channel_id=1, source_target_pairs={{0,3},{1,2},{2,1},{3,0},{4,7},{5,6},{6,5},{7,4},{8,11},{9,10},{10,... | collective-permute-start | bytes 196616 | tf_op jit(solution)/shard_map/ppermute | solution.py:301
  27.9 6.5 %collective-permute-start.10 = (f32[32,512]{1,0:T(8,128)S(1)}, f32[32,512]{1,0:T(8,128)S(1)}, u32[]{:S(2)}, u32[]{:S(2)}) collective-permute-start(f32[32,512]{1,0:T(8,128)S(1)} %get-tuple-element.52.refs_0_), channel_id=1, source_target_pairs={{0,2},{1,3},{2,0},{3,1},{4,6},{5,7},{6,4},{7,5},{8,10},{9,11},{10,... | collective-permute-start | bytes 196616 | tf_op jit(solution)/shard_map/ppermute | solution.py:301
  28.4 5.9 %collective-permute-start.9 = (f32[32,512]{1,0:T(8,128)S(1)}, f32[32,512]{1,0:T(8,128)S(1)}, u32[]{:S(2)}, u32[]{:S(2)}) collective-permute-start(f32[32,512]{1,0:T(8,128)S(1)} %get-tuple-element.52.refs_0_), channel_id=1, source_target_pairs={{0,1},{1,0},{2,3},{3,2},{4,5},{5,4},{6,7},{7,6},{8,9},{9,8},{10,11... | collective-permute-start | bytes 196616 | tf_op jit(solution)/shard_map/ppermute | solution.py:301
  33.5 1.3 %collective-permute-start.6 = (f32[12,512]{1,0:T(8,128)S(1)}, f32[12,512]{1,0:T(8,128)S(1)}, u32[]{:S(2)}, u32[]{:S(2)}) collective-permute-start(f32[12,512]{1,0:T(8,128)S(1)} %bitcast.9), channel_id=1, source_target_pairs={{0,8},{8,0},{16,24},{24,16},{1,9},{9,1},{17,25},{25,17},{2,10},{10... | collective-permute-start | bytes 73736 | tf_op jit(solution)/shard_map/ppermute | solution.py:301
